TPU v7x, 32 devices: a whole 2x2x4 slice. The times are simulated.
32 devices in a mesh: dp: 2 (over x), fsdp: 16 (over z, y, core).
Axes of the slice: x: 2, y: 2, z: 4, core: 2. Of those that a mesh axis runs over, the one named last changes fastest.
Arguments:
- layer_input: bfloat16 [4096, 2048], P(('dp', 'fsdp')), may hold values from -12 to 12
- first_gain: bfloat16 [2048], P('fsdp'), may hold values from 0.25 to 1.75
- in_weight: bfloat16 [2048, 6144], P('fsdp'), may hold values from -0.125 to 0.125
- out_weight: bfloat16 [2048, 2048], P('fsdp'), may hold values from -0.5 to 0.5
- mix_gate: bfloat16 [2048], P('fsdp'), may hold values from -2 to 2
- second_gain: bfloat16 [2048], P('fsdp'), may hold values from 0.25 to 1.75
- gate_up: bfloat16 [2048, 16384], P('fsdp'), may hold values from -0.125 to 0.125
- down_weight: bfloat16 [2048, 8192], P('fsdp'), may hold values from -0.0625 to 0.0625
- document_starts: int32 [2, 2], P('dp'), may hold values from 0 to 1, as said below
- cotangent: bfloat16 [4096, 2048], P(('dp', 'fsdp')), may hold values from -6 to 6
Outputs:
- layer_output: bfloat16 [4096, 2048], P(('dp', 'fsdp'))
- input_grad: float32 [4096, 2048], P(('dp', 'fsdp'))
- first_gain_grad: float32 [2048], P('fsdp')
- in_weight_grad: float32 [2048, 6144], P('fsdp')
- out_weight_grad: float32 [2048, 2048], P('fsdp')
- mix_gate_grad: float32 [2048], P('fsdp')
- second_gain_grad: float32 [2048], P('fsdp')
- gate_up_grad: float32 [2048, 16384], P('fsdp')
- down_weight_grad: float32 [2048, 8192], P('fsdp')
Inputs may be any that keep to these rules, and one draw needn't show every extreme that they name: document_starts[n, 0] is 0; one packed sequence, which one drawn from the seed, has no 1 at all (a single document); every other packed sequence has at least one 1.
All inputs are finite; a program needn't handle non-finite values.
Results may differ from a plain program's by a relative error of at most 0.013.
Values may be sent and summed in bfloat16 or wider, within the bound.
A program may use at most 832 MiB of HBM per device.

v0:
```python
import math

import jax
import jax.numpy as jnp
from jax import lax
from jax.sharding import PartitionSpec as P

H = 16
DH = 128
FF = 8192
SEG = 1024


highest_precision = lax.Precision.HIGHEST
epsilon = 1e-06


def from_behind(block, axis, distance):
    devices = range(lax.axis_size(axis))
    route = [(i - distance, i) for i in devices if i - distance in devices]
    return lax.ppermute(block, axis, route)


def carried_in(value, axis, join, neutral):
    place = lax.axis_index(axis)
    gathered = jax.tree.map(
        lambda a, kind: lax.all_gather(a.astype(kind), axis),
        value,
        (jnp.bfloat16, jnp.bfloat16, jnp.bfloat16, jnp.bfloat16, jnp.bfloat16, jnp.bfloat16),
    )
    state = jax.tree.map(lambda a, e: jnp.zeros_like(a) + jnp.asarray(e, a.dtype), value, neutral)

    def one(lap, state):
        return join(
            state,
            jax.tree.map(
                lambda a, own: lax.dynamic_index_in_dim(a, lap, 0, False).astype(own.dtype),
                gathered,
                value,
            ),
        )

    return lax.fori_loop(0, place, one, state)


def carried_in_2(value, axis, join, neutral):
    count = lax.axis_size(axis)
    place = lax.axis_index(axis)
    ahead = count - 1 - place
    gathered = jax.tree.map(
        lambda a, kind: lax.all_gather(a.astype(kind), axis),
        value,
        jax.tree.map(lambda a: jnp.bfloat16 if a.dtype == jnp.float32 else a.dtype, value),
    )
    state = jax.tree.map(lambda a, e: jnp.zeros_like(a) + jnp.asarray(e, a.dtype), value, neutral)

    def one(lap, state):
        source = count - 1 - lap
        return join(
            state,
            jax.tree.map(
                lambda a, own: lax.dynamic_index_in_dim(a, source, 0, False).astype(own.dtype),
                gathered,
                value,
            ),
        )

    return lax.fori_loop(0, ahead, one, state)


def feature(values):
    return jax.nn.elu(values) + 1.0


def feature_slope(values):
    return jnp.where(values > 0, 1.0, jnp.exp(jnp.minimum(values, 0.0)))


def norm_forward(values, gain):
    factor = lax.rsqrt(jnp.mean(values * values, axis=-1, keepdims=True) + epsilon)
    return (values * factor * gain, factor)


def norm_backward(values, factor, gain, upstream):
    scaled = upstream * gain
    gain_grad = jnp.sum(upstream * values * factor, axis=0)
    value_grad = factor * scaled - values * (factor * factor * factor) * jnp.mean(
        scaled * values, axis=-1, keepdims=True
    )
    return (value_grad, gain_grad)


def contract_rows(left, right):
    return lax.dot_general(
        left, right, (((0,), (0,)), ((), ())), preferred_element_type=jnp.float32
    )


def contract_cols(left, right):
    return lax.dot_general(
        left, right, (((1,), (1,)), ((), ())), preferred_element_type=jnp.float32
    )


def join_prefix(earlier, later):
    keep_doc = later[5] > 0.5
    keep_seg = later[4] > 0.5
    full = tuple(
        (jnp.where(keep_doc, late, early + late) for early, late in zip(earlier[0:2], later[0:2]))
    )
    done = tuple(
        (
            jnp.where(keep_seg, jnp.where(keep_doc, late, early_full + late), early_done)
            for early_full, early_done, late in zip(earlier[0:2], earlier[2:4], later[2:4])
        )
    )
    return full + done + (jnp.maximum(earlier[4], later[4]), jnp.maximum(earlier[5], later[5]))


def join_suffix(earlier, later):
    lower_doc = later[5] > 0.5
    lower_seg = later[4] > 0.5
    full = tuple(
        (
            jnp.where(lower_doc, lower, lower + upper)
            for upper, lower in zip(earlier[0:2], later[0:2])
        )
    )
    tail = tuple(
        (
            jnp.where(
                lower_seg, jnp.where(lower_doc, lower_tail, lower_tail + upper_full), upper_tail
            )
            for upper_full, upper_tail, lower_tail in zip(earlier[0:2], earlier[2:4], later[2:4])
        )
    )
    return full + tail + (jnp.maximum(earlier[4], later[4]), jnp.maximum(earlier[5], later[5]))


def body(
    layer_input,
    first_gain,
    in_weight,
    out_weight,
    mix_gate,
    second_gain,
    gate_up,
    down_weight,
    document_starts,
    cotangent,
):
    tokens = layer_input.shape[0]
    width = layer_input.shape[1]
    group = SEG // tokens
    scale = 1.0 / math.sqrt(DH)
    position = lax.axis_index("fsdp")
    offset = position % group
    segment = position // group
    single_float = jnp.float32
    gain_all, in_all, out_all, mix_all = (
        lax.all_gather(first_gain, "fsdp", axis=0, tiled=True),
        lax.all_gather(in_weight, "fsdp", axis=0, tiled=True),
        lax.all_gather(out_weight, "fsdp", axis=0, tiled=True),
        lax.all_gather(mix_gate, "fsdp", axis=0, tiled=True),
    )
    inputs = layer_input.astype(single_float)
    first_gain_f = gain_all.astype(single_float)
    normed, first_factor = norm_forward(inputs, first_gain_f)
    normed_low = normed.astype(jnp.bfloat16)
    projected = jnp.dot(normed_low, in_all, preferred_element_type=single_float).astype(
        jnp.bfloat16
    )
    query = projected[:, :width]
    key = projected[:, width : 2 * width]
    value = projected[:, 2 * width :]
    query_heads = query.reshape(tokens, H, DH)
    key_heads = key.reshape(tokens, H, DH)
    value_head_count = value.reshape(tokens, H, DH)
    pair = jnp.stack([key, value])
    pieces = [pair]
    for distance in range(1, group):
        pieces.append(from_behind(pair, "fsdp", distance))
    window = jnp.stack(pieces)
    key_flat = window[:, 0].reshape(group * tokens, H, DH)
    value_flat = window[:, 1].reshape(group * tokens, H, DH)
    key_index = jnp.arange(group * tokens, dtype=jnp.int32)
    distance_of = key_index // tokens
    within = key_index % tokens
    query_index = jnp.arange(tokens, dtype=jnp.int32)
    allowed = (distance_of[None, :] <= offset) & (
        within[None, :] - distance_of[None, :] * tokens <= query_index[:, None]
    )

    def attention_scores():
        raw = (
            jnp.einsum("qhc,khc->hqk", query_heads, key_flat, preferred_element_type=single_float)
            * scale
        )
        return jnp.where(allowed[None], raw, -1e30)

    scores = attention_scores()
    top = jnp.max(scores, axis=-1, keepdims=True)
    expo = jnp.exp(scores - top)
    total = jnp.sum(expo, axis=-1, keepdims=True)
    log_total = top + jnp.log(total)
    probs_low = (expo / total).astype(jnp.bfloat16)
    local_out = jnp.einsum(
        "hqk,khc->qhc", probs_low, value_flat, preferred_element_type=single_float
    )
    query_float = query_heads.astype(single_float)
    key_float = key_heads.astype(single_float)
    query_feature = feature(query_float).astype(jnp.bfloat16)
    key_feature_map = feature(key_float).astype(jnp.bfloat16)
    memory_update = jnp.einsum(
        "lwc,lwa->wca", key_feature_map, value_head_count, preferred_element_type=single_float
    )
    key_feature_single = key_feature_map.astype(single_float)
    count = jnp.sum(key_feature_single, axis=0)
    seg_start = offset == 0
    flag = lax.dynamic_index_in_dim(document_starts[0], segment, 0, keepdims=False)
    doc_start = seg_start & ((segment == 0) | (flag > 0))
    seg_flag = seg_start.astype(single_float)
    doc_flag = doc_start.astype(single_float)
    zero_state = jnp.zeros((H, DH, DH), single_float)
    zero_norm = jnp.zeros((H, DH), single_float)
    zero_flag = jnp.zeros((), single_float)
    identity = (zero_state, zero_norm, zero_state, zero_norm, zero_flag, zero_flag)
    prefix = carried_in(
        (memory_update, count, zero_state, zero_norm, seg_flag, doc_flag),
        "fsdp",
        join_prefix,
        identity,
    )
    memory_matrix = jnp.where(doc_start, zero_state, jnp.where(seg_start, prefix[0], prefix[2]))
    normal = jnp.where(doc_start, zero_norm, jnp.where(seg_start, prefix[1], prefix[3]))
    query_feature_single = query_feature.astype(single_float)
    numerator = jnp.einsum(
        "ier,erj->iej", query_feature_single, memory_matrix, precision=highest_precision
    )
    raw_denom = jnp.einsum("thk,hk->th", query_feature_single, normal, precision=highest_precision)
    denom = jnp.maximum(raw_denom, 1.0)
    memory_out = numerator / denom[..., None]
    mix = jax.nn.sigmoid(mix_all.astype(single_float)).reshape(H, DH)
    combined = mix * memory_out + (1.0 - mix) * local_out
    combined_low = combined.reshape(tokens, width).astype(jnp.bfloat16)
    attended = jnp.dot(combined_low, out_all, preferred_element_type=single_float)
    middle = inputs + attended
    second_all, gate_up_all, down_all = (
        lax.all_gather(second_gain, "fsdp", axis=0, tiled=True),
        lax.all_gather(gate_up, "fsdp", axis=0, tiled=True),
        lax.all_gather(down_weight, "fsdp", axis=0, tiled=True),
    )
    second_gain_f = second_all.astype(single_float)
    hidden, second_factor = norm_forward(middle, second_gain_f)
    hidden_low = hidden.astype(jnp.bfloat16)
    both = jnp.dot(hidden_low, gate_up_all, preferred_element_type=single_float)
    gate_part = both[:, :FF]
    up_part = both[:, FF:]
    sigma = jax.nn.sigmoid(gate_part)
    silu = gate_part * sigma
    activated = (silu * up_part).astype(jnp.bfloat16)
    feed_out = contract_cols(activated, down_all)
    layer_output = (middle + feed_out).astype(jnp.bfloat16)
    upstream = cotangent.astype(single_float)
    gate_up_back, down_back = (
        lax.all_gather(gate_up, "fsdp", axis=0, tiled=True),
        lax.all_gather(down_weight, "fsdp", axis=0, tiled=True),
    )
    out_grad_low = upstream.astype(jnp.bfloat16)
    act_grad = jnp.dot(out_grad_low, down_back, preferred_element_type=single_float)
    silu_slope = sigma * (1.0 + gate_part * (1.0 - sigma))
    feed_grad_low = jnp.concatenate(
        [act_grad * up_part * silu_slope, act_grad * silu], axis=1
    ).astype(jnp.bfloat16)
    hidden_grad = contract_cols(feed_grad_low, gate_up_back)
    feed_grads = lax.psum_scatter(
        jnp.concatenate(
            [contract_rows(hidden_low, feed_grad_low), contract_rows(out_grad_low, activated)],
            axis=1,
        ),
        "fsdp",
        scatter_dimension=0,
        tiled=True,
    )
    middle_norm_grad, second_gain_local = norm_backward(
        middle, second_factor, second_gain_f, hidden_grad
    )
    middle_grad = upstream + middle_norm_grad
    in_back, out_back = (
        lax.all_gather(in_weight, "fsdp", axis=0, tiled=True),
        lax.all_gather(out_weight, "fsdp", axis=0, tiled=True),
    )
    attended_grad_low = middle_grad.astype(jnp.bfloat16)
    combined_grad = contract_cols(attended_grad_low, out_back).reshape(tokens, H, DH)
    out_weight_local = contract_rows(combined_low, attended_grad_low)
    mix_local = jnp.sum(combined_grad * (memory_out - local_out), axis=0) * mix * (1.0 - mix)
    memory_grad = combined_grad * mix
    local_grad_low = (combined_grad * (1.0 - mix)).astype(jnp.bfloat16)
    numerator_gradient = memory_grad / denom[..., None]
    denom_grad = -jnp.sum(memory_grad * memory_out, axis=-1) / denom
    raw_grad = jnp.where(raw_denom > 1.0, denom_grad, 0.0)
    query_feature_grad = (
        jnp.einsum("arp,rfp->arf", numerator_gradient, memory_matrix, precision=highest_precision)
        + raw_grad[..., None] * normal[None]
    )
    state_gradient = jnp.einsum(
        "lwc,lwa->wca", query_feature_single, numerator_gradient, precision=highest_precision
    )
    normal_grad = jnp.einsum(
        "th,thk->hk", raw_grad, query_feature_single, precision=highest_precision
    )
    lone_full = (
        jnp.where(doc_start, zero_state, state_gradient),
        jnp.where(doc_start, zero_norm, normal_grad),
    )
    opens = seg_start & jnp.logical_not(doc_start)
    lone_tail = (
        jnp.where(opens, state_gradient, zero_state),
        jnp.where(opens, normal_grad, zero_norm),
    )
    suffix = carried_in_2(
        lone_full + lone_tail + (seg_flag, doc_flag), "fsdp", join_suffix, identity
    )
    memory_update_gradient = suffix[2]
    count_gradient = suffix[3]
    value_single = value_head_count.astype(single_float)
    key_feature_grad = (
        jnp.einsum(
            "arp,rfp->arf", value_single, memory_update_gradient, precision=highest_precision
        )
        + count_gradient[None]
    )
    value_memory_gradient = jnp.einsum(
        "ier,erj->iej", key_feature_single, memory_update_gradient, precision=highest_precision
    )
    query_memory_grad = query_feature_grad * feature_slope(query_float)
    key_memory_grad = key_feature_grad * feature_slope(key_float)
    scores = attention_scores()
    probs = jnp.exp(scores - log_total)
    probs_low = probs.astype(jnp.bfloat16)
    prob_grad = jnp.einsum(
        "qhc,khc->hqk", local_grad_low, value_flat, preferred_element_type=single_float
    )
    row_term = jnp.sum(probs * prob_grad, axis=-1, keepdims=True)
    score_grad_low = (probs * (prob_grad - row_term)).astype(jnp.bfloat16)
    query_attend_grad = (
        jnp.einsum("hqk,khc->qhc", score_grad_low, key_flat, preferred_element_type=single_float)
        * scale
    )
    key_window_grad = (
        jnp.einsum("hqk,qhc->khc", score_grad_low, query_heads, preferred_element_type=single_float)
        * scale
    )
    value_window_grad = jnp.einsum(
        "hqk,qhc->khc", probs_low, local_grad_low, preferred_element_type=single_float
    )
    window_grad = jnp.stack(
        [
            key_window_grad.reshape(group, tokens, width),
            value_window_grad.reshape(group, tokens, width),
        ],
        axis=1,
    )
    returned = window_grad[0]
    for distance in range(1, group):
        returned = returned + from_behind(
            window_grad[distance].astype(jnp.bfloat16), "fsdp", -distance
        ).astype(jnp.float32)
    query_grad = (query_attend_grad + query_memory_grad).reshape(tokens, width)
    key_grad = returned[0] + key_memory_grad.reshape(tokens, width)
    value_grad = returned[1] + value_memory_gradient.reshape(tokens, width)
    projected_grad = jnp.concatenate([query_grad, key_grad, value_grad], axis=1).astype(
        jnp.bfloat16
    )
    in_weight_local = contract_rows(normed_low, projected_grad)
    normed_grad = contract_cols(projected_grad, in_back)
    input_norm_grad, first_gain_local = norm_backward(
        inputs, first_factor, first_gain_f, normed_grad
    )
    input_grad = middle_grad + input_norm_grad
    first_part, in_part, out_part, mix_part, second_part = (
        lax.psum_scatter(first_gain_local, "fsdp", scatter_dimension=0, tiled=True),
        lax.psum_scatter(in_weight_local, "fsdp", scatter_dimension=0, tiled=True),
        lax.psum_scatter(out_weight_local, "fsdp", scatter_dimension=0, tiled=True),
        lax.psum_scatter(mix_local.reshape(width), "fsdp", scatter_dimension=0, tiled=True),
        lax.psum_scatter(second_gain_local, "fsdp", scatter_dimension=0, tiled=True),
    )
    first_sum, in_sum, out_sum, mix_sum, second_sum, feed_sum = (
        lax.psum(first_part.astype(jnp.bfloat16), "dp").astype(jnp.float32),
        lax.psum(in_part.astype(jnp.bfloat16), "dp").astype(jnp.float32),
        lax.psum(out_part.astype(jnp.bfloat16), "dp").astype(jnp.float32),
        lax.psum(mix_part.astype(jnp.bfloat16), "dp").astype(jnp.float32),
        lax.psum(second_part.astype(jnp.bfloat16), "dp").astype(jnp.float32),
        lax.psum(feed_grads.astype(jnp.bfloat16), "dp").astype(jnp.float32),
    )
    gate_up_grad = feed_sum[:, : 2 * FF]
    down_weight_grad = feed_sum[:, 2 * FF :]
    return (
        layer_output,
        input_grad,
        first_sum,
        in_sum,
        out_sum,
        mix_sum,
        second_sum,
        gate_up_grad,
        down_weight_grad,
    )


def solution(mesh):
    return jax.shard_map(
        body,
        mesh=mesh,
        in_specs=(
            P(("dp", "fsdp"), None),
            P("fsdp"),
            P("fsdp", None),
            P("fsdp", None),
            P("fsdp"),
            P("fsdp"),
            P("fsdp", None),
            P("fsdp", None),
            P("dp", None),
            P(("dp", "fsdp"), None),
        ),
        out_specs=(
            P(("dp", "fsdp"), None),
            P(("dp", "fsdp"), None),
            P("fsdp"),
            P("fsdp", None),
            P("fsdp", None),
            P("fsdp"),
            P("fsdp"),
            P("fsdp", None),
            P("fsdp", None),
        ),
        check_vma=False,
    )
```

profile of v0, /device:TPU:0, one launch (start us, length us, event | category | flops | bytes accessed | tf_op | source)
XLA Modules:
  0.0 4029.8 jit_solution(742388443887060821)
XLA Ops:
  8.0 23.2 all-gather.6
  33.0 107.9 %all-gather.16.cloned.1.call-done = bf16[2048,6144]{1,0:T(8,128)(2,1)} async-done(((bf16[128,6144]{1,0:T(8,128)(2,1)}), bf16[2048,6144]{1,0:T(8,128)(2,1)}) %all-gather.16.cloned.1.call-update) | async-done | bytes 25165840 | tf_op jit(solution)/shard_map/all_gather | solution.py:162
  140.9 11.9 convolution_convert_fusion
  162.9 20.4 all-gather.5
  190.0 80.3 %all-reduce.7 = (bf16[16]{0:T(256)(128)(2,1)S(1)}, bf16[16]{0:T(256)(128)(2,1)S(1)}) all-reduce(bf16[16]{0:T(256)(128)(2,1)S(1)} %dynamic-update-slice, bf16[16]{0:T(256)(128)(2,1)S(1)} %dynamic-update-slice.1), channel_id=1, replica_groups=mesh['dp'=2,'fsdp'=16] {'fsdp'}, use_global_device_ids=true, to_apply=%add | all-reduce | flops 32 | bytes 128
  270.3 18.4 all-gather.7
  293.6 5.4 collective-permute-start.2
  300.3 106.4 %all_gather.89 = bf16[16,16,128]{2,1,0:T(8,128)(2,1)S(1)} all-gather(bf16[1,16,128]{2,1,0:T(8,128)(2,1)S(1)} %bitcast.275), channel_id=1, replica_groups=mesh['dp'=2,'fsdp'=16] {'fsdp'}, dimensions={0}, use_global_device_ids=true | all-gather | bytes 69632 | tf_op jit(solution)/shard_map/all_gather | solution.py:27
  406.8 68.7 %collective-permute-start.3 = (bf16[2,128,2048]{2,1,0:T(8,128)(2,1)}, bf16[2,128,2048]{2,1,0:T(8,128)(2,1)S(1)}, u32[]{:S(2)}, u32[]{:S(2)}) collective-permute-start(bf16[2,128,2048]{2,1,0:T(8,128)(2,1)} %pad_maximum_fusion.6), channel_id=1, source_target_pairs={{0,4},{1,5},{2,6},{3,7},{4,8},{5,9},{6,10},{7,11},{8,12},{9,13},{1... | collective-permute-start | bytes 3145736 | tf_op jit(solution)/shard_map/ppermute | solution.py:21
  477.8 5.3 collective-permute-start.6
  487.8 33.9 collective-permute-done.3
  527.4 39.0 collective-permute-done.6
  578.5 6.8 copy.116
  599.7 6.2 add_convert_fusion
  605.9 5.1 multiply_reduce_fusion.5
  611.0 134.9 %all-gather.20.cloned.1.call-done = bf16[2048,16384]{1,0:T(8,128)(2,1)} async-done(((bf16[128,16384]{1,0:T(8,128)(2,1)}), bf16[2048,16384]{1,0:T(8,128)(2,1)}) %all-gather.20.cloned.1.call-update) | async-done | bytes 67108880 | tf_op jit(solution)/shard_map/all_gather | solution.py:250
  745.9 26.2 fusion.96
  772.1 207.6 %all-gather.22.cloned.1.call-done = bf16[2048,8192]{1,0:T(8,128)(2,1)} async-done(((bf16[128,8192]{1,0:T(8,128)(2,1)}), bf16[2048,8192]{1,0:T(8,128)(2,1)}) %all-gather.22.cloned.1.call-update) | async-done | bytes 33554448 | tf_op jit(solution)/shard_map/all_gather | solution.py:251
  979.8 18.7 multiply_convert_fusion.2
  998.5 31.2 multiply_reduce_fusion.1
  1031.5 6.1 fusion.71
  1041.0 8.4 fusion.69
  1049.5 4.5 fusion.5
  1054.1 5.3 copy.149
  1059.4 9.3 copy.120
  1068.7 6.2 multiply_reduce_fusion
  1074.9 4.4 multiply_convert_fusion
  1082.6 5.5 copy.148
  1088.1 9.4 copy.119
  1097.5 6.9 fusion.2
  1117.2 4.7 fusion.29
  1123.2 38.3 collective-permute-done.13
  1169.7 152.7 %all-gather.4 = bf16[256,128]{1,0:T(8,128)(2,1)S(1)} all-gather(bf16[16,128]{1,0:T(8,128)(2,1)S(1)} %get-tuple-element.493), channel_id=6, replica_groups=mesh['dp'=2,'fsdp'=16] {'fsdp'}, dimensions={0}, use_global_device_ids=true | all-gather | bytes 69632 | tf_op jit(solution)/shard_map/all_gather | solution.py:51
  1322.4 138.7 %all-gather.2 = bf16[256,128]{1,0:T(8,128)(2,1)S(1)} all-gather(bf16[16,128]{1,0:T(8,128)(2,1)S(1)} %get-tuple-element.494), channel_id=4, replica_groups=mesh['dp'=2,'fsdp'=16] {'fsdp'}, dimensions={0}, use_global_device_ids=true | all-gather | bytes 69632 | tf_op jit(solution)/shard_map/all_gather | solution.py:51
  1461.1 6.9 fusion.24
  1468.3 67.5 %while.44 = (s32[]{:T(128)}, f32[16,128,128]{2,1,0:T(8,128)S(1)}, f32[16,128]{1,0:T(8,128)S(1)}, f32[16,128,128]{2,1,0:T(8,128)S(1)}, f32[16,128]{1,0:T(8,128)S(...) while((s32[]{:T(128)}, f32[16,128,128]{2,1,0:T(8,128)S(1)}, ...), condition=%wide.region_11.12_spmd, body=%wide.region_10.11_spmd.sunk | while | flops 1849352 | bytes 5284093 | solution.py:68
  1547.6 20.8 fusion.60
  1570.0 43.4 %convolution_bitcast_fusion = f32[2048,8192]{1,0:T(8,128)} fusion(bf16[128,8192]{1,0:T(8,128)(2,1)S(1)} %copy-done.16, bf16[128,2048]{1,0:T(8,128)(2,1)} %param.23), kind=kOutput, calls=%fused_computation.11 | convolution fusion | flops 4294967296 | bytes 69730304 | tf_op jit(solution)/shard_map/dot_general | solution.py:94
  1613.4 52.2 %fusion.13 = f32[2048,16384]{1,0:T(8,128)} fusion(bf16[128,8192]{1,0:T(8,128)(2,1)} %get-tuple-element.472, bf16[128,8192]{1,0:T(8,128)(2,1)} %copy-done.19, f32[128,2048]{1,0:T(8,128)S(1)} %copy-done.3, f32[2048]{0:T(1024)S(1)} %bitcast.262, f32[128]{0:T(128)S(1)} %copy-done.40), kind=kOutput, calls=%fused_computation.40 | convolution fusion | flops 8599109632 | bytes 139469312 | tf_op jit(solution)/shard_map/dot_general | solution.py:94
  1665.6 134.4 %pad_maximum_fusion = f32[2048,24576]{1,0:T(8,128)} fusion(f32[2048,8192]{1,0:T(8,128)} %convolution_bitcast_fusion, f32[2048,16384]{1,0:T(8,128)} %fusion.13), kind=kLoop, calls=%fused_computation.10 | loop fusion | flops 50331648 | bytes 402653184 | tf_op jit(solution)/shard_map/concatenate | solution.py:277
  1802.4 230.8 %reduce-scatter.6.cloned.1.call-done = f32[128,6144]{1,0:T(8,128)} async-done(((f32[2048,6144]{1,0:T(8,128)}), f32[128,6144]{1,0:T(8,128)}) %reduce-scatter.6.cloned.1.call-update) | async-done | bytes 3145744 | tf_op jit(solution)/shard_map/reduce_scatter | solution.py:383
  2036.4 1768.6 %reduce-scatter.10.cloned.1.call-done = f32[128,24576]{1,0:T(8,128)} async-done(((f32[2048,24576]{1,0:T(8,128)}), f32[128,24576]{1,0:T(8,128)}) %reduce-scatter.10.cloned.1.call-update) | async-done | bytes 12582928
  3805.0 8.0 convert_element_type.368
  3814.3 18.3 fusion.15
  3832.7 14.9 fusion.52
  3847.5 58.6 %all-reduce.6 = (bf16[2048]{0:T(1024)(128)(2,1)S(1)}, bf16[2048]{0:T(1024)(128)(2,1)S(1)}, bf16[2048]{0:T(1024)(128)(2,1)S(1)}) all-reduce(f32[2048]{0:T(1024)S(1)} %get-tuple-element.404, f32[2048]{0:T(1024)S(1)} %fusion.75, f32[2048]{0:T(1024)S(1)} %copy-done.43), channel_id=7, replica_groups=mesh['dp'=2,'fsdp'=16] {'fsdp'}, use_global_device_ids=true, to_apply=%region_14.15.clone | all-reduce | flops 6144 | bytes 36864
  3906.3 4.9 all-reduce.8
  3915.4 96.1 %all-reduce.12.cloned.1.call-done = (bf16[128,6144]{1,0:T(8,128)(2,1)}, bf16[128,2048]{1,0:T(8,128)(2,1)}, bf16[128,24576]{1,0:T(8,128)(2,1)}) async-done(((bf16[128,6144]{1,0:T(8,128)(2,1)}, bf16[128,2048]{1,0:T(8,128)(2,1)}, bf16[128,24576]{1,0:T(8,128)(2,1)}), (bf16[128,6144]{1,0:T(8,128)(2,1)}, bf16[128,2048]{1,0:T(8,128)(2,1)}, bf16[128,24576]{1,0:T(8,128)(2,1)})) %all-reduce.12.cloned.1.call-update) | async-done | bytes 8388624 | tf_op jit(solution)/shard_map/psum | solution.py:390
  (310 shorter events, 176.8 us)
Async XLA Ops:
  7.2 133.8 %all-gather.16.cloned.1.call-start = ((), (), s32[]{:S(2)}) async-start(), calls=%async_computation.3 | async-start | bytes 26738688 | tf_op jit(solution)/shard_map/all_gather | solution.py:162
  7.9 586.8 %all-gather.24.cloned.1.call-start = ((), (), s32[]{:S(2)}) async-start(), calls=%async_computation.9 | async-start | bytes 8912896 | tf_op jit(solution)/shard_map/all_gather | solution.py:27
  31.2 121.7 %copy-start.35 = (f32[16,1,128]{2,1,0:T(1,128)}, f32[16,1,128]{2,1,0:T(1,128)S(1)}, u32[]{:S(2)}) copy-start(f32[16,1,128]{2,1,0:T(1,128)S(1)} %convert_element_type.378) | copy-start | bytes 24580
  33.0 119.9 %copy-start.47 = (f32[128]{0:T(128)}, f32[128]{0:T(128)S(1)}, u32[]{:S(2)}) copy-start(f32[128]{0:T(128)S(1)} %get-tuple-element.498) | copy-start | bytes 1540
  154.3 115.9 %copy-start.55 = (bf16[128]{0:T(256)(128)(2,1)S(1)}, bf16[128]{0:T(256)(128)(2,1)}, u32[]{:S(2)}) copy-start(bf16[128]{0:T(256)(128)(2,1)} %param.19) | copy-start | bytes 772
  154.7 323.1 %copy-start.17 = (f32[128,2048]{0,1:T(8,128)}, f32[128,2048]{0,1:T(8,128)S(1)}, u32[]{:S(2)}) copy-start(f32[128,2048]{0,1:T(8,128)S(1)} %copy.143) | copy-start | bytes 3145732
  154.7 145.3 %copy-start.32 = (bf16[128,2048]{1,0:T(8,128)(2,1)S(1)}, bf16[128,2048]{1,0:T(8,128)(2,1)}, u32[]{:S(2)}) copy-start(bf16[128,2048]{1,0:T(8,128)(2,1)} %get-tuple-element.488) | copy-start | bytes 1572868
  157.5 448.4 %all-gather.18.cloned.1.call-start = ((), (), s32[]{:S(2)}) async-start(), calls=%async_computation.4 | async-start | bytes 8912896 | tf_op jit(solution)/shard_map/all_gather | solution.py:163
  158.3 587.6 %all-gather.20.cloned.1.call-start = ((), (), s32[]{:S(2)}) async-start(), calls=%async_computation.5 | async-start | bytes 71303168 | tf_op jit(solution)/shard_map/all_gather | solution.py:250
  158.8 820.9 %all-gather.22.cloned.1.call-start = ((), (), s32[]{:S(2)}) async-start(), calls=%async_computation.6 | async-start | bytes 35651584 | tf_op jit(solution)/shard_map/all_gather | solution.py:251
  159.4 1308.6 %all-gather.28.cloned.1.call-start = ((), (), s32[]{:S(2)}) async-start(), calls=%async_computation.11 | async-start | bytes 8912896 | tf_op jit(solution)/shard_map/all_gather | solution.py:51
  183.3 116.7 %copy-start.41 = (bf16[16,1,128]{2,1,0:T(2,128)(2,1)}, bf16[16,1,128]{2,1,0:T(2,128)(2,1)S(1)}, u32[]{:S(2)}) copy-start(bf16[16,1,128]{2,1,0:T(2,128)(2,1)S(1)} %all-gather.5) | copy-start | bytes 12292
  184.4 222.3 %collective-permute-start = (bf16[2,128,2048]{2,1,0:T(8,128)(2,1)}, bf16[2,128,2048]{2,1,0:T(8,128)(2,1)}, u32[]{:S(2)}, u32[]{:S(2)}) collective-permute-start(bf16[2,128,2048]{2,1,0:T(8,128)(2,1)} %pad_maximum_fusion.6), channel_id=1, source_target_pairs={{0,1},{1,2},{2,3},{3,4},{4,5},{5,6},{6,7},{7,8},{8,9},{9,10},{10,1... | collective-permute-start | bytes 3145736 | tf_op jit(solution)/shard_map/ppermute | solution.py:21
  187.6 290.2 %collective-permute-start.1 = (bf16[2,128,2048]{2,1,0:T(8,128)(2,1)}, bf16[2,128,2048]{2,1,0:T(8,128)(2,1)}, u32[]{:S(2)}, u32[]{:S(2)}) collective-permute-start(bf16[2,128,2048]{2,1,0:T(8,128)(2,1)} %pad_maximum_fusion.6), channel_id=1, source_target_pairs={{0,2},{1,3},{2,4},{3,5},{4,6},{5,7},{6,8},{7,9},{8,10},{9,11},{10,... | collective-permute-start | bytes 3145736 | tf_op jit(solution)/shard_map/ppermute | solution.py:21
  288.7 741.0 %copy-start.25 = (f32[16,1,128]{2,1,0:T(1,128)}, f32[16,1,128]{2,1,0:T(1,128)S(1)}, u32[]{:S(2)}) copy-start(f32[16,1,128]{2,1,0:T(1,128)S(1)} %convert_element_type.379) | copy-start | bytes 24580
  288.8 236.3 %collective-permute-start.5 = (bf16[2,128,2048]{2,1,0:T(8,128)(2,1)}, bf16[2,128,2048]{2,1,0:T(8,128)(2,1)}, u32[]{:S(2)}, u32[]{:S(2)}) collective-permute-start(bf16[2,128,2048]{2,1,0:T(8,128)(2,1)} %pad_maximum_fusion.6), channel_id=1, source_target_pairs={{0,6},{1,7},{2,8},{3,9},{4,10},{5,11},{6,12},{7,13},{8,14},{9,15},... | collective-permute-start | bytes 3145736 | tf_op jit(solution)/shard_map/ppermute | solution.py:21
  291.1 231.7 %collective-permute-start.4 = (bf16[2,128,2048]{2,1,0:T(8,128)(2,1)}, bf16[2,128,2048]{2,1,0:T(8,128)(2,1)}, u32[]{:S(2)}, u32[]{:S(2)}) collective-permute-start(bf16[2,128,2048]{2,1,0:T(8,128)(2,1)} %pad_maximum_fusion.6), channel_id=1, source_target_pairs={{0,5},{1,6},{2,7},{3,8},{4,9},{5,10},{6,11},{7,12},{8,13},{9,14},{... | collective-permute-start | bytes 3145736 | tf_op jit(solution)/shard_map/ppermute | solution.py:21
  293.6 191.9 %collective-permute-start.2 = (bf16[2,128,2048]{2,1,0:T(8,128)(2,1)}, bf16[2,128,2048]{2,1,0:T(8,128)(2,1)}, u32[]{:S(2)}, u32[]{:S(2)}) collective-permute-start(bf16[2,128,2048]{2,1,0:T(8,128)(2,1)} %pad_maximum_fusion.6), channel_id=1, source_target_pairs={{0,3},{1,4},{2,5},{3,6},{4,7},{5,8},{6,9},{7,10},{8,11},{9,12},{10... | collective-permute-start | bytes 3145736 | tf_op jit(solution)/shard_map/ppermute | solution.py:21
  300.3 295.6 %copy-start.20 = (bf16[128,2048]{0,1:T(8,128)(2,1)}, bf16[128,2048]{0,1:T(8,128)(2,1)S(1)}, u32[]{:S(2)}) copy-start(bf16[128,2048]{0,1:T(8,128)(2,1)S(1)} %copy.144) | copy-start | bytes 1572868
  406.8 115.0 %collective-permute-start.3 = (bf16[2,128,2048]{2,1,0:T(8,128)(2,1)}, bf16[2,128,2048]{2,1,0:T(8,128)(2,1)S(1)}, u32[]{:S(2)}, u32[]{:S(2)}) collective-permute-start(bf16[2,128,2048]{2,1,0:T(8,128)(2,1)} %pad_maximum_fusion.6), channel_id=1, source_target_pairs={{0,4},{1,5},{2,6},{3,7},{4,8},{5,9},{6,10},{7,11},{8,12},{9,13},{1... | collective-permute-start | bytes 3145736 | tf_op jit(solution)/shard_map/ppermute | solution.py:21
  477.8 88.6 %collective-permute-start.6 = (bf16[2,128,2048]{2,1,0:T(8,128)(2,1)}, bf16[2,128,2048]{2,1,0:T(8,128)(2,1)S(1)}, u32[]{:S(2)}, u32[]{:S(2)}) collective-permute-start(bf16[2,128,2048]{2,1,0:T(8,128)(2,1)} %pad_maximum_fusion.6), channel_id=1, source_target_pairs={{0,7},{1,8},{2,9},{3,10},{4,11},{5,12},{6,13},{7,14},{8,15},{16,23... | collective-permute-start | bytes 3145736 | tf_op jit(solution)/shard_map/ppermute | solution.py:21
  611.0 418.7 %copy-start.2 = (f32[128,2048]{1,0:T(8,128)}, f32[128,2048]{1,0:T(8,128)S(1)}, u32[]{:S(2)}) copy-start(f32[128,2048]{1,0:T(8,128)S(1)} %get-tuple-element.506) | copy-start | bytes 3145732
  611.0 418.7 %copy-start.39 = (f32[128]{0:T(128)}, f32[128]{0:T(128)S(1)}, u32[]{:S(2)}) copy-start(f32[128]{0:T(128)S(1)} %get-tuple-element.500) | copy-start | bytes 1540
  998.5 31.2 copy-start.19
  1040.2 427.8 %all-gather.26.cloned.1.call-start = ((), (), s32[]{:S(2)}) async-start(), calls=%async_computation.10 | async-start | bytes 8912896 | tf_op jit(solution)/shard_map/all_gather | solution.py:51
  1041.0 759.4 %reduce-scatter.8.cloned.1.call-start = ((), (), s32[]{:S(2)}) async-start(), calls=%async_computation.8 | async-start | bytes 17825792 | tf_op jit(solution)/shard_map/reduce_scatter | solution.py:384
  1049.5 983.7 %reduce-scatter.6.cloned.1.call-start = ((), (), s32[]{:S(2)}) async-start(), calls=%async_computation.7 | async-start | bytes 53477376 | tf_op jit(solution)/shard_map/reduce_scatter | solution.py:383
  1107.4 55.4 %copy-start.46 = (f32[16,1,128]{2,1,0:T(1,128)S(1)}, f32[16,1,128]{2,1,0:T(1,128)}, u32[]{:S(2)}) copy-start(f32[16,1,128]{2,1,0:T(1,128)} %copy-done.45) | copy-start | bytes 24580
  1107.4 55.4 %copy-start.7 = (f32[16,128,128]{2,1,0:T(8,128)S(1)}, f32[16,128,128]{2,1,0:T(8,128)}, u32[]{:S(2)}) copy-start(f32[16,128,128]{2,1,0:T(8,128)} %copy-done.6) | copy-start | bytes 3145732
  1107.4 55.4 %copy-start.9 = (f32[16,128,128]{2,1,0:T(8,128)S(1)}, f32[16,128,128]{2,1,0:T(8,128)}, u32[]{:S(2)}) copy-start(f32[16,128,128]{2,1,0:T(8,128)} %copy-done.8) | copy-start | bytes 3145732
  1107.4 55.4 %copy-start.51 = (f32[16,128]{1,0:T(8,128)S(1)}, f32[16,128]{1,0:T(8,128)}, u32[]{:S(2)}) copy-start(f32[16,128]{1,0:T(8,128)} %copy-done.50) | copy-start | bytes 24580
  1107.4 14.5 collective-permute-start.7
  1108.9 52.7 %collective-permute-start.13 = (bf16[2,128,2048]{2,1,0:T(8,128)(2,1)}, bf16[2,128,2048]{2,1,0:T(8,128)(2,1)}, u32[]{:S(2)}, u32[]{:S(2)}) collective-permute-start(bf16[2,128,2048]{2,1,0:T(8,128)(2,1)} %get-tuple-element.474), channel_id=1, source_target_pairs={{7,0},{8,1},{9,2},{10,3},{11,4},{12,5},{13,6},{14,7},{15,8},{23,16... | collective-permute-start | bytes 3145736 | tf_op jit(solution)/shard_map/ppermute | solution.py:21
  1110.2 52.7 %copy-start.22 = (bf16[128,2048]{0,1:T(8,128)(2,1)S(1)}, bf16[128,2048]{0,1:T(8,128)(2,1)}, u32[]{:S(2)}) copy-start(bf16[128,2048]{0,1:T(8,128)(2,1)} %copy-done.20) | copy-start | bytes 1572868
  1110.2 350.9 %collective-permute-start.12 = (bf16[2,128,2048]{2,1,0:T(8,128)(2,1)}, bf16[2,128,2048]{2,1,0:T(8,128)(2,1)}, u32[]{:S(2)}, u32[]{:S(2)}) collective-permute-start(bf16[2,128,2048]{2,1,0:T(8,128)(2,1)} %get-tuple-element.475), channel_id=1, source_target_pairs={{6,0},{7,1},{8,2},{9,3},{10,4},{11,5},{12,6},{13,7},{14,8},{15,9},... | collective-permute-start | bytes 3145736 | tf_op jit(solution)/shard_map/ppermute | solution.py:21
  1111.6 349.5 %collective-permute-start.11 = (bf16[2,128,2048]{2,1,0:T(8,128)(2,1)}, bf16[2,128,2048]{2,1,0:T(8,128)(2,1)}, u32[]{:S(2)}, u32[]{:S(2)}) collective-permute-start(bf16[2,128,2048]{2,1,0:T(8,128)(2,1)} %get-tuple-element.476), channel_id=1, source_target_pairs={{5,0},{6,1},{7,2},{8,3},{9,4},{10,5},{11,6},{12,7},{13,8},{14,9},{... | collective-permute-start | bytes 3145736 | tf_op jit(solution)/shard_map/ppermute | solution.py:21
  1112.9 348.2 %collective-permute-start.10 = (bf16[2,128,2048]{2,1,0:T(8,128)(2,1)}, bf16[2,128,2048]{2,1,0:T(8,128)(2,1)}, u32[]{:S(2)}, u32[]{:S(2)}) collective-permute-start(bf16[2,128,2048]{2,1,0:T(8,128)(2,1)} %get-tuple-element.477), channel_id=1, source_target_pairs={{4,0},{5,1},{6,2},{7,3},{8,4},{9,5},{10,6},{11,7},{12,8},{13,9},{1... | collective-permute-start | bytes 3145736 | tf_op jit(solution)/shard_map/ppermute | solution.py:21
  1121.9 339.2 %collective-permute-start.9 = (bf16[2,128,2048]{2,1,0:T(8,128)(2,1)}, bf16[2,128,2048]{2,1,0:T(8,128)(2,1)}, u32[]{:S(2)}, u32[]{:S(2)}) collective-permute-start(bf16[2,128,2048]{2,1,0:T(8,128)(2,1)} %get-tuple-element.478), channel_id=1, source_target_pairs={{3,0},{4,1},{5,2},{6,3},{7,4},{8,5},{9,6},{10,7},{11,8},{12,9},{13... | collective-permute-start | bytes 3145736 | tf_op jit(solution)/shard_map/ppermute | solution.py:21
  1161.5 299.6 %collective-permute-start.8 = (bf16[2,128,2048]{2,1,0:T(8,128)(2,1)}, bf16[2,128,2048]{2,1,0:T(8,128)(2,1)}, u32[]{:S(2)}, u32[]{:S(2)}) collective-permute-start(bf16[2,128,2048]{2,1,0:T(8,128)(2,1)} %get-tuple-element.479), channel_id=1, source_target_pairs={{2,0},{3,1},{4,2},{5,3},{6,4},{7,5},{8,6},{9,7},{10,8},{11,9},{12,... | collective-permute-start | bytes 3145736 | tf_op jit(solution)/shard_map/ppermute | solution.py:21
  1468.3 67.5 %copy-start.18 = (f32[128,2048]{0,1:T(8,128)S(1)}, f32[128,2048]{0,1:T(8,128)}, u32[]{:S(2)}) copy-start(f32[128,2048]{0,1:T(8,128)} %copy-done.17) | copy-start | bytes 3145732
  1547.6 20.9 copy-start.27
  1568.5 2236.5 %reduce-scatter.10.cloned.1.call-start = ((), (), s32[]{:S(2)}) async-start(), calls=%async_computation.12 | async-start | bytes 213909504
  1570.0 43.4 %copy-start.3 = (f32[128,2048]{1,0:T(8,128)S(1)}, f32[128,2048]{1,0:T(8,128)}, u32[]{:S(2)}) copy-start(f32[128,2048]{1,0:T(8,128)} %copy-done.2) | copy-start | bytes 3145732
  1570.0 43.4 %copy-start.26 = (f32[16,1,128]{2,1,0:T(1,128)S(1)}, f32[16,1,128]{2,1,0:T(1,128)}, u32[]{:S(2)}) copy-start(f32[16,1,128]{2,1,0:T(1,128)} %copy-done.25) | copy-start | bytes 24580
  1570.0 43.4 %copy-start.40 = (f32[128]{0:T(128)S(1)}, f32[128]{0:T(128)}, u32[]{:S(2)}) copy-start(f32[128]{0:T(128)} %copy-done.39) | copy-start | bytes 1540
  1800.1 2211.5 %all-reduce.12.cloned.1.call-start = ((), (), s32[]{:S(2)}) async-start(), calls=%async_computation.13 | async-start | bytes 16777216 | tf_op jit(solution)/shard_map/psum | solution.py:390
  3832.6 80.2 %copy-start.12 = (f32[128,2048]{1,0:T(8,128)S(1)}, f32[128,2048]{1,0:T(8,128)}, u32[]{:S(2)}) copy-start(f32[128,2048]{1,0:T(8,128)} %copy-done.11) | copy-start | bytes 3145732
  3832.7 80.1 %copy-start.53 = (f32[128]{0:T(128)S(1)}, f32[128]{0:T(128)}, u32[]{:S(2)}) copy-start(f32[128]{0:T(128)} %get-tuple-element.497) | copy-start | bytes 1540
  (38 other events, 349.9 us)
Sparse Core Ops, SparseCore 0:
  9.6 131.2 all-gather.15
  157.7 95.2 all-gather.23
  255.1 103.5 all-gather.17
  360.1 385.7 all-gather.19
  747.4 232.3 all-gather.21
  1040.3 74.8 all-gather.27
  1117.4 167.3 all-gather.25
  1289.0 213.6 reduce-scatter.7
  1568.6 464.5 reduce-scatter.5
  2037.3 1767.6 reduce-scatter.9
  3813.2 198.3 all-reduce.11
where the time goes:
time: 4040 us; the launch traced here: 4030 us
  waiting for transfers between devices  2660 us (66%)
  blocking collectives  604 us (15%)
  matrix products  302 us (7%)
  other arithmetic  217 us (5%)
  local copies, waits for them, and re-layouts  110 us (3%)
  starting transfers between devices  99.9 us (2%)
    unnamed x12, waiting for transfers between devices  1770 us
    all_gather x2, blocking collectives, carried_in_2(): lax.all_gather(a.astype(kind), axis)  291 us
    reduce_scatter x1, waiting for transfers between devices, body(): lax.psum_scatter(in_weight_local, 'fsdp', scatter_dimension=0, tiled=True)  231 us
    all_gather x1, waiting for transfers between devices, body(): lax.all_gather(down_weight, 'fsdp', axis=0, tiled=True)  208 us
    unnamed x2, blocking collectives  139 us
    all_gather x1, waiting for transfers between devices, body(): lax.all_gather(gate_up, 'fsdp', axis=0, tiled=True)  135 us
    concatenate x1, other arithmetic, body(): jnp.concatenate([contract_rows(hidden_low, feed_grad_low), contract_rows(...  134 us
    dot_general x4, matrix products, contract_rows(): lax.dot_general(left, right, (((0,), (0,)), ((), ())), preferred_element_...  125 us
  transfers between devices with their start and end apart: 25, of which 9 were waited for; matrix products, arithmetic and copies ran while one was open for 13% of the time, Pallas kernels for 0%

commit v1 on v0

v1 whole, which is shorter than its diff:
```python
import math

import jax
import jax.numpy as jnp
from jax import lax
from jax.sharding import PartitionSpec as P

H = 16
DH = 128
FF = 8192
SEG = 1024

highest = lax.Precision.HIGHEST
epsilon = 1e-06
f32 = jnp.float32
bf16 = jnp.bfloat16
AXIS = "fsdp"


def feature(values):
    return jax.nn.elu(values) + 1.0


def feature_slope(values):
    return jnp.where(values > 0, 1.0, jnp.exp(jnp.minimum(values, 0.0)))


def norm_forward(values, gain):
    factor = lax.rsqrt(jnp.mean(values * values, axis=-1, keepdims=True) + epsilon)
    return (values * factor * gain, factor)


def norm_backward(values, factor, gain, upstream):
    scaled = upstream * gain
    gain_grad = jnp.sum(upstream * values * factor, axis=0)
    value_grad = factor * scaled - values * (factor * factor * factor) * jnp.mean(
        scaled * values, axis=-1, keepdims=True
    )
    return (value_grad, gain_grad)


def dot(left, right, dims):
    return lax.dot_general(left, right, ((dims[0], dims[1]), ((), ())), preferred_element_type=f32)


def rows_dot(left, right):
    return dot(left, right, ((0,), (0,)))


def cols_dot(left, right):
    return dot(left, right, ((1,), (1,)))


class Layout:
    def __init__(self):
        self.count = lax.axis_size(AXIS)
        self.groups = self.count // H
        self.place = lax.axis_index(AXIS)
        self.head = self.place % H
        self.group = self.place // H
        self.inside = None
        self.across = None
        if self.groups > 1:
            self.inside = [[g * H + j for j in range(H)] for g in range(self.groups)]
            self.across = [[g * H + j for g in range(self.groups)] for j in range(H)]

    def gather(self, block):
        return lax.all_gather(block, AXIS, axis=0, tiled=True, axis_index_groups=self.inside)

    def gather_all(self, block):
        return lax.all_gather(block, AXIS, axis=0, tiled=True)

    def scatter_sum(self, whole):
        return lax.psum_scatter(
            whole, AXIS, scatter_dimension=0, tiled=True, axis_index_groups=self.inside
        )

    def columns(self, block, parts):
        rows, width = block.shape
        each = width // (parts * H)
        if self.groups == 1:
            split = block.reshape(rows, parts, H, each)
            out = lax.all_to_all(split, AXIS, 2, 0, tiled=True)
            return out.reshape(rows * self.count, parts * each)
        whole = self.gather_all(block).reshape(rows * self.count, parts, H, each)
        out = lax.dynamic_index_in_dim(whole, self.head, 2, False)
        return out.reshape(rows * self.count, parts * each)

    def own_rows(self, grad, parts):
        rows, width = grad.shape
        each = width // parts
        if self.groups == 1:
            split = grad.astype(bf16).reshape(rows, parts, 1, each)
            out = lax.all_to_all(split, AXIS, 0, 2, tiled=True)
            return out.reshape(rows // self.count, parts * H * each)
        whole = jnp.zeros((rows, parts, H, each), f32)
        whole = lax.dynamic_update_slice_in_dim(
            whole, grad.reshape(rows, parts, 1, each), self.head, 2
        )
        return lax.psum_scatter(
            whole.reshape(rows, parts * H * each), AXIS, scatter_dimension=0, tiled=True
        )

    def to_tokens(self, by_head):
        tokens, each = by_head.shape
        out = lax.all_to_all(
            by_head.reshape(H, tokens // H, each), AXIS, 0, 0, tiled=False,
            axis_index_groups=self.inside,
        )
        return out.transpose(1, 0, 2).reshape(tokens // H, H * each)

    def to_heads(self, by_token):
        tokens, width = by_token.shape
        split = by_token.reshape(tokens, H, width // H).transpose(1, 0, 2)
        out = lax.all_to_all(
            split, AXIS, 0, 0, tiled=False, axis_index_groups=self.inside
        )
        return out.reshape(H * tokens, width // H)


def carry_forward(layout, delta, count, fresh):
    segments = delta.shape[0]

    def walk(state):
        before = []
        for s in range(segments):
            state = jax.tree.map(lambda a: jnp.where(fresh[s], jnp.zeros_like(a), a), state)
            before.append(state)
            state = (state[0] + delta[s], state[1] + count[s])
        return before, state

    state = (jnp.zeros_like(delta[0]), jnp.zeros_like(count[0]))
    if layout.groups > 1:
        _, last = walk(state)
        renewed = jnp.any(fresh).astype(f32)
        every = jax.tree.map(
            lambda a: lax.all_gather(a, AXIS, axis_index_groups=layout.across), last + (renewed,)
        )
        for g in range(layout.groups - 1):
            keep = every[2][g] < 0.5
            after = jax.tree.map(lambda a, e: jnp.where(keep, a, 0.0) + e[g], state, every[:2])
            state = jax.tree.map(lambda a, b: jnp.where(g < layout.group, b, a), state, after)
    before, _ = walk(state)
    return jnp.stack([b[0] for b in before]), jnp.stack([b[1] for b in before])


def carry_backward(layout, state_grad, norm_grad, fresh):
    segments = state_grad.shape[0]

    def walk(state):
        after = [None] * segments
        for s in reversed(range(segments)):
            after[s] = state
            state = (state[0] + state_grad[s], state[1] + norm_grad[s])
            state = jax.tree.map(lambda a: jnp.where(fresh[s], jnp.zeros_like(a), a), state)
        return after, state

    state = (jnp.zeros_like(state_grad[0]), jnp.zeros_like(norm_grad[0]))
    if layout.groups > 1:
        _, first = walk(state)
        renewed = jnp.any(fresh).astype(f32)
        every = jax.tree.map(
            lambda a: lax.all_gather(a, AXIS, axis_index_groups=layout.across), first + (renewed,)
        )
        for g in reversed(range(1, layout.groups)):
            keep = every[2][g] < 0.5
            before = jax.tree.map(lambda a, e: jnp.where(keep, a, 0.0) + e[g], state, every[:2])
            state = jax.tree.map(lambda a, b: jnp.where(g > layout.group, b, a), state, before)
    after, _ = walk(state)
    return jnp.stack([a[0] for a in after]), jnp.stack([a[1] for a in after])


def body(
    layer_input,
    first_gain,
    in_weight,
    out_weight,
    mix_gate,
    second_gain,
    gate_up,
    down_weight,
    document_starts,
    cotangent,
):
    layout = Layout()
    tokens, width = layer_input.shape
    group_tokens = tokens * H
    segments = group_tokens // SEG
    scale = 1.0 / math.sqrt(DH)

    gains = jnp.stack([first_gain, second_gain])
    gains = lax.all_gather(gains, AXIS, axis=1, tiled=True).astype(f32)
    first_all, second_all = gains[0], gains[1]
    if layout.groups == 1:
        mix_own = mix_gate
    else:
        mix_own = lax.dynamic_slice_in_dim(layout.gather_all(mix_gate), layout.head * DH, DH)
    mix = jax.nn.sigmoid(mix_own.astype(f32))[None]

    inputs = layer_input.astype(f32)
    normed, first_factor = norm_forward(inputs, first_all)
    normed_all = layout.gather(normed.astype(bf16))
    in_cols = layout.columns(in_weight, 3)
    out_all = layout.gather_all(out_weight)
    cot_all = layout.gather(cotangent)
    gate_up_cols = layout.columns(gate_up, 2)
    down_cols = layout.columns(down_weight, 1)

    projected = jnp.dot(normed_all, in_cols, preferred_element_type=f32).astype(bf16)
    by_segment = projected.reshape(segments, SEG, 3, DH)
    query, key, value = by_segment[:, :, 0], by_segment[:, :, 1], by_segment[:, :, 2]
    index = jnp.arange(SEG, dtype=jnp.int32)
    allowed = index[None, :] <= index[:, None]

    def attention_scores():
        raw = jnp.einsum("sqc,skc->sqk", query, key, preferred_element_type=f32) * scale
        return jnp.where(allowed[None], raw, -1e30)

    scores = attention_scores()
    top = jnp.max(scores, axis=-1, keepdims=True)
    expo = jnp.exp(scores - top)
    total = jnp.sum(expo, axis=-1, keepdims=True)
    log_total = top + jnp.log(total)
    probs_low = (expo / total).astype(bf16)
    local_out = jnp.einsum("sqk,skc->sqc", probs_low, value, preferred_element_type=f32)

    query_f, key_f, value_f = query.astype(f32), key.astype(f32), value.astype(f32)
    query_feature = feature(query_f).astype(bf16)
    key_feature = feature(key_f).astype(bf16)
    delta = jnp.einsum("slc,sla->sca", key_feature, value, preferred_element_type=f32)
    count = jnp.sum(key_feature.astype(f32), axis=1)
    numbers = layout.group * segments + jnp.arange(segments)
    fresh = (numbers == 0) | (
        lax.dynamic_slice_in_dim(document_starts[0], layout.group * segments, segments) > 0
    )
    memory, normal = carry_forward(layout, delta, count, fresh)
    query_feature_f = query_feature.astype(f32)
    numerator = jnp.einsum("sie,sej->sij", query_feature_f, memory, precision=highest)
    raw_denom = jnp.einsum("sik,sk->si", query_feature_f, normal, precision=highest)[..., None]
    denom = jnp.maximum(raw_denom, 1.0)
    memory_out = numerator / denom
    combined = mix * memory_out + (1.0 - mix) * local_out
    combined_head = combined.reshape(group_tokens, DH).astype(bf16)
    combined_low = layout.to_tokens(combined_head)
    attended = jnp.dot(combined_low, out_all, preferred_element_type=f32)
    middle = inputs + attended

    hidden, second_factor = norm_forward(middle, second_all)
    hidden_all = layout.gather(hidden.astype(bf16))
    act_grad = jnp.dot(cot_all, down_cols, preferred_element_type=f32)
    both = jnp.dot(hidden_all, gate_up_cols, preferred_element_type=f32)
    half = both.shape[1] // 2
    gate_part, up_part = both[:, :half], both[:, half:]
    sigma = jax.nn.sigmoid(gate_part)
    silu = gate_part * sigma
    activated = (silu * up_part).astype(bf16)
    silu_slope = sigma * (1.0 + gate_part * (1.0 - sigma))
    feed_grad = jnp.concatenate(
        [act_grad * up_part * silu_slope, act_grad * silu], axis=1
    ).astype(bf16)
    feed_out = layout.scatter_sum(cols_dot(activated, down_cols).astype(bf16))
    hidden_grad = layout.scatter_sum(cols_dot(feed_grad, gate_up_cols).astype(bf16))
    layer_output = (middle + feed_out.astype(f32)).astype(bf16)
    gate_up_part = layout.own_rows(rows_dot(hidden_all, feed_grad), 2)
    down_part = layout.own_rows(rows_dot(cot_all, activated), 1)

    upstream = cotangent.astype(f32)
    middle_norm_grad, second_local = norm_backward(
        middle, second_factor, second_all, hidden_grad.astype(f32)
    )
    middle_grad = upstream + middle_norm_grad
    attended_grad = middle_grad.astype(bf16)
    attended_grad_all = layout.gather(attended_grad)
    combined_grad = layout.to_heads(cols_dot(attended_grad, out_all).astype(bf16))
    combined_grad = combined_grad.astype(f32).reshape(segments, SEG, DH)
    out_rows_grad = rows_dot(combined_head, attended_grad_all)
    if layout.groups == 1:
        out_part = out_rows_grad
    else:
        whole = jnp.zeros((H * DH, width), f32)
        whole = lax.dynamic_update_slice_in_dim(whole, out_rows_grad, layout.head * DH, 0)
        out_part = lax.psum_scatter(whole, AXIS, scatter_dimension=0, tiled=True)
    mix_local = jnp.sum(combined_grad * (memory_out - local_out), axis=(0, 1)) * (
        mix * (1.0 - mix)
    ).reshape(DH)

    memory_grad = combined_grad * mix
    local_grad = (combined_grad * (1.0 - mix)).astype(bf16)
    numer_grad = memory_grad / denom
    denom_grad = -jnp.sum(memory_grad * memory_out, axis=-1, keepdims=True) / denom
    raw_grad = jnp.where(raw_denom > 1.0, denom_grad, 0.0)
    query_feature_grad = (
        jnp.einsum("sij,sej->sie", numer_grad, memory, precision=highest)
        + raw_grad * normal[:, None]
    )
    state_grad = jnp.einsum("sie,sij->sej", query_feature_f, numer_grad, precision=highest)
    norm_grad = jnp.sum(raw_grad * query_feature_f, axis=1)
    delta_grad, count_grad = carry_backward(layout, state_grad, norm_grad, fresh)
    key_feature_grad = (
        jnp.einsum("sij,sej->sie", value_f, delta_grad, precision=highest) + count_grad[:, None]
    )
    value_memory_grad = jnp.einsum(
        "sie,sej->sij", key_feature.astype(f32), delta_grad, precision=highest
    )
    query_memory_grad = query_feature_grad * feature_slope(query_f)
    key_memory_grad = key_feature_grad * feature_slope(key_f)

    probs = jnp.exp(attention_scores() - log_total)
    prob_grad = jnp.einsum("sqc,skc->sqk", local_grad, value, preferred_element_type=f32)
    row_term = jnp.sum(probs * prob_grad, axis=-1, keepdims=True)
    score_grad = (probs * (prob_grad - row_term)).astype(bf16)
    query_grad = query_memory_grad + scale * jnp.einsum(
        "sqk,skc->sqc", score_grad, key, preferred_element_type=f32
    )
    key_grad = key_memory_grad + scale * jnp.einsum(
        "sqk,sqc->skc", score_grad, query, preferred_element_type=f32
    )
    value_grad = value_memory_grad + jnp.einsum(
        "sqk,sqc->skc", probs.astype(bf16), local_grad, preferred_element_type=f32
    )
    projected_grad = (
        jnp.stack([query_grad, key_grad, value_grad], axis=2)
        .reshape(group_tokens, 3 * DH)
        .astype(bf16)
    )
    normed_grad = layout.scatter_sum(cols_dot(projected_grad, in_cols).astype(bf16))
    in_part = layout.own_rows(rows_dot(normed_all, projected_grad), 3)
    input_norm_grad, first_local = norm_backward(
        inputs, first_factor, first_all, normed_grad.astype(f32)
    )
    input_grad = middle_grad + input_norm_grad

    gains_part = lax.psum_scatter(
        jnp.stack([first_local, second_local]), AXIS, scatter_dimension=1, tiled=True
    )
    if layout.groups == 1:
        mix_part = mix_local
    else:
        whole = jnp.zeros((H * DH,), f32)
        whole = lax.dynamic_update_slice_in_dim(whole, mix_local, layout.head * DH, 0)
        mix_part = lax.psum_scatter(whole, AXIS, scatter_dimension=0, tiled=True)

    def over_sequences(part):
        return lax.psum(part.astype(bf16), "dp").astype(f32)

    small = over_sequences(jnp.concatenate([gains_part, mix_part[None]]))
    return (
        layer_output,
        input_grad,
        small[0],
        over_sequences(in_part),
        over_sequences(out_part),
        small[2],
        small[1],
        over_sequences(gate_up_part),
        over_sequences(down_part),
    )


def solution(mesh):
    return jax.shard_map(
        body,
        mesh=mesh,
        in_specs=(
            P(("dp", "fsdp"), None),
            P("fsdp"),
            P("fsdp", None),
            P("fsdp", None),
            P("fsdp"),
            P("fsdp"),
            P("fsdp", None),
            P("fsdp", None),
            P("dp", None),
            P(("dp", "fsdp"), None),
        ),
        out_specs=(
            P(("dp", "fsdp"), None),
            P(("dp", "fsdp"), None),
            P("fsdp"),
            P("fsdp", None),
            P("fsdp", None),
            P("fsdp"),
            P("fsdp"),
            P("fsdp", None),
            P("fsdp", None),
        ),
        check_vma=False,
    )
```

time: 4040 us -> 1380 us (0.34)
  waiting for transfers between devices: 2660 us -> 935 us
  blocking collectives: 604 us -> 27.9 us
  other arithmetic: 217 us -> 33.6 us
  matrix products: 302 us -> 138 us
    unnamed x12 -> x11, waiting for transfers between devices: 1770 us -> 60.6 us
    all_gather x6 -> x1, blocking collectives: 460 us -> 23 us  [body(): gains = lax.all_gather(gains, AXIS, axis=1, tiled=True).astype(f32)]
    all_to_all x0 -> x8, waiting for transfers between devices: none -> 354 us  [the longest x3 189 us: columns(): out = lax.all_to_all(split, AXIS, 2, 0, tiled=True)]
    all_gather x7 -> x5, waiting for transfers between devices: 450 us -> 121 us  [the longest x4 69.7 us: gather(): lax.all_gather(block, AXIS, axis=0, tiled=True, axis_index_groups=self.in...]
    dot_general x26 -> x23, matrix products: 302 us -> 135 us  [the longest x8 74.7 us: dot(): lax.dot_general(left, right, ((dims[0], dims[1]), ((), ())), preferred_el...]
    unnamed x2 -> x0, blocking collectives: 139 us -> none
    concatenate x1, other arithmetic: 134 us -> 0.02 us  [body(): small = over_sequences(jnp.concatenate([gains_part, mix_part[None]]))]
    ppermute x14 -> x0, waiting for transfers between devices: 111 us -> none  [from_behind(): return lax.ppermute(block, axis, route)]
  transfers between devices with their start and end apart: 25 -> 18, of which waited for: 9 -> 14; matrix products, arithmetic and copies ran while one was open for 13% -> 14% of each run, Pallas kernels for 0% -> 0%
where the time goes in v1:
time: 1380 us; the launch traced here: 1370 us
  waiting for transfers between devices  935 us (68%)
  matrix products  138 us (10%)
  local copies, waits for them, and re-layouts  114 us (8%)
  starting transfers between devices  110 us (8%)
  other arithmetic  33.6 us (2%)
  blocking collectives  27.9 us (2%)
  between operations  15.3 us (1%)
    reduce_scatter x3, waiting for transfers between devices, scatter_sum(): lax.psum_scatter(whole, AXIS, scatter_dimension=0, tiled=True, axis_index...  204 us
    psum x1, waiting for transfers between devices, over_sequences(): return lax.psum(part.astype(bf16), 'dp').astype(f32)  196 us
    all_to_all x3, waiting for transfers between devices, columns(): out = lax.all_to_all(split, AXIS, 2, 0, tiled=True)  189 us
    all_to_all x3, waiting for transfers between devices, own_rows(): out = lax.all_to_all(split, AXIS, 0, 2, tiled=True)  151 us
    dot_general x8, matrix products, dot(): lax.dot_general(left, right, ((dims[0], dims[1]), ((), ())), preferred_el...  74.7 us
    all_gather x4, waiting for transfers between devices, gather(): lax.all_gather(block, AXIS, axis=0, tiled=True, axis_index_groups=self.in...  69.7 us
    all_to_all x3, starting transfers between devices, own_rows(): out = lax.all_to_all(split, AXIS, 0, 2, tiled=True)  61.9 us
    unnamed x11, waiting for transfers between devices  60.6 us
  transfers between devices with their start and end apart: 18, of which 14 were waited for; matrix products, arithmetic and copies ran while one was open for 14% of the time, Pallas kernels for 0%

profile of v1, /device:TPU:0, one launch (start us, length us, event | category | flops | bytes accessed | tf_op | source)
XLA Modules:
  0.0 1373.8 jit_solution(16027786437920457909)
XLA Ops:
  7.9 23.0 %all_gather.18 = bf16[2,2048]{1,0:T(2,128)(2,1)S(1)} all-gather(bf16[2,128]{1,0:T(2,128)(2,1)S(1)} %pad_maximum_fusion.5), channel_id=1, replica_groups=mesh['dp'=2,'fsdp'=16] {'fsdp'}, dimensions={1}, use_global_device_ids=true | all-gather | bytes 8704 | tf_op jit(solution)/shard_map/all_gather | solution.py:192
  44.3 45.0 %all-to-all-done = bf16[128,3,16,128]{0,3,1,2:T(8,128)(2,1)S(1)} async-done(((bf16[128,3,16,128]{0,3,1,2:T(8,128)(2,1)}), bf16[128,3,16,128]{0,3,1,2:T(8,128)(2,1)S(1)}, u32[]{:S(2)}, u32[]{:S(2)}) %all-to-all-start) | async-done | bytes 1572896 | tf_op jit(solution)/shard_map/all_to_all | solution.py:83
  91.5 40.8 %all-gather.6.cloned.1.call-done = bf16[2048,2048]{1,0:T(8,128)(2,1)} async-done(((bf16[128,2048]{1,0:T(8,128)(2,1)}), bf16[2048,2048]{1,0:T(8,128)(2,1)}) %all-gather.6.cloned.1.call-update) | async-done | bytes 8388624 | tf_op jit(solution)/shard_map/all_gather | solution.py:68
  132.3 9.5 convolution_convert_fusion.6
  141.8 4.0 reshape.187
  165.9 50.9 %all-gather.8.cloned.1.call-done = bf16[2048,2048]{1,0:T(8,128)(2,1)} async-done(((bf16[128,2048]{1,0:T(8,128)(2,1)}), bf16[2048,2048]{1,0:T(8,128)(2,1)}) %all-gather.8.cloned.1.call-update) | async-done | bytes 8388624 | tf_op jit(solution)/shard_map/all_gather | solution.py:71
  216.8 4.7 multiply_reduce_fusion.2
  223.2 4.1 copy.124
  227.2 3.8 all-to-all-start.3
  231.1 6.4 copy.121
  237.4 4.6 copy.122
  242.1 46.3 %all-to-all-done.3 = bf16[128,1,16,512]{0,3,1,2:T(8,128)(2,1)S(1)} async-done(((bf16[128,1,16,512]{0,3,1,2:T(8,128)(2,1)}), bf16[128,1,16,512]{0,3,1,2:T(8,128)(2,1)S(1)}, u32[]{:S(2)}, u32[]{:S(2)}) %all-to-all-start.3) | async-done | bytes 2097184 | tf_op jit(solution)/shard_map/all_to_all | solution.py:83
  288.4 31.7 %all-to-all-start.2 = ((bf16[128,2,16,512]{0,3,1,2:T(8,128)(2,1)}), bf16[128,2,16,512]{0,3,1,2:T(8,128)(2,1)}, u32[]{:S(2)}, u32[]{:S(2)}) async-start(bf16[128,2,16,512]{0,3,1,2:T(8,128)(2,1)} %copy.122), calls=%async_computation.2 | async-start | bytes 8388608 | tf_op jit(solution)/shard_map/all_to_all | solution.py:83
  323.0 97.6 %all-to-all-done.2 = bf16[128,2,16,512]{0,3,1,2:T(8,128)(2,1)} async-done(((bf16[128,2,16,512]{0,3,1,2:T(8,128)(2,1)}), bf16[128,2,16,512]{0,3,1,2:T(8,128)(2,1)}, u32[]{:S(2)}, u32[]{:S(2)}) %all-to-all-start.2) | async-done | bytes 4194336 | tf_op jit(solution)/shard_map/all_to_all | solution.py:83
  420.5 7.9 copy.123
  428.5 14.9 %fusion.5 = f32[2048,1024]{0,1:T(8,128)} fusion(bf16[2048,2048]{1,0:T(8,128)(2,1)} %all-gather.10.cloned.1.call-done, bf16[128,8,16,128]{3,2,1,0:T(8,128)(2,1)} %bitcast.166), kind=kOutput, calls=%fused_computation.13 | convolution fusion | flops 8589934592 | bytes 20971520 | tf_op jit(solution)/shard_map/dot_general | solution.py:251
  443.3 28.9 %all-gather.12.cloned.1.call-done = bf16[2048,2048]{1,0:T(8,128)(2,1)} async-done(((bf16[128,2048]{1,0:T(8,128)(2,1)}), bf16[2048,2048]{1,0:T(8,128)(2,1)}) %all-gather.12.cloned.1.call-update) | async-done | bytes 8388624 | tf_op jit(solution)/shard_map/all_gather | solution.py:68
  472.2 12.2 multiply_convert_fusion.2
  486.5 12.0 convolution_convert_fusion.1
  498.5 119.5 %reduce-scatter.9.cloned.1.call-done = bf16[128,2048]{1,0:T(8,128)(2,1)} async-done(((bf16[2048,2048]{1,0:T(8,128)(2,1)}), bf16[128,2048]{1,0:T(8,128)(2,1)}) %reduce-scatter.9.cloned.1.call-update) | async-done | bytes 524304 | tf_op jit(solution)/shard_map/reduce_scatter | solution.py:74
  620.9 6.5 fusion.31
  628.3 4.5 all-to-all-start.4
  633.3 14.0 %all-to-all-done.4 = bf16[16,128,128]{2,1,0:T(8,128)(2,1)S(1)} async-done(((bf16[16,128,128]{2,1,0:T(8,128)(2,1)}), bf16[16,128,128]{2,1,0:T(8,128)(2,1)S(1)}, u32[]{:S(2)}, u32[]{:S(2)}) %all-to-all-start.4) | async-done | bytes 524320 | tf_op jit(solution)/shard_map/all_to_all | solution.py:115
  648.8 4.8 fusion.2
  672.1 8.2 convolution_convert_fusion
  682.0 9.0 fusion.12
  691.5 4.1 reduce
  698.2 4.7 reshape.188
  702.9 4.0 all-to-all-start.7
  707.1 10.1 convolution_convert_fusion.2
  717.2 13.8 %convolution_convert_fusion.3 = bf16[2048,1024]{0,1:T(8,128)(2,1)} fusion(bf16[2048,2048]{1,0:T(8,128)(2,1)} %all-gather.10.cloned.1.call-done, bf16[2048,512]{0,1:T(8,128)(2,1)} %copy-done.34, bf16[2048,512]{0,1:T(8,128)(2,1)} %copy-done.33), kind=kOutput, calls=%fused_computation.24 | convolution fusion | flops 8600420352 | bytes 16777216 | tf_op jit(solution)/shard_map/dot_general | solution.py:43
  731.0 11.2 copy.133
  742.2 33.6 %all-to-all-done.7 = bf16[16,2,32768]{2,1,0:T(2,128)(2,1)S(1)} async-done(((bf16[16,2,32768]{2,1,0:T(2,128)(2,1)}), bf16[16,2,32768]{2,1,0:T(2,128)(2,1)S(1)}, u32[]{:S(2)}, u32[]{:S(2)}) %all-to-all-start.7) | async-done | bytes 2097184 | tf_op jit(solution)/shard_map/all_to_all | solution.py:94
  775.7 17.1 %all-to-all-start.6 = ((bf16[2048,2,1,512]{3,1,2,0:T(2,128)(2,1)}), bf16[2048,2,1,512]{3,1,2,0:T(2,128)(2,1)}, u32[]{:S(2)}, u32[]{:S(2)}) async-start(bf16[2048,2,1,512]{3,1,2,0:T(2,128)(2,1)} %copy.133), calls=%async_computation.9 | async-start | bytes 8388608 | tf_op jit(solution)/shard_map/all_to_all | solution.py:94
  792.9 8.5 convolution_convert_fusion.5
  801.4 4.2 copy.131
  805.5 97.1 %all-to-all-done.6 = bf16[2048,2,1,512]{3,1,2,0:T(2,128)(2,1)} async-done(((bf16[2048,2,1,512]{3,1,2,0:T(2,128)(2,1)}), bf16[2048,2,1,512]{3,1,2,0:T(2,128)(2,1)}, u32[]{:S(2)}, u32[]{:S(2)}) %all-to-all-start.6) | async-done | bytes 4194336 | tf_op jit(solution)/shard_map/all_to_all | solution.py:94
  902.7 40.8 %all-to-all-start.5 = ((bf16[2048,3,1,128]{3,1,2,0:T(4,128)(2,1)}), bf16[2048,3,1,128]{3,1,2,0:T(4,128)(2,1)}, u32[]{:S(2)}, u32[]{:S(2)}) async-start(bf16[2048,3,1,128]{3,1,2,0:T(4,128)(2,1)} %copy.131), calls=%async_computation.8 | async-start | bytes 4194304 | tf_op jit(solution)/shard_map/all_to_all | solution.py:94
  943.7 6.7 reshape.189
  955.6 8.7 copy.134
  964.3 7.4 reshape.179
  971.7 20.1 %all-to-all-done.5 = bf16[2048,3,1,128]{3,1,2,0:T(4,128)(2,1)} async-done(((bf16[2048,3,1,128]{3,1,2,0:T(4,128)(2,1)}), bf16[2048,3,1,128]{3,1,2,0:T(4,128)(2,1)}, u32[]{:S(2)}, u32[]{:S(2)}) %all-to-all-start.5) | async-done | bytes 1572896 | tf_op jit(solution)/shard_map/all_to_all | solution.py:94
  999.8 6.5 convolution_convert_fusion.7
  1006.4 84.1 %reduce-scatter.7.cloned.1.call-done = bf16[128,2048]{1,0:T(8,128)(2,1)} async-done(((bf16[2048,2048]{1,0:T(8,128)(2,1)}), bf16[128,2048]{1,0:T(8,128)(2,1)}) %reduce-scatter.7.cloned.1.call-update) | async-done | bytes 524304 | tf_op jit(solution)/shard_map/reduce_scatter | solution.py:74
  1093.2 58.6 %reduce-scatter.13.cloned.1.call-done = f32[128,2]{1,0:T(8,128)} async-done(((f32[2048,2]{1,0:T(8,128)}), f32[128,2]{1,0:T(8,128)}) %reduce-scatter.13.cloned.1.call-update) | async-done | bytes 1040
  1152.7 4.9 psum.35
  1158.2 196.1 %all-reduce.7.cloned.1.call-done = (bf16[128,8192]{0,1:T(8,128)(2,1)}, bf16[128,6144]{1,0:T(8,128)(2,1)}, bf16[128,2048]{1,0:T(8,128)(2,1)}, bf16[128,16384]{1,0:T(8,128)(2,1)}) async-done(((bf16[128,8192]{0,1:T(8,128)(2,1)}, bf16[128,6144]{1,0:T(8,128)(2,1)}, bf16[128,2048]{1,0:T(8,128)(2,1)}, bf16[128,16384]{1,0:T(8,128)(2,1)}), (bf16[128,8192]{0,1:T(8,128)(2,1)}, bf16[128,6144]{1,0:T(8,128)(2,1)}, ...) | async-done | bytes 8388624 | tf_op jit(solution)/shard_map/psum | solution.py:344
  1358.9 4.2 convert_element_type.185
  (169 shorter events, 97.2 us)
Async XLA Ops:
  7.2 125.1 %all-gather.6.cloned.1.call-start = ((), (), s32[]{:S(2)}) async-start(), calls=%async_computation.12 | async-start | bytes 8912896 | tf_op jit(solution)/shard_map/all_gather | solution.py:68
  30.9 7.8 copy-start.25
  32.7 6.0 copy-start.27
  34.7 182.1 %all-gather.8.cloned.1.call-start = ((), (), s32[]{:S(2)}) async-start(), calls=%async_computation.13 | async-start | bytes 8912896 | tf_op jit(solution)/shard_map/all_gather | solution.py:71
  35.5 6.9 copy-start.30
  37.4 6.9 copy-start.31
  38.7 50.7 %all-to-all-start = ((bf16[128,3,16,128]{0,3,1,2:T(8,128)(2,1)}), bf16[128,3,16,128]{0,3,1,2:T(8,128)(2,1)S(1)}, u32[]{:S(2)}, u32[]{:S(2)}) async-start(bf16[128,3,16,128]{0,3,1,2:T(8,128)(2,1)} %copy.112), calls=%async_computation | async-start | bytes 3145728 | tf_op jit(solution)/shard_map/all_to_all | solution.py:83
  149.0 3.8 copy-start.14
  149.8 3.0 copy-start.4
  149.9 6.0 copy-start.16
  152.8 3.1 copy-start.20
  154.7 3.4 copy-start
  158.1 58.7 %copy-start.1 = (bf16[128,2048]{1,0:T(8,128)(2,1)S(1)}, bf16[128,2048]{1,0:T(8,128)(2,1)}, u32[]{:S(2)}) copy-start(bf16[128,2048]{1,0:T(8,128)(2,1)} %param.10) | copy-start | bytes 1572868
  161.3 55.6 %copy-start.9 = (bf16[2,1024,128]{2,1,0:T(8,128)(2,1)}, bf16[2,1024,128]{2,1,0:T(8,128)(2,1)S(1)}, u32[]{:S(2)}) copy-start(bf16[2,1024,128]{2,1,0:T(8,128)(2,1)S(1)} %get-tuple-element.51) | copy-start | bytes 1572868
  162.3 54.5 %all-to-all-start.1 = ((bf16[16,128,128]{1,2,0:T(8,128)(2,1)}), bf16[16,128,128]{1,2,0:T(8,128)(2,1)S(1)}, u32[]{:S(2)}, u32[]{:S(2)}) async-start(bf16[16,128,128]{1,2,0:T(8,128)(2,1)} %copy.120), calls=%async_computation.1 | async-start | bytes 1048576 | tf_op jit(solution)/shard_map/all_to_all | solution.py:106
  165.9 262.6 %all-gather.10.cloned.1.call-start = ((), (), s32[]{:S(2)}) async-start(), calls=%async_computation.14 | async-start | bytes 8912896 | tf_op jit(solution)/shard_map/all_gather | solution.py:68
  222.6 249.7 %all-gather.12.cloned.1.call-start = ((), (), s32[]{:S(2)}) async-start(), calls=%async_computation.16 | async-start | bytes 8912896 | tf_op jit(solution)/shard_map/all_gather | solution.py:68
  227.2 61.2 %all-to-all-start.3 = ((bf16[128,1,16,512]{0,3,1,2:T(8,128)(2,1)}), bf16[128,1,16,512]{0,3,1,2:T(8,128)(2,1)S(1)}, u32[]{:S(2)}, u32[]{:S(2)}) async-start(bf16[128,1,16,512]{0,3,1,2:T(8,128)(2,1)} %bitcast.159), calls=%async_computation.3 | async-start | bytes 4194304 | tf_op jit(solution)/shard_map/all_to_all | solution.py:83
  288.4 132.1 %all-to-all-start.2 = ((bf16[128,2,16,512]{0,3,1,2:T(8,128)(2,1)}), bf16[128,2,16,512]{0,3,1,2:T(8,128)(2,1)}, u32[]{:S(2)}, u32[]{:S(2)}) async-start(bf16[128,2,16,512]{0,3,1,2:T(8,128)(2,1)} %copy.122), calls=%async_computation.2 | async-start | bytes 8388608 | tf_op jit(solution)/shard_map/all_to_all | solution.py:83
  320.1 297.9 %reduce-scatter.9.cloned.1.call-start = ((), (), s32[]{:S(2)}) async-start(), calls=%async_computation.17 | async-start | bytes 8912896 | tf_op jit(solution)/shard_map/reduce_scatter | solution.py:74
  428.4 43.8 %copy-start.13 = (bf16[128,1,16,512]{3,0,2,1:T(8,128)(2,1)S(1)}, bf16[128,1,16,512]{3,0,2,1:T(8,128)(2,1)}, u32[]{:S(2)}) copy-start(bf16[128,1,16,512]{3,0,2,1:T(8,128)(2,1)} %copy.126) | copy-start | bytes 6291460
  472.2 14.3 %copy-start.11 = (bf16[16,128,2,1,512]{1,0,4,2,3:T(8,128)(2,1)S(1)}, bf16[16,128,2,1,512]{1,0,4,2,3:T(8,128)(2,1)}, u32[]{:S(2)}) copy-start(bf16[16,128,2,1,512]{1,0,4,2,3:T(8,128)(2,1)} %copy.123) | copy-start | bytes 12582916
  498.5 120.9 %copy-start.6 = (bf16[128,2048]{1,0:T(8,128)(2,1)S(1)}, bf16[128,2048]{1,0:T(8,128)(2,1)}, u32[]{:S(2)}) copy-start(bf16[128,2048]{1,0:T(8,128)(2,1)} %param.19) | copy-start | bytes 1572868
  620.8 6.5 copy-start.3
  620.9 26.4 %copy-start.5 = (bf16[2,1024,128]{2,1,0:T(8,128)(2,1)S(1)}, bf16[2,1024,128]{2,1,0:T(8,128)(2,1)}, u32[]{:S(2)}) copy-start(bf16[2,1024,128]{2,1,0:T(8,128)(2,1)} %copy-done.4) | copy-start | bytes 1572868
  628.3 19.0 %all-to-all-start.4 = ((bf16[16,128,128]{2,1,0:T(8,128)(2,1)}), bf16[16,128,128]{2,1,0:T(8,128)(2,1)S(1)}, u32[]{:S(2)}, u32[]{:S(2)}) async-start(bf16[16,128,128]{2,1,0:T(8,128)(2,1)} %bitcast.173), calls=%async_computation.6 | async-start | bytes 1048576 | tf_op jit(solution)/shard_map/all_to_all | solution.py:115
  632.8 364.1 %reduce-scatter.11.cloned.1.call-start = ((), (), s32[]{:S(2)}) async-start(), calls=%async_computation.18 | async-start | bytes 8912896 | tf_op jit(solution)/shard_map/reduce_scatter | solution.py:74
  647.2 6.4 slice-start
  648.8 4.8 slice-start.1
  648.8 4.8 copy-start.17
  655.8 2.7 copy-start.15
  680.4 319.4 %all-gather.14.cloned.1.call-start = ((), (), s32[]{:S(2)}) async-start(), calls=%async_computation.19 | async-start | bytes 8912896 | tf_op jit(solution)/shard_map/all_gather | solution.py:68
  702.9 72.9 %all-to-all-start.7 = ((bf16[16,2,32768]{2,1,0:T(2,128)(2,1)}), bf16[16,2,32768]{2,1,0:T(2,128)(2,1)S(1)}, u32[]{:S(2)}, u32[]{:S(2)}) async-start(bf16[16,2,32768]{2,1,0:T(2,128)(2,1)} %reshape.188), calls=%async_computation.10 | async-start | bytes 4194304 | tf_op jit(solution)/shard_map/all_to_all | solution.py:94
  706.8 383.6 %reduce-scatter.7.cloned.1.call-start = ((), (), s32[]{:S(2)}) async-start(), calls=%async_computation.15 | async-start | bytes 8912896 | tf_op jit(solution)/shard_map/reduce_scatter | solution.py:74
  775.7 126.9 %all-to-all-start.6 = ((bf16[2048,2,1,512]{3,1,2,0:T(2,128)(2,1)}), bf16[2048,2,1,512]{3,1,2,0:T(2,128)(2,1)}, u32[]{:S(2)}, u32[]{:S(2)}) async-start(bf16[2048,2,1,512]{3,1,2,0:T(2,128)(2,1)} %copy.133), calls=%async_computation.9 | async-start | bytes 8388608 | tf_op jit(solution)/shard_map/all_to_all | solution.py:94
  902.7 89.2 %all-to-all-start.5 = ((bf16[2048,3,1,128]{3,1,2,0:T(4,128)(2,1)}), bf16[2048,3,1,128]{3,1,2,0:T(4,128)(2,1)}, u32[]{:S(2)}, u32[]{:S(2)}) async-start(bf16[2048,3,1,128]{3,1,2,0:T(4,128)(2,1)} %copy.131), calls=%async_computation.8 | async-start | bytes 4194304 | tf_op jit(solution)/shard_map/all_to_all | solution.py:94
  943.4 208.3 %reduce-scatter.13.cloned.1.call-start = ((), (), s32[]{:S(2)}) async-start(), calls=%async_computation.20 | async-start | bytes 1114112
  971.7 25.2 %copy-start.2 = (bf16[128,2048]{1,0:T(8,128)(2,1)S(1)}, bf16[128,2048]{1,0:T(8,128)(2,1)}, u32[]{:S(2)}) copy-start(bf16[128,2048]{1,0:T(8,128)(2,1)} %param.10) | copy-start | bytes 1572868
  971.7 25.2 %copy-start.26 = (f32[1,2048]{1,0:T(1,128)S(1)}, f32[1,2048]{1,0:T(1,128)}, u32[]{:S(2)}) copy-start(f32[1,2048]{1,0:T(1,128)} %copy-done.25) | copy-start | bytes 24580
  971.7 25.2 %copy-start.28 = (f32[128]{0:T(128)S(1)}, f32[128]{0:T(128)}, u32[]{:S(2)}) copy-start(f32[128]{0:T(128)} %copy-done.27) | copy-start | bytes 1540
  999.7 354.6 %all-reduce.7.cloned.1.call-start = ((), (), s32[]{:S(2)}) async-start(), calls=%async_computation.21 | async-start | bytes 16777216 | tf_op jit(solution)/shard_map/psum | solution.py:344
  1006.3 84.2 %copy-start.7 = (bf16[128,2048]{1,0:T(8,128)(2,1)S(1)}, bf16[128,2048]{1,0:T(8,128)(2,1)}, u32[]{:S(2)}) copy-start(bf16[128,2048]{1,0:T(8,128)(2,1)} %param.19) | copy-start | bytes 1572868
  1006.3 84.2 %copy-start.8 = (bf16[128,2048]{1,0:T(8,128)(2,1)S(1)}, bf16[128,2048]{1,0:T(8,128)(2,1)}, u32[]{:S(2)}) copy-start(bf16[128,2048]{1,0:T(8,128)(2,1)} %reduce-scatter.9.cloned.1.call-done) | copy-start | bytes 1572868
  1006.3 84.2 %copy-start.18 = (bf16[128,2048]{1,0:T(8,128)(2,1)S(1)}, bf16[128,2048]{1,0:T(8,128)(2,1)}, u32[]{:S(2)}) copy-start(bf16[128,2048]{1,0:T(8,128)(2,1)} %reduce-scatter.11.cloned.1.call-done) | copy-start | bytes 1572868
  1006.3 84.2 %copy-start.29 = (f32[128]{0:T(128)S(1)}, f32[128]{0:T(128)}, u32[]{:S(2)}) copy-start(f32[128]{0:T(128)} %get-tuple-element.45) | copy-start | bytes 1540
  1354.3 3.5 copy-start.24
  1354.3 4.6 copy-start.10
  1358.9 4.2 copy-start.12
  (7 other events, 11.7 us)
Sparse Core Ops, SparseCore 0:
  34.8 97.3 all-gather.5
  134.4 82.3 all-gather.7
  222.7 135.6 all-gather.9
  360.4 111.7 all-gather.11
  498.7 119.3 reduce-scatter.8
  680.5 181.5 reduce-scatter.10
  864.3 119.9 all-gather.13
  988.3 102.1 reduce-scatter.6
  1094.7 57.0 reduce-scatter.12
  1155.5 198.6 all-reduce.6

commit v2 on v1

--- a/solution.py
+++ b/solution.py
@@ -1,8 +1,11 @@
+import functools
 import math
 
 import jax
 import jax.numpy as jnp
 from jax import lax
+from jax.experimental import pallas as pl
+from jax.experimental.pallas import tpu as pltpu
 from jax.sharding import PartitionSpec as P
 
 H = 16
@@ -170,7 +173,7 @@
     return jnp.stack([a[0] for a in after]), jnp.stack([a[1] for a in after])
 
 
-def body(
+def body_groups(
     layer_input,
     first_gain,
     in_weight,
@@ -357,9 +360,1063 @@
     )
 
 
+MESH = pl.DeviceIdType.MESH
+LIMIT = 60 * 2**20
+CHUNKS = 4
+QUARTERS = 4
+ROWS = 256
+dma = pltpu.SemaphoreType.DMA
+VM = pltpu.VMEM
+
+
+def vmem():
+    return pl.BlockSpec(memory_space=pltpu.VMEM)
+
+
+def anywhere():
+    return pl.BlockSpec(memory_space=pl.ANY)
+
+
+class Spot:
+    def __init__(self):
+        self.dp = lax.axis_index("dp")
+        self.me = lax.axis_index(AXIS)
+        self.z = self.me // 4
+        self.y = (self.me // 2) % 2
+        self.c = self.me % 2
+
+    def at(self, z, y, c):
+        return z * 4 + y * 2 + c
+
+    def arrival(self, j):
+        if j == 0:
+            return self.z
+        ends = jnp.where(self.z == 0, j, 3 - j)
+        middle = {1: (0, 3), 2: (2, 1), 3: (3, 0)}[j]
+        inner = jnp.where(self.z == 1, middle[0], middle[1])
+        return jnp.where((self.z == 0) | (self.z == 3), ends, inner)
+
+
+def greet(s, plane=True, other=True):
+    ids = []
+    if plane:
+        ids += [{AXIS: (s.me + k) % 16} for k in range(1, 16)]
+    else:
+        ids += [{AXIS: s.at((s.z + k) % 4, s.y, s.c)} for k in (1, 2, 3)]
+        ids += [{AXIS: s.at(s.z, 1 - s.y, s.c)}, {AXIS: s.at(s.z, s.y, 1 - s.c)}]
+    if other:
+        ids += [{"dp": 1 - s.dp}]
+    barrier = pltpu.get_barrier_semaphore()
+    for d in ids:
+        pl.semaphore_signal(barrier, inc=1, device_id=d, device_id_type=MESH)
+    pl.semaphore_wait(barrier, len(ids))
+
+
+def send(src, dst, ssem, rsem, to):
+    return pltpu.make_async_remote_copy(
+        src_ref=src, dst_ref=dst, send_sem=ssem, recv_sem=rsem,
+        device_id={AXIS: to}, device_id_type=MESH,
+    )
+
+
+def send_over(src, dst, ssem, rsem, s):
+    return pltpu.make_async_remote_copy(
+        src_ref=src, dst_ref=dst, send_sem=ssem, recv_sem=rsem,
+        device_id={"dp": 1 - s.dp}, device_id_type=MESH,
+    )
+
+
+def merged(*lists):
+    keyed = []
+    for n, tasks in enumerate(lists):
+        keyed += [((i + 0.5) / len(tasks), n, i, t) for i, t in enumerate(tasks)]
+    for _, _, _, t in sorted(keyed, key=lambda e: e[:3]):
+        t()
+
+
+class Gather:
+    @staticmethod
+    def sems():
+        return [dma((CHUNKS, 4))] * 5 + [dma((CHUNKS, 8))] * 2
+
+    def __init__(self, s, src, dst, sems):
+        self.s, self.src, self.dst = s, src, dst
+        self.zr, self.zu, self.zd, self.ys, self.yr, self.ss, self.sr = sems
+        self.rows = 128 // CHUNKS
+
+    def block(self, ch, z, y, c):
+        start = pl.multiple_of(self.s.at(z, y, c) * 128 + ch * self.rows, self.rows)
+        return self.dst.at[pl.ds(start, self.rows)]
+
+    def own(self, ch):
+        return self.src.at[pl.ds(ch * self.rows, self.rows)]
+
+    def zcopy(self, ch, zo, up, own=False):
+        s = self.s
+        dst = self.block(ch, zo, s.y, s.c)
+        to = s.at(s.z + 1 if up else s.z - 1, s.y, s.c)
+        return send(
+            self.own(ch) if own else dst, dst,
+            (self.zu if up else self.zd).at[ch, zo], self.zr.at[ch, zo], to,
+        )
+
+    def ycopy(self, ch, zo, own=False):
+        s = self.s
+        dst = self.block(ch, zo, s.y, s.c)
+        src = self.own(ch) if own else dst
+        return send(src, dst, self.ys.at[ch, zo], self.yr.at[ch, zo], s.at(s.z, 1 - s.y, s.c))
+
+    def scopy(self, ch, zo, yo, own=False):
+        s = self.s
+        dst = self.block(ch, zo, yo, s.c)
+        n = zo * 2 + yo
+        src = self.own(ch) if own else dst
+        return send(src, dst, self.ss.at[ch, n], self.sr.at[ch, n], s.at(s.z, s.y, 1 - s.c))
+
+    def start(self):
+        s = self.s
+        for ch in range(CHUNKS):
+            pl.when(s.z < 3)(lambda: self.zcopy(ch, s.z, True, True).start())
+            pl.when(s.z > 0)(lambda: self.zcopy(ch, s.z, False, True).start())
+            self.ycopy(ch, s.z, True).start()
+            self.scopy(ch, s.z, s.y, True).start()
+
+    def z_arrive(self, ch, j):
+        s = self.s
+        zo = s.arrival(j)
+        self.zcopy(ch, zo, True).wait_recv()
+        pl.when((zo < s.z) & (s.z < 3))(lambda: self.zcopy(ch, zo, True).start())
+        pl.when((zo > s.z) & (s.z > 0))(lambda: self.zcopy(ch, zo, False).start())
+        self.ycopy(ch, zo).start()
+        self.scopy(ch, zo, s.y).start()
+
+    def y_arrive(self, ch, j):
+        s = self.s
+        zo = s.arrival(j)
+        b = self.block(ch, zo, 1 - s.y, s.c)
+        send(b, b, self.ys.at[ch, zo], self.yr.at[ch, zo], s.me).wait_recv()
+        self.scopy(ch, zo, 1 - s.y).start()
+
+    def s_arrive(self, j):
+        s = self.s
+        zo = s.arrival(j)
+        for ch in range(CHUNKS):
+            for yo in range(2):
+                n = zo * 2 + yo
+                b = self.block(ch, zo, yo, 1 - s.c)
+                send(b, b, self.ss.at[ch, n], self.sr.at[ch, n], s.me).wait_recv()
+
+    def tasks(self, use=None):
+        out = []
+        for step in range(5):
+            for ch in range(CHUNKS):
+                if 0 < step < 4:
+                    out.append(functools.partial(self.z_arrive, ch, step))
+                if step > 0:
+                    out.append(functools.partial(self.y_arrive, ch, step - 1))
+            if step > 0:
+                out.append(functools.partial(self.s_arrive, step - 1))
+                if use is not None:
+                    out.append(functools.partial(use, step - 1))
+        return out
+
+    def drain(self):
+        s = self.s
+        for ch in range(CHUNKS):
+            for zo in range(4):
+                pl.when((s.z < 3) & (zo <= s.z))(lambda: self.zcopy(ch, zo, True).wait_send())
+                pl.when((s.z > 0) & (zo >= s.z))(lambda: self.zcopy(ch, zo, False).wait_send())
+                self.ycopy(ch, zo).wait_send()
+                for yo in range(2):
+                    self.scopy(ch, zo, yo).wait_send()
+
+
+class Columns:
+    @staticmethod
+    def sems(parts):
+        return [dma((16, parts)), dma((16, parts)), dma((16,)), dma((16,)), dma((parts,))]
+
+    def __init__(self, s, w, dst, parts, sems):
+        self.s, self.w, self.dst, self.parts = s, w, dst, parts
+        self.e = dst.shape[1] // parts
+        self.ps, self.pr, self.xs, self.xr, self.own = sems
+
+    def rows(self, src, half):
+        return pl.ds(pl.multiple_of(src * 128 + half * 64, 64), 64)
+
+    def cols(self, p, h):
+        return pl.ds(pl.multiple_of(p * 16 * self.e + h * self.e, 128), self.e)
+
+    def copy(self, k, p):
+        s = self.s
+        to = (s.me + k) % 16
+        half = pl.ds(pl.multiple_of(s.dp * 64, 64), 64)
+        return send(
+            self.w.at[half, self.cols(p, to)],
+            self.dst.at[self.rows(s.me, s.dp), pl.ds(p * self.e, self.e)],
+            self.ps.at[k, p], self.pr.at[s.me, p], to,
+        )
+
+    def local(self, p):
+        s = self.s
+        return pltpu.make_async_copy(
+            self.w.at[:, self.cols(p, s.me)],
+            self.dst.at[pl.ds(pl.multiple_of(s.me * 128, 128), 128), pl.ds(p * self.e, self.e)],
+            self.own.at[p],
+        )
+
+    def start(self):
+        for k in range(1, 16):
+            for p in range(self.parts):
+                self.copy(k, p).start()
+        for p in range(self.parts):
+            self.local(p).start()
+
+    def over(self, src):
+        s = self.s
+        b = self.dst.at[self.rows(src, s.dp)]
+        return send_over(b, b, self.xs.at[src], self.xr.at[src], s)
+
+    def arrive(self, k):
+        s = self.s
+        src = (s.me + 16 - k) % 16
+        for p in range(self.parts):
+            b = self.dst.at[self.rows(src, s.dp), pl.ds(p * self.e, self.e)]
+            send(b, b, self.ps.at[k, p], self.pr.at[src, p], s.me).wait_recv()
+        self.over(src).start()
+
+    def tasks(self):
+        return [functools.partial(self.arrive, k) for k in range(1, 16)]
+
+    def finish(self):
+        s = self.s
+        for k in range(1, 16):
+            src = (s.me + 16 - k) % 16
+            b = self.dst.at[self.rows(src, 1 - s.dp)]
+            send_over(b, b, self.xs.at[src], self.xr.at[src], s).wait_recv()
+        for p in range(self.parts):
+            self.local(p).wait()
+
+    def drain(self):
+        s = self.s
+        for k in range(1, 16):
+            for p in range(self.parts):
+                self.copy(k, p).wait_send()
+            self.over((s.me + 16 - k) % 16).wait_send()
+
+
+class Return:
+    @staticmethod
+    def sems(parts):
+        return [dma((16, parts))] * 4 + [dma((parts,))]
+
+    def __init__(self, s, src, dst, parts, sems, other=None):
+        self.s, self.src, self.dst, self.parts, self.other = s, src, dst, parts, other
+        self.e = src.shape[2] // parts
+        self.ps, self.pr, self.xs, self.xr, self.own = sems
+
+    def place(self, ref, p, h):
+        return ref.at[:, pl.ds(pl.multiple_of(p * 16 * self.e + h * self.e, 128), self.e)]
+
+    def copy(self, k, p):
+        s = self.s
+        to = (s.me + k) % 16
+        return send(
+            self.src.at[to, :, pl.ds(p * self.e, self.e)], self.place(self.dst, p, s.me),
+            self.ps.at[k, p], self.pr.at[s.me, p], to,
+        )
+
+    def local(self, p):
+        s = self.s
+        return pltpu.make_async_copy(
+            self.src.at[s.me, :, pl.ds(p * self.e, self.e)], self.place(self.dst, p, s.me),
+            self.own.at[p],
+        )
+
+    def start(self):
+        for p in range(self.parts):
+            self.local(p).start()
+        for k in range(1, 16):
+            for p in range(self.parts):
+                self.copy(k, p).start()
+        if self.other is not None:
+            for p in range(self.parts):
+                self.over(self.s.me, p, own=True).start()
+
+    def over(self, h, p, own=False):
+        s = self.s
+        src = self.src.at[s.me, :, pl.ds(p * self.e, self.e)] if own else self.place(self.dst, p, h)
+        return send_over(src, self.place(self.other, p, h), self.xs.at[h, p], self.xr.at[h, p], s)
+
+    def arrive(self, k):
+        s = self.s
+        h = (s.me + 16 - k) % 16
+        for p in range(self.parts):
+            b = self.place(self.dst, p, h)
+            send(b, b, self.ps.at[k, p], self.pr.at[h, p], s.me).wait_recv()
+            if self.other is not None:
+                self.over(h, p).start()
+
+    def tasks(self):
+        return [functools.partial(self.arrive, k) for k in range(1, 16)]
+
+    def finish(self):
+        s = self.s
+        for p in range(self.parts):
+            self.local(p).wait()
+        if self.other is not None:
+            for k in range(16):
+                h = (s.me + 16 - k) % 16
+                for p in range(self.parts):
+                    b = self.place(self.other, p, h)
+                    send_over(b, b, self.xs.at[h, p], self.xr.at[h, p], s).wait_recv()
+        for k in range(1, 16):
+            for p in range(self.parts):
+                self.copy(k, p).wait_send()
+        if self.other is not None:
+            for k in range(16):
+                for p in range(self.parts):
+                    self.over((s.me + 16 - k) % 16, p).wait_send()
+
+
+class Scatter:
+    @staticmethod
+    def scratch(width):
+        q = QUARTERS
+        return [
+            VM((4, 2, 256, width), bf16), VM((4, 2, 128, width), bf16), VM((4, 2, 128, width), bf16),
+            VM((4, 128, width), bf16), VM((3, 128, width), bf16),
+            dma((4, q, 2)), dma((4, q, 2)), dma((4, q)), dma((4, q)), dma((3, q)), dma((3, q)),
+        ]
+
+    def __init__(self, s, left, right, out, scratch):
+        self.s, self.left, self.right, self.out = s, left, right, out
+        self.part, self.sib, self.mid, self.got_y, self.got_z = scratch[:5]
+        self.ss, self.sr, self.ys, self.yr, self.zs, self.zr = scratch[5:]
+        self.cols = right.shape[0] // QUARTERS
+        self.order = [(s.z + 2) % 4, 3 - s.z, s.z + 1 - 2 * (s.z % 2), s.z]
+
+    def w(self, h):
+        return pl.ds(h * self.cols, self.cols)
+
+    def compute(self, k, h, yd, slot):
+        tok = pl.multiple_of((self.order[k] * 2 + yd) * 256, 256)
+        p = cols_dot(self.left[pl.ds(tok, 256), :], self.right[self.w(h), :])
+        self.part[k, slot, :, self.w(h)] = p.astype(bf16)
+
+    def sib_copy(self, k, h, slot):
+        s = self.s
+        src = self.part.at[k, slot, pl.ds(pl.multiple_of((1 - s.c) * 128, 128), 128), self.w(h)]
+        return send(
+            src, self.sib.at[k, slot, :, self.w(h)],
+            self.ss.at[k, h, slot], self.sr.at[k, h, slot], s.at(s.z, s.y, 1 - s.c),
+        )
+
+    def y_copy(self, k, h):
+        s = self.s
+        return send(
+            self.mid.at[k, 0, :, self.w(h)], self.got_y.at[k, :, self.w(h)],
+            self.ys.at[k, h], self.yr.at[k, h], s.at(s.z, 1 - s.y, s.c),
+        )
+
+    def z_copy(self, k, h):
+        s = self.s
+        return send(
+            self.mid.at[k, 1, :, self.w(h)], self.got_z.at[k, :, self.w(h)],
+            self.zs.at[k, h], self.zr.at[k, h], s.at(self.order[k], s.y, s.c),
+        )
+
+    def fold(self, k, h, slot):
+        s = self.s
+        self.sib_copy(k, h, slot).wait_recv()
+        own = self.part[k, slot, pl.ds(pl.multiple_of(s.c * 128, 128), 128), self.w(h)]
+        total = own.astype(f32) + self.sib[k, slot, :, self.w(h)].astype(f32)
+        self.mid[k, slot, :, self.w(h)] = total.astype(bf16)
+
+    def after_y(self, k, h):
+        self.y_copy(k, h).wait_recv()
+        w = self.w(h)
+        total = self.mid[k, 1, :, w].astype(f32) + self.got_y[k, :, w].astype(f32)
+        if k < 3:
+            self.mid[k, 1, :, w] = total.astype(bf16)
+            self.z_copy(k, h).start()
+        else:
+            self.out[:, w] = total
+
+    def tasks(self):
+        steps = [(k, h) for k in range(4) for h in range(QUARTERS)]
+        s = self.s
+
+        def step(i):
+            k, h = steps[i]
+            self.compute(k, h, 1 - s.y, 0)
+            self.sib_copy(k, h, 0).start()
+            self.compute(k, h, s.y, 1)
+            self.sib_copy(k, h, 1).start()
+            self.fold(k, h, 0)
+            self.y_copy(k, h).start()
+            self.fold(k, h, 1)
+            if i >= 2:
+                self.after_y(*steps[i - 2])
+
+        out = [functools.partial(step, i) for i in range(len(steps))]
+        out += [functools.partial(self.after_y, *steps[i]) for i in (len(steps) - 2, len(steps) - 1)]
+        return out
+
+    def finish(self):
+        for k in range(3):
+            for h in range(QUARTERS):
+                self.z_copy(k, h).wait_recv()
+                self.out[:, self.w(h)] += self.got_z[k, :, self.w(h)].astype(f32)
+        for k in range(4):
+            for h in range(QUARTERS):
+                self.sib_copy(k, h, 0).wait_send()
+                self.sib_copy(k, h, 1).wait_send()
+                self.y_copy(k, h).wait_send()
+                if k < 3:
+                    self.z_copy(k, h).wait_send()
+
+
+def halves_of(refs, counts):
+    out, at = [], 0
+    for n in counts:
+        out.append(refs[at:at + n])
+        at += n
+    return out
+
+
+def communicate(kernel, name, number, ins, in_specs, outs, out_specs, scratch, flops=0):
+    return pl.pallas_call(
+        kernel, out_shape=outs, in_specs=in_specs, out_specs=out_specs, scratch_shapes=scratch,
+        compiler_params=pltpu.CompilerParams(
+            collective_id=number, has_side_effects=True, vmem_limit_bytes=LIMIT
+        ),
+        cost_estimate=pl.CostEstimate(flops=flops, bytes_accessed=2**24, transcendentals=0),
+        name=name,
+    )(*ins)
+
+
+def project_kernel(x, gains, in_w, normed_all, in_cols, gains_all, projected, normed, *rest):
+    g_s, g_r = rest[:2]
+    gather_sems, col_sems = halves_of(rest[2:], [7, 5])
+    s = Spot()
+    greet(s)
+
+    def gain_copy(k):
+        return send(gains, gains_all.at[s.me], g_s.at[k], g_r.at[s.me], (s.me + k) % 16)
+
+    for k in range(1, 16):
+        gain_copy(k).start()
+    columns = Columns(s, in_w, in_cols, 3, col_sems)
+    columns.start()
+    gains_all[s.me] = gains[...]
+    values = x[...].astype(f32)
+    factor = lax.rsqrt(jnp.mean(values * values, axis=-1, keepdims=True) + epsilon)
+    for k in range(1, 16):
+        src = (s.me + 16 - k) % 16
+        b = gains_all.at[src]
+        send(b, b, g_s.at[k], g_r.at[src], s.me).wait_recv()
+    mine = pl.ds(pl.multiple_of(s.me * 128, 128), 128)
+    for j in range(16):
+        w = pl.ds(j * 128, 128)
+        part = (x[:, w].astype(f32) * factor * gains_all[j, 0:1, :]).astype(bf16)
+        normed[:, w] = part
+        normed_all[mine, w] = part
+    gather = Gather(s, normed, normed_all, gather_sems)
+    gather.start()
+
+    def use(j):
+        if j == 3:
+            columns.finish()
+            for i in range(4):
+                tok = pl.ds(pl.multiple_of(s.arrival(i) * 512, 512), 512)
+                out = jnp.dot(normed_all[tok, :], in_cols[...], preferred_element_type=f32)
+                projected[tok, :] = out.astype(bf16)
+
+    merged(gather.tasks(use), columns.tasks() + [lambda: None] * 6)
+    gather.drain()
+    columns.drain()
+    for k in range(1, 16):
+        gain_copy(k).wait_send()
+
+
+def project(x, gains, in_weight, number):
+    tokens, width = x.shape
+    return communicate(
+        project_kernel, "project", number, (x, gains, in_weight), [vmem(), vmem(), anywhere()],
+        [
+            jax.ShapeDtypeStruct((16 * tokens, width), bf16),
+            jax.ShapeDtypeStruct((width, 3 * DH), bf16),
+            jax.ShapeDtypeStruct((16, 8, 128), f32),
+            jax.ShapeDtypeStruct((16 * tokens, 3 * DH), bf16),
+        ],
+        [vmem()] * 4,
+        [VM((tokens, width), bf16), dma((16,)), dma((16,))] + Gather.sems() + Columns.sems(3),
+    )
+
+
+def kernel_feature(t):
+    return jnp.where(t > 0, t + 1.0, jnp.exp(jnp.minimum(t, 0.0)))
+
+
+def dot_high(left, right, dims=((1,), (0,))):
+    return lax.dot_general(
+        left, right, (dims, ((), ())), preferred_element_type=f32, precision=highest
+    )
+
+
+def scores_of(query, keys, first):
+    raw = cols_dot(query, keys) * (1.0 / math.sqrt(DH))
+    row = lax.broadcasted_iota(jnp.int32, raw.shape, 0) + first
+    col = lax.broadcasted_iota(jnp.int32, raw.shape, 1)
+    return jnp.where(col <= row, raw, -1e30)
+
+
+class Attend:
+    def __init__(self, qkv, keep, mix, local, mem_out, lse, combined, memory, normal):
+        self.qkv, self.keep, self.mix = qkv, keep, mix
+        self.local, self.mem_out, self.lse, self.combined = local, mem_out, lse, combined
+        self.memory, self.normal = memory, normal
+        self.segments = qkv.shape[0] // SEG
+
+    def states(self):
+        state = jnp.zeros((DH, DH), f32)
+        norm = jnp.zeros((1, DH), f32)
+        for n in range(self.segments):
+            keep = self.keep[n, 0:1, :]
+            state, norm = state * keep, norm * keep
+            self.memory[n] = state
+            self.normal[n, 0:1, :] = norm
+            if n + 1 < self.segments:
+                rows = pl.ds(n * SEG, SEG)
+                fk = kernel_feature(self.qkv[rows, DH:2 * DH].astype(f32)).astype(bf16)
+                state = state + rows_dot(fk, self.qkv[rows, 2 * DH:])
+                norm = norm + jnp.sum(fk.astype(f32), axis=0, keepdims=True)
+
+    def block(self, n, i):
+        rows = pl.ds(n * SEG + i * ROWS, ROWS)
+        seen = pl.ds(n * SEG, (i + 1) * ROWS)
+        query = self.qkv[rows, :DH]
+        scores = scores_of(query, self.qkv[seen, DH:2 * DH], i * ROWS)
+        top = jnp.max(scores, axis=-1, keepdims=True)
+        expo = jnp.exp(scores - top)
+        total = jnp.sum(expo, axis=-1, keepdims=True)
+        probs = (expo * (1.0 / total)).astype(bf16)
+        local = jnp.dot(probs, self.qkv[seen, 2 * DH:], preferred_element_type=f32)
+        fq = kernel_feature(query.astype(f32)).astype(bf16).astype(f32)
+        den = jnp.maximum(jnp.sum(fq * self.normal[n, 0:1, :], axis=-1, keepdims=True), 1.0)
+        mem_out = dot_high(fq, self.memory[n]) / den
+        mix = self.mix[0:1, :]
+        self.local[rows, :] = local
+        self.mem_out[rows, :] = mem_out
+        self.lse[rows, :] = jnp.broadcast_to(top + jnp.log(total), (ROWS, DH))
+        self.combined[rows, :] = (mix * mem_out + (1.0 - mix) * local).astype(bf16)
+
+    def blocks(self):
+        return [(n, i) for n in range(self.segments) for i in range(SEG // ROWS)]
+
+
+class AttendBack:
+    def __init__(self, qkv, keep, mix, local, mem_out, lse, memory, normal, upstream, grad,
+                 mix_grad, dk, dv, state_grad, norm_grad):
+        self.qkv, self.keep, self.mix = qkv, keep, mix
+        self.local, self.mem_out, self.lse = local, mem_out, lse
+        self.memory, self.normal, self.upstream, self.grad = memory, normal, upstream, grad
+        self.mix_grad, self.dk, self.dv = mix_grad, dk, dv
+        self.state_grad, self.norm_grad = state_grad, norm_grad
+        self.segments = qkv.shape[0] // SEG
+
+    def clear(self):
+        self.mix_grad[...] = jnp.zeros_like(self.mix_grad)
+        self.dk[...] = jnp.zeros_like(self.dk)
+        self.dv[...] = jnp.zeros_like(self.dv)
+        self.state_grad[...] = jnp.zeros_like(self.state_grad)
+        self.norm_grad[...] = jnp.zeros_like(self.norm_grad)
+
+    def block(self, n, i):
+        scale = 1.0 / math.sqrt(DH)
+        rows = pl.ds(n * SEG + i * ROWS, ROWS)
+        seen = pl.ds(n * SEG, (i + 1) * ROWS)
+        query = self.qkv[rows, :DH]
+        keys = self.qkv[seen, DH:2 * DH]
+        values = self.qkv[seen, 2 * DH:]
+        up = self.upstream[rows, :].astype(f32)
+        mem_out = self.mem_out[rows, :]
+        mix = self.mix[0:1, :]
+        mixed = jnp.sum(up * (mem_out - self.local[rows, :]), axis=0, keepdims=True)
+        self.mix_grad[0:1, :] += mixed * mix * (1.0 - mix)
+        memory_grad = up * mix
+        local_grad = (up * (1.0 - mix)).astype(bf16)
+        query_f = query.astype(f32)
+        fq = kernel_feature(query_f).astype(bf16).astype(f32)
+        normal = self.normal[n, 0:1, :]
+        raw = jnp.sum(fq * normal, axis=-1, keepdims=True)
+        den = jnp.maximum(raw, 1.0)
+        numer_grad = memory_grad / den
+        den_grad = -jnp.sum(memory_grad * mem_out, axis=-1, keepdims=True) / den
+        raw_grad = jnp.where(raw > 1.0, den_grad, 0.0)
+        fq_grad = dot_high(numer_grad, self.memory[n], ((1,), (1,))) + raw_grad * normal
+        if n > 0:
+            self.state_grad[n] += dot_high(fq, numer_grad, ((0,), (0,)))
+            self.norm_grad[n, 0:1, :] += jnp.sum(raw_grad * fq, axis=0, keepdims=True)
+        scores = scores_of(query, keys, i * ROWS)
+        probs = jnp.exp(scores - self.lse[rows, 0:1])
+        prob_grad = cols_dot(local_grad, values)
+        row_term = jnp.sum(probs * prob_grad, axis=-1, keepdims=True)
+        score_grad = (probs * (prob_grad - row_term)).astype(bf16)
+        query_grad = jnp.dot(score_grad, keys, preferred_element_type=f32) * scale
+        query_grad = query_grad + fq_grad * feature_slope(query_f)
+        self.grad[rows, :DH] = query_grad.astype(bf16)
+        self.dk[seen, :] += rows_dot(score_grad, query) * scale
+        self.dv[seen, :] += rows_dot(probs.astype(bf16), local_grad)
+
+    def states(self):
+        state = jnp.zeros((DH, DH), f32)
+        norm = jnp.zeros((1, DH), f32)
+        for n in reversed(range(self.segments)):
+            rows = pl.ds(n * SEG, SEG)
+            key = self.qkv[rows, DH:2 * DH].astype(f32)
+            key_grad = self.dk[rows, :]
+            value_grad = self.dv[rows, :]
+            if n + 1 < self.segments:
+                fk = kernel_feature(key).astype(bf16).astype(f32)
+                value = self.qkv[rows, 2 * DH:].astype(f32)
+                fk_grad = dot_high(value, state, ((1,), (1,))) + norm
+                key_grad = key_grad + fk_grad * feature_slope(key)
+                value_grad = value_grad + dot_high(fk, state)
+            self.grad[rows, DH:2 * DH] = key_grad.astype(bf16)
+            self.grad[rows, 2 * DH:] = value_grad.astype(bf16)
+            if n > 0:
+                keep = self.keep[n, 0:1, :]
+                state = (state + self.state_grad[n]) * keep
+                norm = (norm + self.norm_grad[n, 0:1, :]) * keep
+
+    def blocks(self):
+        return [(n, i) for n in range(self.segments) for i in range(SEG // ROWS)]
+
+
+def attend_kernel(qkv, keep, mix, out_w, cot, gate_up, down,
+                  local, mem_out, lse, combined, memory, normal, mixed_tokens, out_all, cot_all,
+                  gate_up_cols, down_cols, copies, t_s, t_r, *rest):
+    sems_o, sems_c, sems_g, sems_d = halves_of(rest, [7, 7, 5, 5])
+    s = Spot()
+    mine = pl.ds(pl.multiple_of(s.me * 128, 128), 128)
+    own = [
+        pltpu.make_async_copy(out_w, out_all.at[mine], copies.at[0]),
+        pltpu.make_async_copy(cot, cot_all.at[mine], copies.at[1]),
+    ]
+    for cp in own:
+        cp.start()
+    greet(s)
+    gather_o = Gather(s, out_w, out_all, sems_o)
+    gather_c = Gather(s, cot, cot_all, sems_c)
+    columns_g = Columns(s, gate_up, gate_up_cols, 2, sems_g)
+    columns_d = Columns(s, down, down_cols, 1, sems_d)
+    gather_o.start()
+    columns_g.start()
+    attend = Attend(qkv, keep, mix, local, mem_out, lse, combined, memory, normal)
+
+    def token_copy(j):
+        return send(
+            combined.at[pl.ds(j * 128, 128)],
+            mixed_tokens.at[:, pl.ds(pl.multiple_of(s.me * DH, DH), DH)],
+            t_s.at[j], t_r.at[s.me], j,
+        )
+
+    def block(n, i):
+        attend.block(n, i)
+        for j in range((n * SEG + i * ROWS) // 128, (n * SEG + (i + 1) * ROWS) // 128):
+            pl.when(s.me != j)(lambda: token_copy(j).start())
+
+    def late():
+        gather_c.start()
+        columns_d.start()
+
+    compute = [attend.states] + [functools.partial(block, n, i) for n, i in attend.blocks()]
+    merged(
+        gather_o.tasks() + [late] + gather_c.tasks(),
+        compute + [lambda: None] * len(compute),
+        [lambda: None] * 3 + columns_g.tasks() + [lambda: None] * 3 + columns_d.tasks(),
+    )
+    mixed_tokens[:, pl.ds(pl.multiple_of(s.me * DH, DH), DH)] = combined[mine, :]
+    columns_g.finish()
+    columns_d.finish()
+    for k in range(1, 16):
+        src = (s.me + 16 - k) % 16
+        b = mixed_tokens.at[:, pl.ds(pl.multiple_of(src * DH, DH), DH)]
+        send(b, b, t_s.at[0], t_r.at[src], s.me).wait_recv()
+    for j in range(16):
+        pl.when(s.me != j)(lambda: token_copy(j).wait_send())
+    gather_o.drain()
+    gather_c.drain()
+    columns_g.drain()
+    columns_d.drain()
+    for cp in own:
+        cp.wait()
+
+
+def attend_forward(qkv, keep, mix, out_weight, cotangent, gate_up, down, number):
+    tokens, width = cotangent.shape
+    total = qkv.shape[0]
+    segments = total // SEG
+    shape = jax.ShapeDtypeStruct
+    return communicate(
+        attend_kernel, "attend", number, (qkv, keep, mix, out_weight, cotangent, gate_up, down),
+        [vmem()] * 3 + [anywhere()] * 4,
+        [
+            shape((total, DH), f32), shape((total, DH), f32), shape((total, DH), f32),
+            shape((total, DH), bf16), shape((segments, DH, DH), f32), shape((segments, 8, DH), f32),
+            shape((tokens, width), bf16),
+            shape((total, width), bf16), shape((total, width), bf16),
+            shape((width, gate_up.shape[1] // 16), bf16), shape((width, down.shape[1] // 16), bf16),
+        ],
+        [vmem()] * 7 + [anywhere()] * 4,
+        [dma((2,)), dma((16,)), dma((16,))] + Gather.sems() * 2 + Columns.sems(2) + Columns.sems(1),
+    )
+
+
+def feed_kernel(combined, x, gains_all, out_all, cot_all, gate_up_cols, down_cols,
+                middle, hidden_all, act, feed_grad, out_v, cot_v, gate_up_v, down_v, hidden, copies,
+                *sems):
+    s = Spot()
+    loads = [
+        pltpu.make_async_copy(a, b, copies.at[i])
+        for i, (a, b) in enumerate(
+            [(out_all, out_v), (gate_up_cols, gate_up_v), (cot_all, cot_v), (down_cols, down_v)]
+        )
+    ]
+    for cp in loads:
+        cp.start()
+    greet(s, plane=False, other=False)
+    loads[0].wait()
+    width = x.shape[1]
+    squares = jnp.zeros((x.shape[0], 1), f32)
+    for j in range(4):
+        w = pl.ds(j * 512, 512)
+        got = jnp.dot(combined[...], out_v[:, w], preferred_element_type=f32)
+        got = got + x[:, w].astype(f32)
+        middle[:, w] = got
+        squares = squares + jnp.sum(got * got, axis=-1, keepdims=True)
+    factor = lax.rsqrt(squares * (1.0 / width) + epsilon)
+    mine = pl.ds(pl.multiple_of(s.me * 128, 128), 128)
+    for j in range(16):
+        w = pl.ds(j * 128, 128)
+        part = (middle[:, w] * factor * gains_all[j, 1:2, :]).astype(bf16)
+        hidden[:, w] = part
+        hidden_all[mine, w] = part
+    gather = Gather(s, hidden, hidden_all, sems)
+    gather.start()
+    half = act.shape[1]
+
+    def use(j):
+        if j == 0:
+            for cp in loads[1:]:
+                cp.wait()
+        tok = pl.ds(pl.multiple_of(s.arrival(j) * 512, 512), 512)
+        act_grad = jnp.dot(cot_v[tok, :], down_v[...], preferred_element_type=f32)
+        gate = jnp.dot(hidden_all[tok, :], gate_up_v[:, :half], preferred_element_type=f32)
+        up = jnp.dot(hidden_all[tok, :], gate_up_v[:, half:], preferred_element_type=f32)
+        sigma = jax.nn.sigmoid(gate)
+        silu = gate * sigma
+        act[tok, :] = (silu * up).astype(bf16)
+        slope = sigma * (1.0 + gate * (1.0 - sigma))
+        feed_grad[tok, :half] = (act_grad * up * slope).astype(bf16)
+        feed_grad[tok, half:] = (act_grad * silu).astype(bf16)
+
+    merged(gather.tasks(use))
+    gather.drain()
+
+
+def feed(combined, x, gains_all, out_all, cot_all, gate_up_cols, down_cols, number):
+    tokens, width = x.shape
+    total = cot_all.shape[0]
+    half = down_cols.shape[1]
+    shape = jax.ShapeDtypeStruct
+    return communicate(
+        feed_kernel, "feed", number,
+        (combined, x, gains_all, out_all, cot_all, gate_up_cols, down_cols),
+        [vmem()] * 3 + [anywhere()] * 4,
+        [
+            shape((tokens, width), f32), shape((total, width), bf16),
+            shape((total, half), bf16), shape((total, 2 * half), bf16),
+        ],
+        [vmem()] * 4,
+        [
+            VM(out_all.shape, bf16), VM(cot_all.shape, bf16), VM(gate_up_cols.shape, bf16),
+            VM(down_cols.shape, bf16), VM((tokens, width), bf16), dma((4,)),
+        ] + Gather.sems(),
+    )
+
+
+def scatter_kernel(exchanges, left, right, *rest):
+    sent = rest[:exchanges]
+    out = rest[exchanges]
+    got = rest[exchanges + 1:2 * exchanges + 1]
+    x_s, x_r = rest[2 * exchanges + 1:2 * exchanges + 3]
+    s = Spot()
+    greet(s, plane=False)
+    overs = [send_over(a, b, x_s.at[i], x_r.at[i], s) for i, (a, b) in enumerate(zip(sent, got))]
+    scatter = Scatter(s, left, right, out, rest[2 * exchanges + 3:])
+    for cp in overs:
+        cp.start()
+    merged(scatter.tasks())
+    scatter.finish()
+    for cp in overs:
+        cp.wait()
+
+
+def scatter_dot(left, right, sent, name, number):
+    shape = jax.ShapeDtypeStruct
+    width = right.shape[0]
+    n = len(sent)
+    return communicate(
+        functools.partial(scatter_kernel, n), name, number, (left, right, *sent),
+        [vmem()] * 2 + [anywhere()] * n,
+        [shape((left.shape[0] // 16, width), f32)] + [shape(a.shape, a.dtype) for a in sent],
+        [vmem()] + [anywhere()] * n,
+        [dma((max(n, 1),)), dma((max(n, 1),))] + Scatter.scratch(width),
+    )
+
+
+def attend_back_kernel(attended, out_all, qkv, keep, mix, local, mem_out, lse, memory, normal,
+                       gate_up_half, down_half,
+                       attended_all, grad, mix_grad, gate_up_rows, down_rows,
+                       out_v, by_token, upstream, dk, dv, state_grad, norm_grad, copies, h_s, h_r,
+                       *rest):
+    sems_a, sems_g, sems_d = halves_of(rest, [7, 5, 5])
+    s = Spot()
+    mine = pl.ds(pl.multiple_of(s.me * 128, 128), 128)
+    load = pltpu.make_async_copy(out_all, out_v, copies.at[0])
+    load.start()
+    own = pltpu.make_async_copy(attended, attended_all.at[mine], copies.at[1])
+    own.start()
+    greet(s, other=False)
+    gather = Gather(s, attended, attended_all, sems_a)
+    back_g = Return(s, gate_up_half, gate_up_rows, 2, sems_g)
+    back_d = Return(s, down_half, down_rows, 1, sems_d)
+    attend = AttendBack(qkv, keep, mix, local, mem_out, lse, memory, normal, upstream, grad,
+                        mix_grad, dk, dv, state_grad, norm_grad)
+    attend.clear()
+    load.wait()
+
+    def head_copy(j):
+        return send(by_token.at[:, pl.ds(j * DH, DH)], upstream.at[mine], h_s.at[j], h_r.at[s.me], j)
+
+    for j in range(4):
+        w = pl.ds(j * 512, 512)
+        by_token[:, w] = cols_dot(attended[...], out_v[w, :]).astype(bf16)
+        for h in range(4 * j, 4 * j + 4):
+            pl.when(s.me != h)(lambda: head_copy(h).start())
+    upstream[mine, :] = by_token[:, pl.ds(pl.multiple_of(s.me * DH, DH), DH)]
+    gather.start()
+    back_g.start()
+    back_d.start()
+
+    def arrive(j):
+        b = upstream.at[pl.ds(j * 128, 128)]
+        pl.when(s.me != j)(lambda: send(b, b, h_s.at[j], h_r.at[j], s.me).wait_recv())
+
+    def block(n, i):
+        for j in range((n * SEG + i * ROWS) // 128, (n * SEG + (i + 1) * ROWS) // 128):
+            arrive(j)
+        attend.block(n, i)
+
+    compute = [functools.partial(block, n, i) for n, i in attend.blocks()] + [attend.states]
+    merged(
+        gather.tasks(),
+        [lambda: None] * 2 + compute,
+        [lambda: None] * 10 + back_g.tasks() + back_d.tasks(),
+    )
+    back_g.finish()
+    back_d.finish()
+    for j in range(16):
+        pl.when(s.me != j)(lambda: head_copy(j).wait_send())
+    gather.drain()
+    own.wait()
+
+
+def attend_backward(attended, out_all, qkv, keep, mix, saved, gate_up_half, down_half, number):
+    tokens, width = attended.shape
+    total = qkv.shape[0]
+    segments = total // SEG
+    shape = jax.ShapeDtypeStruct
+    local, mem_out, lse, memory, normal = saved
+    return communicate(
+        attend_back_kernel, "attend_back", number,
+        (attended, out_all, qkv, keep, mix, local, mem_out, lse, memory, normal,
+         gate_up_half, down_half),
+        [vmem(), anywhere()] + [vmem()] * 8 + [anywhere()] * 2,
+        [
+            shape((total, width), bf16), shape((total, 3 * DH), bf16), shape((8, DH), f32),
+            shape((64, 16 * gate_up_half.shape[2]), bf16), shape((64, 16 * down_half.shape[2]), bf16),
+        ],
+        [anywhere(), vmem(), vmem(), anywhere(), anywhere()],
+        [
+            VM(out_all.shape, bf16), VM((tokens, width), bf16), VM((total, DH), bf16),
+            VM((total, DH), f32), VM((total, DH), f32), VM((segments, DH, DH), f32),
+            VM((segments, 8, DH), f32), dma((2,)), dma((16,)), dma((16,)),
+        ] + Gather.sems() + Return.sems(2) + Return.sems(1),
+    )
+
+
+def last_kernel(act, down_cols, in_half, gate_up_rows, down_rows, out_rows, gains,
+                feed_out, in_mine, in_other, gate_up_other, down_other, out_other, gains_out,
+                got, total, theirs, x_s, x_r, g_s, g_r, *rest):
+    sems_i, scratch = rest[:5], rest[5:]
+    s = Spot()
+    greet(s)
+
+    def gain_copy(k):
+        to = (s.me + k) % 16
+        return send(gains.at[to], got.at[s.me], g_s.at[k], g_r.at[s.me], to)
+
+    back = Return(s, in_half, in_mine, 3, sems_i, other=in_other)
+    back.start()
+    for k in range(1, 16):
+        gain_copy(k).start()
+    pairs = [(gate_up_rows, gate_up_other), (down_rows, down_other), (out_rows, out_other)]
+    overs = [send_over(a, b, x_s.at[i], x_r.at[i], s) for i, (a, b) in enumerate(pairs)]
+    scatter = Scatter(s, act, down_cols, feed_out, scratch)
+    for cp in overs:
+        cp.start()
+
+    def sum_gains():
+        for k in range(1, 16):
+            src = (s.me + 16 - k) % 16
+            b = got.at[src]
+            send(b, b, g_s.at[k], g_r.at[src], s.me).wait_recv()
+        got[s.me] = gains[s.me]
+        acc = got[0]
+        for k in range(1, 16):
+            acc = acc + got[k]
+        total[...] = acc
+        send_over(total, theirs, x_s.at[3], x_r.at[3], s).start()
+
+    merged(scatter.tasks(), [lambda: None] * 3 + back.tasks() + [sum_gains])
+    scatter.finish()
+    back.finish()
+    cp = send_over(total, theirs, x_s.at[3], x_r.at[3], s)
+    cp.wait()
+    gains_out[...] = total[...] + theirs[...]
+    for cp in overs:
+        cp.wait()
+    for k in range(1, 16):
+        gain_copy(k).wait_send()
+
+
+def last(act, down_cols, in_half, gate_up_rows, down_rows, out_rows, gains, number):
+    shape = jax.ShapeDtypeStruct
+    total = act.shape[0]
+    width = down_cols.shape[0]
+    in_rows = shape((64, 16 * in_half.shape[2]), bf16)
+    like = [shape(a.shape, a.dtype) for a in (gate_up_rows, down_rows, out_rows)]
+    return communicate(
+        last_kernel, "last", number,
+        (act, down_cols, in_half, gate_up_rows, down_rows, out_rows, gains),
+        [vmem()] * 2 + [anywhere()] * 4 + [vmem()],
+        [shape((total // 16, width), f32), in_rows, in_rows] + like + [shape((8, 128), f32)],
+        [vmem()] + [anywhere()] * 5 + [vmem()],
+        [VM((16, 8, 128), f32), VM((8, 128), f32), VM((8, 128), f32),
+         dma((4,)), dma((4,)), dma((16,)), dma((16,))] + Return.sems(3) + Scatter.scratch(width),
+    )
+
+
+def body(
+    layer_input,
+    first_gain,
+    in_weight,
+    out_weight,
+    mix_gate,
+    second_gain,
+    gate_up,
+    down_weight,
+    document_starts,
+    cotangent,
+):
+    tokens, width = layer_input.shape
+    total = tokens * H
+    segments = total // SEG
+    dp = lax.axis_index("dp")
+
+    own_gains = jnp.zeros((8, tokens), f32)
+    own_gains = own_gains.at[0].set(first_gain.astype(f32)).at[1].set(second_gain.astype(f32))
+    mix = jnp.broadcast_to(jax.nn.sigmoid(mix_gate.astype(f32))[None], (8, DH))
+    numbers = jnp.arange(segments)
+    fresh = (numbers == 0) | (document_starts[0] > 0)
+    keep = jnp.broadcast_to(jnp.where(fresh, 0.0, 1.0)[:, None, None], (segments, 8, DH))
+
+    normed_all, in_cols, gains_all, qkv = project(layer_input, own_gains, in_weight, 0)
+    (local, mem_out, lse, combined, memory, normal, mixed_tokens, out_all, cot_all, gate_up_cols,
+     down_cols) = attend_forward(qkv, keep, mix, out_weight, cotangent, gate_up, down_weight, 1)
+    middle, hidden_all, act, feed_grad = feed(
+        mixed_tokens, layer_input, gains_all, out_all, cot_all, gate_up_cols, down_cols, 2
+    )
+
+    def own_and_other(grad):
+        split = grad.reshape(16, 2, 64, grad.shape[1])
+        mine = lax.dynamic_index_in_dim(split, dp, 1, False)
+        other = lax.dynamic_index_in_dim(split, 1 - dp, 1, False)
+        return mine, other.astype(bf16)
+
+    gate_up_mine, gate_up_sent = own_and_other(rows_dot(hidden_all, feed_grad))
+    down_mine, down_sent = own_and_other(rows_dot(cot_all, act))
+    hidden_grad, gate_up_got, down_got = scatter_dot(
+        feed_grad, gate_up_cols, (gate_up_sent, down_sent), "hidden_grad", 3
+    )
+    gate_up_half = (gate_up_mine + gate_up_got.astype(f32)).astype(bf16)
+    down_half = (down_mine + down_got.astype(f32)).astype(bf16)
+
+    first_all = gains_all[:, 0].reshape(width)
+    second_all = gains_all[:, 1].reshape(width)
+    upstream = cotangent.astype(f32)
+    second_factor = lax.rsqrt(jnp.mean(middle * middle, axis=-1, keepdims=True) + epsilon)
+    middle_norm_grad, second_local = norm_backward(middle, second_factor, second_all, hidden_grad)
+    middle_grad = upstream + middle_norm_grad
+    attended_all, projected_grad, mix_grad, gate_up_rows, down_rows = attend_backward(
+        middle_grad.astype(bf16), out_all, qkv, keep, mix, (local, mem_out, lse, memory, normal),
+        gate_up_half, down_half, 4,
+    )
+    out_rows = rows_dot(combined, attended_all).astype(bf16)
+    in_mine, in_sent = own_and_other(rows_dot(normed_all, projected_grad))
+    normed_grad, in_got = scatter_dot(projected_grad, in_cols, (in_sent,), "normed_grad", 5)
+    in_half = (in_mine + in_got.astype(f32)).astype(bf16)
+    inputs = layer_input.astype(f32)
+    first_factor = lax.rsqrt(jnp.mean(inputs * inputs, axis=-1, keepdims=True) + epsilon)
+    input_norm_grad, first_local = norm_backward(inputs, first_factor, first_all, normed_grad)
+    input_grad = middle_grad + input_norm_grad
+
+    mix_rows = jnp.where((jnp.arange(H) == lax.axis_index(AXIS))[:, None], mix_grad[0:1], 0.0)
+    gain_grads = jnp.stack(
+        [first_local.reshape(16, 128), second_local.reshape(16, 128), mix_rows], axis=1
+    )
+    gain_grads = jnp.pad(gain_grads, ((0, 0), (0, 5), (0, 0)))
+    (feed_out, in_mine_rows, in_other_rows, gate_up_other, down_other, out_other, gains_out) = last(
+        act, down_cols, in_half, gate_up_rows, down_rows, out_rows, gain_grads, 6
+    )
+    layer_output = (middle + feed_out).astype(bf16)
+
+    def both_halves(mine, other):
+        low = jnp.where(dp == 0, mine, other)
+        high = jnp.where(dp == 0, other, mine)
+        return jnp.concatenate([low, high]).astype(f32)
+
+    return (
+        layer_output,
+        input_grad,
+        gains_out[0],
+        both_halves(in_mine_rows, in_other_rows),
+        out_rows.astype(f32) + out_other.astype(f32),
+        gains_out[2],
+        gains_out[1],
+        both_halves(gate_up_rows, gate_up_other),
+        both_halves(down_rows, down_other),
+    )
+
+
 def solution(mesh):
+    one_group = mesh.shape[AXIS] == H and mesh.shape["dp"] == 2
     return jax.shard_map(
-        body,
+        body if one_group else body_groups,
         mesh=mesh,
         in_specs=(
             P(("dp", "fsdp"), None),

time: 1380 us -> 758 us (0.55)
  waiting for transfers between devices: 935 us -> 0 us
  Pallas kernels: 0 us -> 678 us
  matrix products: 138 us -> 26.5 us
  starting transfers between devices: 110 us -> 0 us
  local copies, waits for them, and re-layouts: 114 us -> 12.3 us
  blocking collectives: 27.9 us -> 0 us
  between operations: 15.3 us -> 1.16 us
    pallas_call x0 -> x7, Pallas kernels: none -> 678 us  [communicate(): pl.pallas_call(kernel, out_shape=outs, in_specs=in_specs, out_specs=out_s...]
    all_to_all x8 -> x0, waiting for transfers between devices: 354 us -> none  [the longest x3 189 us: columns(): out = lax.all_to_all(split, AXIS, 2, 0, tiled=True)]
    reduce_scatter x3 -> x0, waiting for transfers between devices: 204 us -> none  [scatter_sum(): lax.psum_scatter(whole, AXIS, scatter_dimension=0, tiled=True, axis_index...]
    psum x1 -> x0, waiting for transfers between devices: 196 us -> none  [over_sequences(): return lax.psum(part.astype(bf16), 'dp').astype(f32)]
    all_gather x5 -> x0, waiting for transfers between devices: 121 us -> none  [the longest x4 69.7 us: gather(): lax.all_gather(block, AXIS, axis=0, tiled=True, axis_index_groups=self.in...]
    all_to_all x8 -> x0, starting transfers between devices: 109 us -> none  [the longest x3 61.9 us: own_rows(): out = lax.all_to_all(split, AXIS, 0, 2, tiled=True)]
    dot_general x15 -> x0, matrix products: 60.7 us -> none  [the longest x1 14.9 us: body(): both = jnp.dot(hidden_all, gate_up_cols, preferred_element_type=f32)]
    unnamed x11 -> x0, waiting for transfers between devices: 60.6 us -> none
  transfers between devices with their start and end apart: 18 -> 0, of which waited for: 14 -> 0; matrix products, arithmetic and copies ran while one was open for 14% -> 0% of each run, Pallas kernels for 0% -> 0%
where the time goes in v2:
time: 758 us; the launch traced here: 749 us
  Pallas kernels  678 us (89%)
  other arithmetic  31 us (4%)
  matrix products  26.5 us (3%)
  local copies, waits for them, and re-layouts  12.3 us (2%)
    pallas_call x7, Pallas kernels, communicate(): pl.pallas_call(kernel, out_shape=outs, in_specs=in_specs, out_specs=out_s...  678 us
    dot_general x4, matrix products, dot(): lax.dot_general(left, right, ((dims[0], dims[1]), ((), ())), preferred_el...  26.5 us

profile of v2, /device:TPU:0, one launch (start us, length us, event | category | flops | bytes accessed | tf_op | source)
XLA Modules:
  0.0 749.1 jit_solution(15908087527419195626)
XLA Ops:
  0.7 0.7 add_divide_fusion
  1.3 0.7 bitcast_convert_fusion.3
  2.0 0.7 fusion.13
  2.7 1.2 fusion.6
  3.9 0.6 broadcast_in_dim.49.mix
  4.5 0.7 pad_convert_fusion
  5.2 0.7 broadcast_in_dim.48.keep
  5.9 77.9 %project.1 = (bf16[2048,2048]{1,0:T(8,128)(2,1)}, bf16[2048,384]{1,0:T(8,128)(2,1)}, f32[16,8,128]{2,1,0:T(8,128)}, bf16[2048,384]{1,0:T(8,128)(2,1)}) custom-call(bf16[128,2048]{1,0:T(8,128)(2,1)} %x.7, f32[8,128]{1,0:T(8,128)} %copy-done.19, bf16[128,6144]{1,0:T(8,128)(2,1)} %in_w.1), custom_call_target="tpu_custom_call" | custom-call | bytes 16777216 | tf_op jit(solution)/shard_map/project/pallas_call | solution.py:789
  83.8 0.9 fusion.15
  84.7 162.9 %attend.1 = (f32[2048,128]{1,0:T(8,128)}, f32[2048,128]{1,0:T(8,128)}, f32[2048,128]{1,0:T(8,128)}, bf16[2048,128]{1,0:T(8,128)(2,1)}, f32[2,128,128]{2,1,0:T(8,...) custom-call(bf16[2048,384]{1,0:T(8,128)(2,1)} %get-tuple-element.69., ...), custom_call_target="tpu_custom_call" | custom-call | bytes 16777216 | tf_op jit(solution)/shard_map/attend/pallas_call | solution.py:789
  247.6 65.7 %feed.1 = (f32[128,2048]{1,0:T(8,128)}, bf16[2048,2048]{1,0:T(8,128)(2,1)}, bf16[2048,512]{1,0:T(8,128)(2,1)}, bf16[2048,1024]{1,0:T(8,128)(2,1)}) custom-call(bf16[128,2048]{1,0:T(8,128)(2,1)} %get-tuple-element.70.combined, bf16[128,2048]{1,0:T(8,128)(2,1)} %x.7, f32[16,8,128]{2,1,0:T(8,128)} %get-tuple-element.71.gains_all, ...), custom_call_target="tpu_custom_call" | custom-call | bytes 16777216 | tf_op jit(solution)/shard_map/feed/pallas_call | solution.py:789
  313.3 0.0 copy-start.9
  313.3 7.7 %fusion.17 = f32[2048,512]{1,0:T(8,128)S(1)} fusion(bf16[2048,2048]{1,0:T(8,128)(2,1)} %get-tuple-element.73.cot_all, bf16[2048,512]{1,0:T(8,128)(2,1)} %get-tuple-element.77.act), kind=kOutput, calls=%fused_computation.62 | convolution fusion | flops 4294967296 | bytes 14680064 | tf_op jit(solution)/shard_map/dot_general | solution.py:46
  321.1 0.0 copy-start.10
  321.1 9.1 %fusion.16 = f32[2048,1024]{1,0:T(8,128)S(1)} fusion(bf16[2048,2048]{1,0:T(8,128)(2,1)S(1)} %copy-done.20, bf16[2048,1024]{1,0:T(8,128)(2,1)S(1)} %copy-done.9), kind=kOutput, calls=%fused_computation.61 | convolution fusion | flops 8589934592 | bytes 20971520 | tf_op jit(solution)/shard_map/dot_general | solution.py:46
  330.3 0.0 copy-start.5
  330.3 0.2 multiply_reduce_fusion.2
  330.4 1.4 fusion.11.rest_1_
  331.8 2.1 copy-done.5
  334.0 1.6 fusion.1.rest_0_
  335.6 76.6 %hidden_grad.1 = (f32[128,2048]{1,0:T(8,128)}, bf16[16,64,1024]{2,1,0:T(8,128)(2,1)}, bf16[16,64,512]{2,1,0:T(8,128)(2,1)}) custom-call(bf16[2048,1024]{1,0:T(8,128)(2,1)} %get-tuple-element.79.left, bf16[2048,1024]{1,0:T(8,128)(2,1)} %get-tuple-element.74.gate_up_cols.right, bf16[16,64,1024]{2,1,0:T(8,128)(2,1)} %fusion.1.rest_0_, ...), custom_call_target="tpu_custom_call" | custom-call | bytes 16777216 | tf_op jit(solution)/shard_map/hidden_grad/pallas_call | solution.py:789
  412.2 3.4 fusion.2.down_half
  415.6 4.5 fusion.gate_up_half
  420.1 0.3 multiply_reduce_fusion
  420.4 1.2 fusion.14
  421.6 125.9 %attend_back.1 = (bf16[2048,2048]{1,0:T(8,128)(2,1)}, bf16[2048,384]{1,0:T(8,128)(2,1)}, f32[8,128]{1,0:T(8,128)}, bf16[64,16384]{1,0:T(8,128)(2,1)}, bf16[64,8192]{1,0:T(8,128)(2,1)}) custom-call(bf16[128,2048]{1,0:T(8,128)(2,1)} %get-tuple-element.109.attended, bf16[2048,2048]{1,0:T(8,128)(2,1)} %get-tuple-element.72.out_all, ...), custom_call_target="tpu_custom_call" | custom-call | bytes 16777216 | tf_op jit(solution)/shard_map/attend_back/pallas_call | solution.py:789
  547.5 7.6 %fusion.18 = f32[2048,384]{1,0:T(8,128)S(1)} fusion(bf16[2048,2048]{1,0:T(8,128)(2,1)} %get-tuple-element.78, bf16[2048,384]{1,0:T(8,128)(2,1)} %get-tuple-element.89.left), kind=kOutput, calls=%fused_computation.63 | convolution fusion | flops 3221225472 | bytes 13107200 | tf_op jit(solution)/shard_map/dot_general | solution.py:46
  555.1 0.0 copy-start.15
  555.2 2.1 convolution_convert_fusion.out_rows
  557.2 0.7 slice_bitcast_fusion.3
  557.9 0.1 broadcast_select_fusion.6
  558.0 1.0 fusion.12.rest_0_
  559.0 60.7 %normed_grad.1 = (f32[128,2048]{1,0:T(8,128)}, bf16[16,64,384]{2,1,0:T(8,128)(2,1)}) custom-call(bf16[2048,384]{1,0:T(8,128)(2,1)} %get-tuple-element.89.left, bf16[2048,384]{1,0:T(8,128)(2,1)} %get-tuple-element.90.right, bf16[16,64,384]{2,1,0:T(8,128)(2,1)} %fusion.12.rest_0_), custom_call_target="tpu_custom_call" | custom-call | bytes 16777216 | tf_op jit(solution)/shard_map/normed_grad/pallas_call | solution.py:789
  619.8 2.8 fusion.3.in_half
  622.6 0.3 fusion.10
  622.9 1.4 fusion.9
  624.3 0.7 select_maximum_fusion.gains
  625.0 108.4 %last.1 = (f32[128,2048]{1,0:T(8,128)}, bf16[64,6144]{1,0:T(8,128)(2,1)}, bf16[64,6144]{1,0:T(8,128)(2,1)}, bf16[64,16384]{1,0:T(8,128)(2,1)}, bf16[64,8192]{1,0...) custom-call(bf16[2048,512]{1,0:T(8,128)(2,1)} %get-tuple-element.77.act, ...), custom_call_target="tpu_custom_call" | custom-call | bytes 16777216 | tf_op jit(solution)/shard_map/last/pallas_call | solution.py:789
  733.4 2.9 convert_add_fusion
  736.4 1.3 slice_bitcast_fusion
  737.7 0.3 broadcast_select_fusion.3
  738.0 0.1 broadcast_select_fusion.5
  738.1 1.2 copy-done.3
  739.3 0.6 copy-done.12
  740.0 0.3 broadcast_select_fusion.1
  740.2 2.0 maximum_convert_fusion.2
  742.2 2.4 maximum_convert_fusion.1
  744.7 4.2 maximum_convert_fusion
  (41 shorter events, 0.1 us)
Async XLA Ops:
  5.2 0.7 copy-start.19
  313.3 7.8 %copy-start.9 = (bf16[2048,1024]{1,0:T(8,128)(2,1)S(1)}, bf16[2048,1024]{1,0:T(8,128)(2,1)}, u32[]{:S(2)}) copy-start(bf16[2048,1024]{1,0:T(8,128)(2,1)} %get-tuple-element.79.left) | copy-start | bytes 12582916
  313.3 7.8 %copy-start.20 = (bf16[2048,2048]{1,0:T(8,128)(2,1)S(1)}, bf16[2048,2048]{1,0:T(8,128)(2,1)}, u32[]{:S(2)}) copy-start(bf16[2048,2048]{1,0:T(8,128)(2,1)} %get-tuple-element.80) | copy-start | bytes 25165828
  321.1 9.3 %copy-start.10 = (f32[2048,512]{1,0:T(8,128)}, f32[2048,512]{1,0:T(8,128)S(1)}, u32[]{:S(2)}) copy-start(f32[2048,512]{1,0:T(8,128)S(1)} %fusion.17) | copy-start | bytes 12582916
  321.1 9.1 %copy-start.1 = (f32[128,2048]{1,0:T(8,128)S(1)}, f32[128,2048]{1,0:T(8,128)}, u32[]{:S(2)}) copy-start(f32[128,2048]{1,0:T(8,128)} %get-tuple-element.76) | copy-start | bytes 3145732
  330.3 3.7 copy-start.5
  412.2 3.4 copy-start.13
  415.6 4.5 copy-start.8
  415.6 4.8 copy-start.11
  547.5 7.6 %copy-start = (bf16[2048,2048]{1,0:T(8,128)(2,1)S(1)}, bf16[2048,2048]{1,0:T(8,128)(2,1)}, u32[]{:S(2)}) copy-start(bf16[2048,2048]{1,0:T(8,128)(2,1)} %get-tuple-element.95) | copy-start | bytes 25165828
  547.5 7.6 %copy-start.14 = (bf16[2048,128]{1,0:T(8,128)(2,1)S(1)}, bf16[2048,128]{1,0:T(8,128)(2,1)}, u32[]{:S(2)}) copy-start(bf16[2048,128]{1,0:T(8,128)(2,1)} %get-tuple-element.94) | copy-start | bytes 1572868
  555.1 2.9 copy-start.15
  559.0 63.5 %copy-start.2 = (bf16[128,2048]{1,0:T(8,128)(2,1)S(1)}, bf16[128,2048]{1,0:T(8,128)(2,1)}, u32[]{:S(2)}) copy-start(bf16[128,2048]{1,0:T(8,128)(2,1)} %x.7) | copy-start | bytes 1572868
  619.8 2.8 copy-start.7
  625.0 108.4 %copy-start.4 = (bf16[128,2048]{1,0:T(8,128)(2,1)S(1)}, bf16[128,2048]{1,0:T(8,128)(2,1)}, u32[]{:S(2)}) copy-start(bf16[128,2048]{1,0:T(8,128)(2,1)} %convolution_convert_fusion.out_rows) | copy-start | bytes 1572868
  733.4 4.3 copy-start.6
  733.4 4.3 copy-start.16
  736.4 1.6 copy-start.17
  736.4 1.6 copy-start.18
  737.7 1.6 copy-start.3
  737.7 2.2 copy-start.12

commit v3 on v2

--- a/solution.py
+++ b/solution.py
@@ -435,21 +435,25 @@
 
 
 class Gather:
-    @staticmethod
-    def sems():
-        return [dma((CHUNKS, 4))] * 5 + [dma((CHUNKS, 8))] * 2
+    chunks = 4
+
+    @classmethod
+    def sems(cls):
+        return [dma((cls.chunks, 4))] * 5 + [dma((cls.chunks, 8))] * 2
 
     def __init__(self, s, src, dst, sems):
         self.s, self.src, self.dst = s, src, dst
-        self.zr, self.zu, self.zd, self.ys, self.yr, self.ss, self.sr = sems
-        self.rows = 128 // CHUNKS
+        self.zr, self.zu, self.zd, self.ys, self.yr, self.ss, self.sr = sems[:7]
+        self.rows = 128 // self.chunks
+        self.skip = 0
 
     def block(self, ch, z, y, c):
-        start = pl.multiple_of(self.s.at(z, y, c) * 128 + ch * self.rows, self.rows)
-        return self.dst.at[pl.ds(start, self.rows)]
+        start = self.s.at(z, y, c) * 128 + self.skip + ch * self.rows
+        return self.dst.at[pl.ds(pl.multiple_of(start, self.rows), self.rows)]
 
     def own(self, ch):
-        return self.src.at[pl.ds(ch * self.rows, self.rows)]
+        start = pl.multiple_of(self.skip + ch * self.rows, self.rows)
+        return self.src.at[pl.ds(start, self.rows)]
 
     def zcopy(self, ch, zo, up, own=False):
         s = self.s
@@ -475,11 +479,14 @@
 
     def start(self):
         s = self.s
-        for ch in range(CHUNKS):
+        for ch in range(self.chunks):
             pl.when(s.z < 3)(lambda: self.zcopy(ch, s.z, True, True).start())
             pl.when(s.z > 0)(lambda: self.zcopy(ch, s.z, False, True).start())
             self.ycopy(ch, s.z, True).start()
             self.scopy(ch, s.z, s.y, True).start()
+
+    def passed_on(self, ch, zo, yo):
+        self.scopy(ch, zo, yo).start()
 
     def z_arrive(self, ch, j):
         s = self.s
@@ -488,19 +495,19 @@
         pl.when((zo < s.z) & (s.z < 3))(lambda: self.zcopy(ch, zo, True).start())
         pl.when((zo > s.z) & (s.z > 0))(lambda: self.zcopy(ch, zo, False).start())
         self.ycopy(ch, zo).start()
-        self.scopy(ch, zo, s.y).start()
+        self.passed_on(ch, zo, s.y)
 
     def y_arrive(self, ch, j):
         s = self.s
         zo = s.arrival(j)
         b = self.block(ch, zo, 1 - s.y, s.c)
         send(b, b, self.ys.at[ch, zo], self.yr.at[ch, zo], s.me).wait_recv()
-        self.scopy(ch, zo, 1 - s.y).start()
+        self.passed_on(ch, zo, 1 - s.y)
 
     def s_arrive(self, j):
         s = self.s
         zo = s.arrival(j)
-        for ch in range(CHUNKS):
+        for ch in range(self.chunks):
             for yo in range(2):
                 n = zo * 2 + yo
                 b = self.block(ch, zo, yo, 1 - s.c)
@@ -509,7 +516,7 @@
     def tasks(self, use=None):
         out = []
         for step in range(5):
-            for ch in range(CHUNKS):
+            for ch in range(self.chunks):
                 if 0 < step < 4:
                     out.append(functools.partial(self.z_arrive, ch, step))
                 if step > 0:
@@ -522,13 +529,87 @@
 
     def drain(self):
         s = self.s
-        for ch in range(CHUNKS):
+        for ch in range(self.chunks):
             for zo in range(4):
                 pl.when((s.z < 3) & (zo <= s.z))(lambda: self.zcopy(ch, zo, True).wait_send())
                 pl.when((s.z > 0) & (zo >= s.z))(lambda: self.zcopy(ch, zo, False).wait_send())
                 self.ycopy(ch, zo).wait_send()
                 for yo in range(2):
                     self.scopy(ch, zo, yo).wait_send()
+
+
+class SharedGather(Gather):
+    chunks = 2
+
+    @classmethod
+    def sems(cls):
+        return Gather.sems.__func__(cls) + [dma((cls.chunks, 8))] * 4
+
+    def __init__(self, s, src, dst, sems):
+        super().__init__(s, src, dst, sems)
+        self.xs, self.xr, self.ts, self.tr = sems[7:]
+        self.rows = 64 // self.chunks
+        self.skip = s.dp * 64
+
+    def other(self, ch, z, y, c):
+        start = self.s.at(z, y, c) * 128 + (1 - self.s.dp) * 64 + ch * self.rows
+        return self.dst.at[pl.ds(pl.multiple_of(start, self.rows), self.rows)]
+
+    def xcopy(self, ch, zo, yo):
+        s = self.s
+        b = self.block(ch, zo, yo, s.c)
+        n = zo * 2 + yo
+        return send_over(b, b, self.xs.at[ch, n], self.xr.at[ch, n], s)
+
+    def tcopy(self, ch, zo, yo, own=False):
+        s = self.s
+        b = self.other(ch, zo, yo, s.c)
+        n = zo * 2 + yo
+        src = b
+        if own:
+            start = pl.multiple_of((1 - s.dp) * 64 + ch * self.rows, self.rows)
+            src = self.src.at[pl.ds(start, self.rows)]
+        return send(src, b, self.ts.at[ch, n], self.tr.at[ch, n], s.at(s.z, s.y, 1 - s.c))
+
+    def start(self):
+        super().start()
+        for ch in range(self.chunks):
+            self.tcopy(ch, self.s.z, self.s.y, True).start()
+
+    def passed_on(self, ch, zo, yo):
+        self.xcopy(ch, zo, yo).start()
+        self.scopy(ch, zo, yo).start()
+
+    def x_arrive(self, j, yo):
+        s = self.s
+        zo = s.arrival(j)
+        row = s.y if yo == 0 else 1 - s.y
+        for ch in range(self.chunks):
+            b = self.other(ch, zo, row, s.c)
+            n = zo * 2 + row
+            send_over(b, b, self.xs.at[ch, n], self.xr.at[ch, n], s).wait_recv()
+            self.tcopy(ch, zo, row).start()
+
+    def tasks(self, use=None):
+        out = super().tasks(use)
+        for j in range(4):
+            for yo in range(2):
+                if j + yo > 0:
+                    out.append(functools.partial(self.x_arrive, j, yo))
+        return out
+
+    def drain(self):
+        s = self.s
+        super().drain()
+        for ch in range(self.chunks):
+            for zo in range(4):
+                for yo in range(2):
+                    n = zo * 2 + yo
+                    b = self.other(ch, zo, yo, 1 - s.c)
+                    send(b, b, self.ts.at[ch, n], self.tr.at[ch, n], s.me).wait_recv()
+                    self.tcopy(ch, zo, yo).wait_send()
+                    far = (s.z != zo) | (s.y != yo)
+                    pl.when(far)(lambda: self.xcopy(ch, zo, yo).wait_send())
 
 
 class Columns:
@@ -680,13 +761,15 @@
 
 
 class Scatter:
+    lag = 3
+
     @staticmethod
     def scratch(width):
         q = QUARTERS
         return [
             VM((4, 2, 256, width), bf16), VM((4, 2, 128, width), bf16), VM((4, 2, 128, width), bf16),
-            VM((4, 128, width), bf16), VM((3, 128, width), bf16),
-            dma((4, q, 2)), dma((4, q, 2)), dma((4, q)), dma((4, q)), dma((3, q)), dma((3, q)),
+            VM((4, 128, width), bf16), VM((5, 128, width), bf16),
+            dma((4, q, 2)), dma((4, q, 2)), dma((4, q)), dma((4, q)), dma((4, q)), dma((5, q)),
         ]
 
     def __init__(self, s, left, right, out, scratch):
@@ -694,7 +777,7 @@
         self.part, self.sib, self.mid, self.got_y, self.got_z = scratch[:5]
         self.ss, self.sr, self.ys, self.yr, self.zs, self.zr = scratch[5:]
         self.cols = right.shape[0] // QUARTERS
-        self.order = [(s.z + 2) % 4, 3 - s.z, s.z + 1 - 2 * (s.z % 2), s.z]
+        self.order = [s.arrival(j) for j in (3, 2, 1, 0)]
 
     def w(self, h):
         return pl.ds(h * self.cols, self.cols)
@@ -721,10 +804,18 @@
 
     def z_copy(self, k, h):
         s = self.s
+        to = self.order[k]
+        up = to > s.z
+        hop = jnp.where(up, s.z + 1, s.z - 1)
+        slot = jnp.where(up | (hop != to), to, 4)
         return send(
-            self.mid.at[k, 1, :, self.w(h)], self.got_z.at[k, :, self.w(h)],
-            self.zs.at[k, h], self.zr.at[k, h], s.at(self.order[k], s.y, s.c),
+            self.mid.at[k, 1, :, self.w(h)], self.got_z.at[slot, :, self.w(h)],
+            self.zs.at[k, h], self.zr.at[slot, h], s.at(hop, s.y, s.c),
         )
+
+    def z_wait(self, slot, h):
+        b = self.got_z.at[slot, :, self.w(h)]
+        send(b, b, self.zs.at[0, h], self.zr.at[slot, h], self.s.me).wait_recv()
 
     def fold(self, k, h, slot):
         s = self.s
@@ -734,14 +825,26 @@
         self.mid[k, slot, :, self.w(h)] = total.astype(bf16)
 
     def after_y(self, k, h):
+        s = self.s
+        w = self.w(h)
         self.y_copy(k, h).wait_recv()
-        w = self.w(h)
         total = self.mid[k, 1, :, w].astype(f32) + self.got_y[k, :, w].astype(f32)
-        if k < 3:
+        if k == 3:
+            self.out[:, w] = total
+            return
+        to = self.order[k]
+        first = jnp.where(to > s.z, s.z == 0, s.z == 3)
+
+        @pl.when(first)
+        def _():
             self.mid[k, 1, :, w] = total.astype(bf16)
-            self.z_copy(k, h).start()
-        else:
-            self.out[:, w] = total
+
+        @pl.when(jnp.logical_not(first))
+        def _():
+            self.z_wait(to, h)
+            self.mid[k, 1, :, w] = (total + self.got_z[to, :, w].astype(f32)).astype(bf16)
+
+        self.z_copy(k, h).start()
 
     def tasks(self):
         steps = [(k, h) for k in range(4) for h in range(QUARTERS)]
@@ -756,18 +859,30 @@
             self.fold(k, h, 0)
             self.y_copy(k, h).start()
             self.fold(k, h, 1)
-            if i >= 2:
-                self.after_y(*steps[i - 2])
-
-        out = [functools.partial(step, i) for i in range(len(steps))]
-        out += [functools.partial(self.after_y, *steps[i]) for i in (len(steps) - 2, len(steps) - 1)]
+
+        out = []
+        for i in range(len(steps) + self.lag):
+            if i < len(steps):
+                out.append(functools.partial(step, i))
+            if i >= self.lag:
+                out.append(functools.partial(self.after_y, *steps[i - self.lag]))
         return out
 
     def finish(self):
-        for k in range(3):
-            for h in range(QUARTERS):
-                self.z_copy(k, h).wait_recv()
-                self.out[:, self.w(h)] += self.got_z[k, :, self.w(h)].astype(f32)
+        s = self.s
+        for h in range(QUARTERS):
+            w = self.w(h)
+
+            @pl.when(s.z > 0)
+            def _():
+                self.z_wait(s.z, h)
+                self.out[:, w] += self.got_z[s.z, :, w].astype(f32)
+
+            @pl.when(s.z < 3)
+            def _():
+                self.z_wait(4, h)
+                self.out[:, w] += self.got_z[4, :, w].astype(f32)
+
         for k in range(4):
             for h in range(QUARTERS):
                 self.sib_copy(k, h, 0).wait_send()
@@ -775,6 +890,53 @@
                 self.y_copy(k, h).wait_send()
                 if k < 3:
                     self.z_copy(k, h).wait_send()
+
+
+class Weigh:
+    steps = 8
+
+    @classmethod
+    def scratch(cls, cols):
+        return [
+            VM((16, 64, cols), f32), VM((16, 64, cols), bf16), VM((16, 64, cols), bf16),
+            dma((cls.steps,)), dma((cls.steps,)),
+        ]
+
+    def __init__(self, s, left, right, half, scratch):
+        self.s, self.left, self.right, self.half = s, left, right, half
+        self.mine, self.sent, self.got, self.xs, self.xr = scratch
+
+    def copy(self, i):
+        w = pl.ds(2 * i, 2)
+        return send_over(self.sent.at[w], self.got.at[w], self.xs.at[i], self.xr.at[i], self.s)
+
+    def compute(self, i):
+        low = self.s.dp == 0
+        got = rows_dot(self.left[:, pl.ds(i * 256, 256)], self.right[...])
+        for n in range(2):
+            a, b = got[n * 128:n * 128 + 64], got[n * 128 + 64:n * 128 + 128]
+            self.mine[2 * i + n] = jnp.where(low, a, b)
+            self.sent[2 * i + n] = jnp.where(low, b, a).astype(bf16)
+        self.copy(i).start()
+
+    def fold(self, i):
+        self.copy(i).wait_recv()
+        w = pl.ds(2 * i, 2)
+        self.half[w] = (self.mine[w] + self.got[w].astype(f32)).astype(bf16)
+
+    def products(self):
+        return [functools.partial(self.compute, i) for i in range(self.steps)]
+
+    def folds(self):
+        return [functools.partial(self.fold, i) for i in range(self.steps)]
+
+    def drain(self):
+        for i in range(self.steps):
+            self.copy(i).wait_send()
+
+
+def nothing(n):
+    return [lambda: None] * n
 
 
 def halves_of(refs, counts):
@@ -826,14 +988,14 @@
     gather.start()
 
     def use(j):
-        if j == 3:
+        if j == 1:
             columns.finish()
-            for i in range(4):
-                tok = pl.ds(pl.multiple_of(s.arrival(i) * 512, 512), 512)
-                out = jnp.dot(normed_all[tok, :], in_cols[...], preferred_element_type=f32)
-                projected[tok, :] = out.astype(bf16)
-
-    merged(gather.tasks(use), columns.tasks() + [lambda: None] * 6)
+        for i in {0: (), 1: (0, 1), 2: (2,), 3: (3,)}[j]:
+            tok = pl.ds(pl.multiple_of(s.arrival(i) * 512, 512), 512)
+            out = jnp.dot(normed_all[tok, :], in_cols[...], preferred_element_type=f32)
+            projected[tok, :] = out.astype(bf16)
+
+    merged(gather.tasks(use), nothing(2) + columns.tasks() + nothing(22))
     gather.drain()
     columns.drain()
     for k in range(1, 16):
@@ -998,7 +1160,7 @@
 def attend_kernel(qkv, keep, mix, out_w, cot, gate_up, down,
                   local, mem_out, lse, combined, memory, normal, mixed_tokens, out_all, cot_all,
                   gate_up_cols, down_cols, copies, t_s, t_r, *rest):
-    sems_o, sems_c, sems_g, sems_d = halves_of(rest, [7, 7, 5, 5])
+    sems_o, sems_c, sems_g, sems_d = halves_of(rest, [11, 7, 5, 5])
     s = Spot()
     mine = pl.ds(pl.multiple_of(s.me * 128, 128), 128)
     own = [
@@ -1008,12 +1170,14 @@
     for cp in own:
         cp.start()
     greet(s)
-    gather_o = Gather(s, out_w, out_all, sems_o)
+    gather_o = SharedGather(s, out_w, out_all, sems_o)
     gather_c = Gather(s, cot, cot_all, sems_c)
     columns_g = Columns(s, gate_up, gate_up_cols, 2, sems_g)
     columns_d = Columns(s, down, down_cols, 1, sems_d)
     gather_o.start()
+    gather_c.start()
     columns_g.start()
+    columns_d.start()
     attend = Attend(qkv, keep, mix, local, mem_out, lse, combined, memory, normal)
 
     def token_copy(j):
@@ -1028,15 +1192,12 @@
         for j in range((n * SEG + i * ROWS) // 128, (n * SEG + (i + 1) * ROWS) // 128):
             pl.when(s.me != j)(lambda: token_copy(j).start())
 
-    def late():
-        gather_c.start()
-        columns_d.start()
-
     compute = [attend.states] + [functools.partial(block, n, i) for n, i in attend.blocks()]
     merged(
-        gather_o.tasks() + [late] + gather_c.tasks(),
-        compute + [lambda: None] * len(compute),
-        [lambda: None] * 3 + columns_g.tasks() + [lambda: None] * 3 + columns_d.tasks(),
+        gather_o.tasks() + nothing(4),
+        gather_c.tasks(),
+        compute + nothing(len(compute)),
+        nothing(2) + columns_g.tasks() + columns_d.tasks(),
     )
     mixed_tokens[:, pl.ds(pl.multiple_of(s.me * DH, DH), DH)] = combined[mine, :]
     columns_g.finish()
@@ -1071,7 +1232,7 @@
             shape((width, gate_up.shape[1] // 16), bf16), shape((width, down.shape[1] // 16), bf16),
         ],
         [vmem()] * 7 + [anywhere()] * 4,
-        [dma((2,)), dma((16,)), dma((16,))] + Gather.sems() * 2 + Columns.sems(2) + Columns.sems(1),
+        [dma((2,)), dma((16,)), dma((16,))] + SharedGather.sems() + Gather.sems() + Columns.sems(2) + Columns.sems(1),
     )
 
 
@@ -1148,52 +1309,89 @@
     )
 
 
-def scatter_kernel(exchanges, left, right, *rest):
-    sent = rest[:exchanges]
-    out = rest[exchanges]
-    got = rest[exchanges + 1:2 * exchanges + 1]
-    x_s, x_r = rest[2 * exchanges + 1:2 * exchanges + 3]
+def hidden_grad_kernel(feed_grad, gate_up_cols, hidden_all, out, half, *rest):
     s = Spot()
     greet(s, plane=False)
-    overs = [send_over(a, b, x_s.at[i], x_r.at[i], s) for i, (a, b) in enumerate(zip(sent, got))]
-    scatter = Scatter(s, left, right, out, rest[2 * exchanges + 3:])
-    for cp in overs:
-        cp.start()
-    merged(scatter.tasks())
+    weigh = Weigh(s, hidden_all, feed_grad, half, rest[:5])
+    scatter = Scatter(s, feed_grad, gate_up_cols, out, rest[5:])
+    products = weigh.products()
+    merged(
+        scatter.tasks(),
+        products + nothing(16),
+        nothing(20) + weigh.folds(),
+    )
     scatter.finish()
-    for cp in overs:
-        cp.wait()
-
-
-def scatter_dot(left, right, sent, name, number):
+    weigh.drain()
+
+
+def hidden_grad_of(feed_grad, gate_up_cols, hidden_all, number):
     shape = jax.ShapeDtypeStruct
-    width = right.shape[0]
-    n = len(sent)
+    total, cols = feed_grad.shape
+    width = gate_up_cols.shape[0]
     return communicate(
-        functools.partial(scatter_kernel, n), name, number, (left, right, *sent),
-        [vmem()] * 2 + [anywhere()] * n,
-        [shape((left.shape[0] // 16, width), f32)] + [shape(a.shape, a.dtype) for a in sent],
-        [vmem()] + [anywhere()] * n,
-        [dma((max(n, 1),)), dma((max(n, 1),))] + Scatter.scratch(width),
+        hidden_grad_kernel, "hidden_grad", number, (feed_grad, gate_up_cols, hidden_all),
+        [vmem()] * 3, [shape((total // 16, width), f32), shape((16, 64, cols), bf16)], [vmem()] * 2,
+        Weigh.scratch(cols) + Scatter.scratch(width),
+    )
+
+
+def normed_grad_kernel(grad, in_cols, normed_all, down_half, gate_up_rows,
+                       out, half, down_rows, gate_up_other, x_s, x_r, *rest):
+    sems_d, sems_w, scratch = halves_of(rest, [5, 5, 11])
+    s = Spot()
+    greet(s)
+    weigh = Weigh(s, normed_all, grad, half, sems_w)
+    back = Return(s, down_half, down_rows, 1, sems_d)
+    scatter = Scatter(s, grad, in_cols, out, scratch)
+    over = send_over(gate_up_rows, gate_up_other, x_s.at[0], x_r.at[0], s)
+    back.start()
+    merged(
+        scatter.tasks(),
+        weigh.products() + [over.start] + nothing(20),
+        nothing(20) + weigh.folds(),
+    )
+    scatter.finish()
+    for task in back.tasks():
+        task()
+    back.finish()
+    weigh.drain()
+    over.wait()
+
+
+def normed_grad_of(grad, in_cols, normed_all, down_half, gate_up_rows, number):
+    shape = jax.ShapeDtypeStruct
+    total, cols = grad.shape
+    width = in_cols.shape[0]
+    return communicate(
+        normed_grad_kernel, "normed_grad", number,
+        (grad, in_cols, normed_all, down_half, gate_up_rows), [vmem()] * 3 + [anywhere()] * 2,
+        [
+            shape((total // 16, width), f32), shape((16, 64, cols), bf16),
+            shape((64, 16 * down_half.shape[2]), bf16), shape(gate_up_rows.shape, bf16),
+        ],
+        [vmem()] * 2 + [anywhere()] * 2,
+        [dma((1,)), dma((1,))] + Return.sems(1) + Weigh.scratch(cols) + Scatter.scratch(width),
     )
 
 
 def attend_back_kernel(attended, out_all, qkv, keep, mix, local, mem_out, lse, memory, normal,
-                       gate_up_half, down_half,
-                       attended_all, grad, mix_grad, gate_up_rows, down_rows,
-                       out_v, by_token, upstream, dk, dv, state_grad, norm_grad, copies, h_s, h_r,
+                       gate_up_half, cot_all, act,
+                       attended_all, grad, mix_grad, gate_up_rows, down_half,
+                       out_v, cot_v, by_token, upstream, dk, dv, state_grad, norm_grad, copies, h_s, h_r,
                        *rest):
-    sems_a, sems_g, sems_d = halves_of(rest, [7, 5, 5])
+    sems_a, sems_g, sems_w = halves_of(rest, [7, 5, 5])
     s = Spot()
     mine = pl.ds(pl.multiple_of(s.me * 128, 128), 128)
+    cot_load = pltpu.make_async_copy(cot_all, cot_v, copies.at[2])
     load = pltpu.make_async_copy(out_all, out_v, copies.at[0])
     load.start()
     own = pltpu.make_async_copy(attended, attended_all.at[mine], copies.at[1])
     own.start()
-    greet(s, other=False)
+    cot_load.start()
+    greet(s)
     gather = Gather(s, attended, attended_all, sems_a)
     back_g = Return(s, gate_up_half, gate_up_rows, 2, sems_g)
-    back_d = Return(s, down_half, down_rows, 1, sems_d)
+    weigh = Weigh(s, cot_v, act, down_half, sems_w)
     attend = AttendBack(qkv, keep, mix, local, mem_out, lse, memory, normal, upstream, grad,
                         mix_grad, dk, dv, state_grad, norm_grad)
     attend.clear()
@@ -1210,7 +1408,7 @@
     upstream[mine, :] = by_token[:, pl.ds(pl.multiple_of(s.me * DH, DH), DH)]
     gather.start()
     back_g.start()
-    back_d.start()
+    cot_load.wait()
 
     def arrive(j):
         b = upstream.at[pl.ds(j * 128, 128)]
@@ -1224,18 +1422,19 @@
     compute = [functools.partial(block, n, i) for n, i in attend.blocks()] + [attend.states]
     merged(
         gather.tasks(),
-        [lambda: None] * 2 + compute,
-        [lambda: None] * 10 + back_g.tasks() + back_d.tasks(),
+        nothing(2) + compute,
+        weigh.products() + weigh.folds(),
+        nothing(10) + back_g.tasks(),
     )
     back_g.finish()
-    back_d.finish()
+    weigh.drain()
     for j in range(16):
         pl.when(s.me != j)(lambda: head_copy(j).wait_send())
     gather.drain()
     own.wait()
 
 
-def attend_backward(attended, out_all, qkv, keep, mix, saved, gate_up_half, down_half, number):
+def attend_backward(attended, out_all, qkv, keep, mix, saved, gate_up_half, cot_all, act, number):
     tokens, width = attended.shape
     total = qkv.shape[0]
     segments = total // SEG
@@ -1244,23 +1443,24 @@
     return communicate(
         attend_back_kernel, "attend_back", number,
         (attended, out_all, qkv, keep, mix, local, mem_out, lse, memory, normal,
-         gate_up_half, down_half),
-        [vmem(), anywhere()] + [vmem()] * 8 + [anywhere()] * 2,
+         gate_up_half, cot_all, act),
+        [vmem(), anywhere()] + [vmem()] * 8 + [anywhere()] * 2 + [vmem()],
         [
             shape((total, width), bf16), shape((total, 3 * DH), bf16), shape((8, DH), f32),
-            shape((64, 16 * gate_up_half.shape[2]), bf16), shape((64, 16 * down_half.shape[2]), bf16),
+            shape((64, 16 * gate_up_half.shape[2]), bf16), shape((16, 64, act.shape[1]), bf16),
         ],
-        [anywhere(), vmem(), vmem(), anywhere(), anywhere()],
+        [anywhere(), vmem(), vmem(), anywhere(), vmem()],
         [
-            VM(out_all.shape, bf16), VM((tokens, width), bf16), VM((total, DH), bf16),
+            VM(out_all.shape, bf16), VM(cot_all.shape, bf16), VM((tokens, width), bf16),
+            VM((total, DH), bf16),
             VM((total, DH), f32), VM((total, DH), f32), VM((segments, DH, DH), f32),
-            VM((segments, 8, DH), f32), dma((2,)), dma((16,)), dma((16,)),
-        ] + Gather.sems() + Return.sems(2) + Return.sems(1),
-    )
-
-
-def last_kernel(act, down_cols, in_half, gate_up_rows, down_rows, out_rows, gains,
-                feed_out, in_mine, in_other, gate_up_other, down_other, out_other, gains_out,
+            VM((segments, 8, DH), f32), dma((3,)), dma((16,)), dma((16,)),
+        ] + Gather.sems() + Return.sems(2) + Weigh.scratch(act.shape[1]),
+    )
+
+
+def last_kernel(act, down_cols, in_half, down_rows, out_rows, gains,
+                feed_out, in_mine, in_other, down_other, out_other, gains_out,
                 got, total, theirs, x_s, x_r, g_s, g_r, *rest):
     sems_i, scratch = rest[:5], rest[5:]
     s = Spot()
@@ -1274,7 +1474,7 @@
     back.start()
     for k in range(1, 16):
         gain_copy(k).start()
-    pairs = [(gate_up_rows, gate_up_other), (down_rows, down_other), (out_rows, out_other)]
+    pairs = [(down_rows, down_other), (out_rows, out_other)]
     overs = [send_over(a, b, x_s.at[i], x_r.at[i], s) for i, (a, b) in enumerate(pairs)]
     scatter = Scatter(s, act, down_cols, feed_out, scratch)
     for cp in overs:
@@ -1304,18 +1504,18 @@
         gain_copy(k).wait_send()
 
 
-def last(act, down_cols, in_half, gate_up_rows, down_rows, out_rows, gains, number):
+def last(act, down_cols, in_half, down_rows, out_rows, gains, number):
     shape = jax.ShapeDtypeStruct
     total = act.shape[0]
     width = down_cols.shape[0]
     in_rows = shape((64, 16 * in_half.shape[2]), bf16)
-    like = [shape(a.shape, a.dtype) for a in (gate_up_rows, down_rows, out_rows)]
+    like = [shape(a.shape, a.dtype) for a in (down_rows, out_rows)]
     return communicate(
         last_kernel, "last", number,
-        (act, down_cols, in_half, gate_up_rows, down_rows, out_rows, gains),
-        [vmem()] * 2 + [anywhere()] * 4 + [vmem()],
+        (act, down_cols, in_half, down_rows, out_rows, gains),
+        [vmem()] * 2 + [anywhere()] * 3 + [vmem()],
         [shape((total // 16, width), f32), in_rows, in_rows] + like + [shape((8, 128), f32)],
-        [vmem()] + [anywhere()] * 5 + [vmem()],
+        [vmem()] + [anywhere()] * 4 + [vmem()],
         [VM((16, 8, 128), f32), VM((8, 128), f32), VM((8, 128), f32),
          dma((4,)), dma((4,)), dma((16,)), dma((16,))] + Return.sems(3) + Scatter.scratch(width),
     )
@@ -1352,19 +1552,7 @@
         mixed_tokens, layer_input, gains_all, out_all, cot_all, gate_up_cols, down_cols, 2
     )
 
-    def own_and_other(grad):
-        split = grad.reshape(16, 2, 64, grad.shape[1])
-        mine = lax.dynamic_index_in_dim(split, dp, 1, False)
-        other = lax.dynamic_index_in_dim(split, 1 - dp, 1, False)
-        return mine, other.astype(bf16)
-
-    gate_up_mine, gate_up_sent = own_and_other(rows_dot(hidden_all, feed_grad))
-    down_mine, down_sent = own_and_other(rows_dot(cot_all, act))
-    hidden_grad, gate_up_got, down_got = scatter_dot(
-        feed_grad, gate_up_cols, (gate_up_sent, down_sent), "hidden_grad", 3
-    )
-    gate_up_half = (gate_up_mine + gate_up_got.astype(f32)).astype(bf16)
-    down_half = (down_mine + down_got.astype(f32)).astype(bf16)
+    hidden_grad, gate_up_half = hidden_grad_of(feed_grad, gate_up_cols, hidden_all, 3)
 
     first_all = gains_all[:, 0].reshape(width)
     second_all = gains_all[:, 1].reshape(width)
@@ -1372,14 +1560,14 @@
     second_factor = lax.rsqrt(jnp.mean(middle * middle, axis=-1, keepdims=True) + epsilon)
     middle_norm_grad, second_local = norm_backward(middle, second_factor, second_all, hidden_grad)
     middle_grad = upstream + middle_norm_grad
-    attended_all, projected_grad, mix_grad, gate_up_rows, down_rows = attend_backward(
+    attended_all, projected_grad, mix_grad, gate_up_rows, down_half = attend_backward(
         middle_grad.astype(bf16), out_all, qkv, keep, mix, (local, mem_out, lse, memory, normal),
-        gate_up_half, down_half, 4,
+        gate_up_half, cot_all, act, 4,
     )
     out_rows = rows_dot(combined, attended_all).astype(bf16)
-    in_mine, in_sent = own_and_other(rows_dot(normed_all, projected_grad))
-    normed_grad, in_got = scatter_dot(projected_grad, in_cols, (in_sent,), "normed_grad", 5)
-    in_half = (in_mine + in_got.astype(f32)).astype(bf16)
+    normed_grad, in_half, down_rows, gate_up_other = normed_grad_of(
+        projected_grad, in_cols, normed_all, down_half, gate_up_rows, 5
+    )
     inputs = layer_input.astype(f32)
     first_factor = lax.rsqrt(jnp.mean(inputs * inputs, axis=-1, keepdims=True) + epsilon)
     input_norm_grad, first_local = norm_backward(inputs, first_factor, first_all, normed_grad)
@@ -1390,8 +1578,8 @@
         [first_local.reshape(16, 128), second_local.reshape(16, 128), mix_rows], axis=1
     )
     gain_grads = jnp.pad(gain_grads, ((0, 0), (0, 5), (0, 0)))
-    (feed_out, in_mine_rows, in_other_rows, gate_up_other, down_other, out_other, gains_out) = last(
-        act, down_cols, in_half, gate_up_rows, down_rows, out_rows, gain_grads, 6
+    feed_out, in_mine_rows, in_other_rows, down_other, out_other, gains_out = last(
+        act, down_cols, in_half, down_rows, out_rows, gain_grads, 6
     )
     layer_output = (middle + feed_out).astype(bf16)
 

time: 758 us -> 683 us (0.901)
  Pallas kernels: 678 us -> 638 us
  matrix products: 26.5 us -> 5.46 us
    pallas_call x7, Pallas kernels: 678 us -> 638 us  [communicate(): pl.pallas_call(kernel, out_shape=outs, in_specs=in_specs, out_specs=out_s...]
    dot_general x4 -> x1, matrix products: 26.5 us -> 5.46 us  [dot(): lax.dot_general(left, right, ((dims[0], dims[1]), ((), ())), preferred_el...]
    convert_element_type x3 -> x0, other arithmetic: 10.7 us -> none  [the longest x1 4.49 us: body(): gate_up_half = (gate_up_mine + gate_up_got.astype(f32)).astype(bf16)]
where the time goes in v3:
time: 683 us; the launch traced here: 674 us
  Pallas kernels  638 us (93%)
  other arithmetic  24 us (4%)
    pallas_call x7, Pallas kernels, communicate(): pl.pallas_call(kernel, out_shape=outs, in_specs=in_specs, out_specs=out_s...  638 us

profile of v3, /device:TPU:0, one launch (start us, length us, event | category | flops | bytes accessed | tf_op | source)
XLA Modules:
  0.0 674.2 jit_solution(10743794018532607737)
XLA Ops:
  0.7 0.7 add_divide_fusion
  1.3 0.7 bitcast_convert_fusion
  2.0 0.7 fusion.7
  2.6 1.2 fusion.2
  3.9 0.6 broadcast_in_dim.49.mix
  4.5 0.7 pad_convert_fusion
  5.2 0.7 broadcast_in_dim.48.keep
  5.8 0.0 copy-done.12
  5.9 75.1 %project.1 = (bf16[2048,2048]{1,0:T(8,128)(2,1)}, bf16[2048,384]{1,0:T(8,128)(2,1)}, f32[16,8,128]{2,1,0:T(8,128)}, bf16[2048,384]{1,0:T(8,128)(2,1)}) custom-call(bf16[128,2048]{1,0:T(8,128)(2,1)} %x.7, f32[8,128]{1,0:T(8,128)} %copy-done.12, bf16[128,6144]{1,0:T(8,128)(2,1)} %in_w.1), custom_call_target="tpu_custom_call" | custom-call | bytes 16777216 | tf_op jit(solution)/shard_map/project/pallas_call | solution.py:951
  81.0 0.9 fusion.9
  81.9 167.7 %attend.1 = (f32[2048,128]{1,0:T(8,128)}, f32[2048,128]{1,0:T(8,128)}, f32[2048,128]{1,0:T(8,128)}, bf16[2048,128]{1,0:T(8,128)(2,1)}, f32[2,128,128]{2,1,0:T(8,...) custom-call(bf16[2048,384]{1,0:T(8,128)(2,1)} %get-tuple-element.69., ...), custom_call_target="tpu_custom_call" | custom-call | bytes 16777216 | tf_op jit(solution)/shard_map/attend/pallas_call | solution.py:951
  249.6 63.6 %feed.1 = (f32[128,2048]{1,0:T(8,128)}, bf16[2048,2048]{1,0:T(8,128)(2,1)}, bf16[2048,512]{1,0:T(8,128)(2,1)}, bf16[2048,1024]{1,0:T(8,128)(2,1)}) custom-call(bf16[128,2048]{1,0:T(8,128)(2,1)} %get-tuple-element.70.combined, bf16[128,2048]{1,0:T(8,128)(2,1)} %x.7, f32[16,8,128]{2,1,0:T(8,128)} %get-tuple-element.71.gains_all, ...), custom_call_target="tpu_custom_call" | custom-call | bytes 16777216 | tf_op jit(solution)/shard_map/feed/pallas_call | solution.py:951
  313.2 0.0 copy-start
  313.2 68.8 %hidden_grad.1 = (f32[128,2048]{1,0:T(8,128)}, bf16[16,64,1024]{2,1,0:T(8,128)(2,1)}) custom-call(bf16[2048,1024]{1,0:T(8,128)(2,1)} %get-tuple-element.78.feed_grad, bf16[2048,1024]{1,0:T(8,128)(2,1)} %get-tuple-element.74.gate_up_cols, bf16[2048,2048]{1,0:T(8,128)(2,1)} %get-tuple-element.79.hidden_all), custom_call_target="tpu_custom_call" | custom-call | bytes 16777216 | tf_op jit(solution)/shard_map/hidden_grad/pallas_call | solution.py:951
  382.0 0.0 copy-start.5
  382.0 0.0 copy-start.6
  382.0 0.0 copy-done
  382.0 0.2 multiply_reduce_fusion.2
  382.2 1.6 multiply_reduce_fusion
  383.8 0.0 copy-done.5
  383.8 0.0 copy-done.6
  383.8 1.2 fusion.8
  385.0 106.3 %attend_back.1 = (bf16[2048,2048]{1,0:T(8,128)(2,1)}, bf16[2048,384]{1,0:T(8,128)(2,1)}, f32[8,128]{1,0:T(8,128)}, bf16[64,16384]{1,0:T(8,128)(2,1)}, bf16[16,64,512]{2,1,0:T(8,128)(2,1)}) custom-call(bf16[128,2048]{1,0:T(8,128)(2,1)} %get-tuple-element.109.attended, bf16[2048,2048]{1,0:T(8,128)(2,1)} %get-tuple-element.72.out_all, ...), custom_call_target="tpu_custom_call" | custom-call | bytes 16777216 | tf_op jit(solution)/shard_map/attend_back/pallas_call | solution.py:951
  491.3 0.0 copy-done.8
  491.3 5.5 convolution_convert_fusion.out_rows
  496.8 84.1 %normed_grad.1 = (f32[128,2048]{1,0:T(8,128)}, bf16[16,64,384]{2,1,0:T(8,128)(2,1)}, bf16[64,8192]{1,0:T(8,128)(2,1)}, bf16[64,16384]{1,0:T(8,128)(2,1)}) custom-call(bf16[2048,384]{1,0:T(8,128)(2,1)} %get-tuple-element.87.grad, bf16[2048,384]{1,0:T(8,128)(2,1)} %get-tuple-element.88.in_cols, bf16[2048,2048]{1,0:T(8,128)(2,1)} %get-tuple-element.89.normed_all, ...), custom_call_target="tpu_custom_call" | custom-call | bytes 16777216 | tf_op jit(solution)/shard_map/normed_grad/pallas_call | solution.py:951
  580.9 0.7 slice_bitcast_fusion.3
  581.5 0.1 broadcast_select_fusion.6
  581.6 0.0 copy-done.1
  581.6 1.5 fusion.6
  583.2 2.6 fusion.5
  585.8 0.7 select_maximum_fusion.gains
  586.5 72.0 %last.1 = (f32[128,2048]{1,0:T(8,128)}, bf16[64,6144]{1,0:T(8,128)(2,1)}, bf16[64,6144]{1,0:T(8,128)(2,1)}, bf16[64,8192]{1,0:T(8,128)(2,1)}, bf16[128,2048]{1,0:T(8,128)(2,1)}, /*index=5*/f32[8,128]{1,0:T(8,128)}) custom-call(bf16[2048,512]{1,0:T(8,128)(2,1)} %get-tuple-element.77.act, bf16[2048,512]{1,0:T(8,128)(2,1)} %get-tuple-element.75.down_cols, ...), custom_call_target="tpu_custom_call" | custom-call | bytes 16777216 | tf_op jit(solution)/shard_map/last/pallas_call | solution.py:951
  658.5 0.0 copy-start.4
  658.5 0.0 copy-start.9
  658.5 0.0 copy-done.3
  658.5 2.9 convert_add_fusion
  661.5 1.3 slice_bitcast_fusion
  662.8 0.0 copy-done.4
  662.8 0.0 copy-done.9
  662.8 0.3 broadcast_select_fusion.3
  663.1 0.1 broadcast_select_fusion.5
  663.2 1.2 copy-done.2
  664.4 0.6 copy-done.7
  665.0 0.3 broadcast_select_fusion.1
  665.3 2.0 maximum_convert_fusion.2
  667.3 2.4 maximum_convert_fusion.1
  669.7 4.2 maximum_convert_fusion
  (16 shorter events, 0.1 us)
Async XLA Ops:
  5.2 0.7 copy-start.12
  313.2 68.8 %copy-start = (f32[128,2048]{1,0:T(8,128)S(1)}, f32[128,2048]{1,0:T(8,128)}, u32[]{:S(2)}) copy-start(f32[128,2048]{1,0:T(8,128)} %get-tuple-element.76) | copy-start | bytes 3145732
  382.0 1.8 copy-start.5
  382.0 1.8 copy-start.6
  385.0 106.3 %copy-start.8 = (bf16[2048,128]{1,0:T(8,128)(2,1)S(1)}, bf16[2048,128]{1,0:T(8,128)(2,1)}, u32[]{:S(2)}) copy-start(bf16[2048,128]{1,0:T(8,128)(2,1)} %get-tuple-element.94) | copy-start | bytes 1572868
  496.8 84.9 %copy-start.1 = (bf16[128,2048]{1,0:T(8,128)(2,1)S(1)}, bf16[128,2048]{1,0:T(8,128)(2,1)}, u32[]{:S(2)}) copy-start(bf16[128,2048]{1,0:T(8,128)(2,1)} %x.7) | copy-start | bytes 1572868
  586.5 72.1 %copy-start.3 = (bf16[128,2048]{1,0:T(8,128)(2,1)S(1)}, bf16[128,2048]{1,0:T(8,128)(2,1)}, u32[]{:S(2)}) copy-start(bf16[128,2048]{1,0:T(8,128)(2,1)} %convolution_convert_fusion.out_rows) | copy-start | bytes 1572868
  658.5 4.3 copy-start.4
  658.5 4.3 copy-start.9
  661.5 1.6 copy-start.10
  661.5 1.6 copy-start.11
  662.8 1.6 copy-start.2
  662.8 2.2 copy-start.7

commit v4 on v3

--- a/solution.py
+++ b/solution.py
@@ -362,8 +362,7 @@
 
 MESH = pl.DeviceIdType.MESH
 LIMIT = 60 * 2**20
-CHUNKS = 4
-QUARTERS = 4
+FILL = ((0, 512), (512, 1024), (1536, 512))
 ROWS = 256
 dma = pltpu.SemaphoreType.DMA
 VM = pltpu.VMEM
@@ -387,6 +386,13 @@
 
     def at(self, z, y, c):
         return z * 4 + y * 2 + c
+
+    def partner(self, k):
+        out = self.me
+        for bit in (1, 2, 4, 8):
+            if k & bit:
+                out = out + bit - 2 * bit * ((self.me // bit) % 2)
+        return out
 
     def arrival(self, j):
         if j == 0:
@@ -515,16 +521,16 @@
 
     def tasks(self, use=None):
         out = []
-        for step in range(5):
+        for step in range(1, 5):
             for ch in range(self.chunks):
-                if 0 < step < 4:
+                if step < 4:
                     out.append(functools.partial(self.z_arrive, ch, step))
-                if step > 0:
-                    out.append(functools.partial(self.y_arrive, ch, step - 1))
-            if step > 0:
-                out.append(functools.partial(self.s_arrive, step - 1))
-                if use is not None:
-                    out.append(functools.partial(use, step - 1))
+                out.append(functools.partial(self.y_arrive, ch, step - 1))
+                if step == 4 and ch < 3 and use is not None:
+                    out.append(functools.partial(use, ch))
+            out.append(functools.partial(self.s_arrive, step - 1))
+        if use is not None:
+            out.append(functools.partial(use, 3))
         return out
 
     def drain(self):
@@ -590,8 +596,8 @@
             send_over(b, b, self.xs.at[ch, n], self.xr.at[ch, n], s).wait_recv()
             self.tcopy(ch, zo, row).start()
 
-    def tasks(self, use=None):
-        out = super().tasks(use)
+    def tasks(self):
+        out = super().tasks()
         for j in range(4):
             for yo in range(2):
                 if j + yo > 0:
@@ -630,7 +636,7 @@
 
     def copy(self, k, p):
         s = self.s
-        to = (s.me + k) % 16
+        to = s.partner(k)
         half = pl.ds(pl.multiple_of(s.dp * 64, 64), 64)
         return send(
             self.w.at[half, self.cols(p, to)],
@@ -646,12 +652,14 @@
             self.own.at[p],
         )
 
-    def start(self):
-        for k in range(1, 16):
-            for p in range(self.parts):
-                self.copy(k, p).start()
+    def begin(self, k):
         for p in range(self.parts):
-            self.local(p).start()
+            (self.copy(k, p) if k else self.local(p)).start()
+
+    def start(self, ahead=16):
+        self.ahead = ahead
+        for k in range(ahead):
+            self.begin(k)
 
     def over(self, src):
         s = self.s
@@ -660,7 +668,9 @@
 
     def arrive(self, k):
         s = self.s
-        src = (s.me + 16 - k) % 16
+        if k + self.ahead - 1 < 16:
+            self.begin(k + self.ahead - 1)
+        src = s.partner(k)
         for p in range(self.parts):
             b = self.dst.at[self.rows(src, s.dp), pl.ds(p * self.e, self.e)]
             send(b, b, self.ps.at[k, p], self.pr.at[src, p], s.me).wait_recv()
@@ -672,7 +682,7 @@
     def finish(self):
         s = self.s
         for k in range(1, 16):
-            src = (s.me + 16 - k) % 16
+            src = s.partner(k)
             b = self.dst.at[self.rows(src, 1 - s.dp)]
             send_over(b, b, self.xs.at[src], self.xr.at[src], s).wait_recv()
         for p in range(self.parts):
@@ -683,7 +693,7 @@
         for k in range(1, 16):
             for p in range(self.parts):
                 self.copy(k, p).wait_send()
-            self.over((s.me + 16 - k) % 16).wait_send()
+            self.over(s.partner(k)).wait_send()
 
 
 class Return:
@@ -691,6 +701,8 @@
     def sems(parts):
         return [dma((16, parts))] * 4 + [dma((parts,))]
 
+    ahead = 16
+
     def __init__(self, s, src, dst, parts, sems, other=None):
         self.s, self.src, self.dst, self.parts, self.other = s, src, dst, parts, other
         self.e = src.shape[2] // parts
@@ -701,7 +713,7 @@
 
     def copy(self, k, p):
         s = self.s
-        to = (s.me + k) % 16
+        to = s.partner(k)
         return send(
             self.src.at[to, :, pl.ds(p * self.e, self.e)], self.place(self.dst, p, s.me),
             self.ps.at[k, p], self.pr.at[s.me, p], to,
@@ -714,15 +726,19 @@
             self.own.at[p],
         )
 
-    def start(self):
+    def begin(self, k):
         for p in range(self.parts):
+            if k:
+                self.copy(k, p).start()
+                continue
             self.local(p).start()
-        for k in range(1, 16):
-            for p in range(self.parts):
-                self.copy(k, p).start()
-        if self.other is not None:
-            for p in range(self.parts):
+            if self.other is not None:
                 self.over(self.s.me, p, own=True).start()
+
+    def start(self, ahead=16):
+        self.ahead = ahead
+        for k in range(ahead):
+            self.begin(k)
 
     def over(self, h, p, own=False):
         s = self.s
@@ -731,7 +747,9 @@
 
     def arrive(self, k):
         s = self.s
-        h = (s.me + 16 - k) % 16
+        if k + self.ahead - 1 < 16:
+            self.begin(k + self.ahead - 1)
+        h = s.partner(k)
         for p in range(self.parts):
             b = self.place(self.dst, p, h)
             send(b, b, self.ps.at[k, p], self.pr.at[h, p], s.me).wait_recv()
@@ -747,7 +765,7 @@
             self.local(p).wait()
         if self.other is not None:
             for k in range(16):
-                h = (s.me + 16 - k) % 16
+                h = s.partner(k)
                 for p in range(self.parts):
                     b = self.place(self.other, p, h)
                     send_over(b, b, self.xs.at[h, p], self.xr.at[h, p], s).wait_recv()
@@ -757,7 +775,7 @@
         if self.other is not None:
             for k in range(16):
                 for p in range(self.parts):
-                    self.over((s.me + 16 - k) % 16, p).wait_send()
+                    self.over(s.partner(k), p).wait_send()
 
 
 class Scatter:
@@ -765,18 +783,19 @@
 
     @staticmethod
     def scratch(width):
-        q = QUARTERS
+        q = width // 512
         return [
             VM((4, 2, 256, width), bf16), VM((4, 2, 128, width), bf16), VM((4, 2, 128, width), bf16),
             VM((4, 128, width), bf16), VM((5, 128, width), bf16),
             dma((4, q, 2)), dma((4, q, 2)), dma((4, q)), dma((4, q)), dma((4, q)), dma((5, q)),
         ]
 
-    def __init__(self, s, left, right, out, scratch):
-        self.s, self.left, self.right, self.out = s, left, right, out
+    def __init__(self, s, left, right, out, scratch, first=0):
+        self.s, self.left, self.right, self.out, self.first = s, left, right, out, first
         self.part, self.sib, self.mid, self.got_y, self.got_z = scratch[:5]
         self.ss, self.sr, self.ys, self.yr, self.zs, self.zr = scratch[5:]
-        self.cols = right.shape[0] // QUARTERS
+        self.cols = 512
+        self.pieces = out.shape[1] // 512
         self.order = [s.arrival(j) for j in (3, 2, 1, 0)]
 
     def w(self, h):
@@ -784,7 +803,7 @@
 
     def compute(self, k, h, yd, slot):
         tok = pl.multiple_of((self.order[k] * 2 + yd) * 256, 256)
-        p = cols_dot(self.left[pl.ds(tok, 256), :], self.right[self.w(h), :])
+        p = cols_dot(self.left[pl.ds(tok, 256), :], self.right[pl.ds(self.first + h * self.cols, self.cols), :])
         self.part[k, slot, :, self.w(h)] = p.astype(bf16)
 
     def sib_copy(self, k, h, slot):
@@ -847,7 +866,7 @@
         self.z_copy(k, h).start()
 
     def tasks(self):
-        steps = [(k, h) for k in range(4) for h in range(QUARTERS)]
+        steps = [(k, h) for k in range(4) for h in range(self.pieces)]
         s = self.s
 
         def step(i):
@@ -870,7 +889,7 @@
 
     def finish(self):
         s = self.s
-        for h in range(QUARTERS):
+        for h in range(self.pieces):
             w = self.w(h)
 
             @pl.when(s.z > 0)
@@ -884,7 +903,7 @@
                 self.out[:, w] += self.got_z[4, :, w].astype(f32)
 
         for k in range(4):
-            for h in range(QUARTERS):
+            for h in range(self.pieces):
                 self.sib_copy(k, h, 0).wait_send()
                 self.sib_copy(k, h, 1).wait_send()
                 self.y_copy(k, h).wait_send()
@@ -902,27 +921,36 @@
             dma((cls.steps,)), dma((cls.steps,)),
         ]
 
-    def __init__(self, s, left, right, half, scratch):
-        self.s, self.left, self.right, self.half = s, left, right, half
+    def __init__(self, s, left, right, half, scratch, back=None):
+        self.s, self.left, self.right, self.half, self.back = s, left, right, half, back
         self.mine, self.sent, self.got, self.xs, self.xr = scratch
 
-    def copy(self, i):
+    def at(self, n):
+        return self.s.partner(2 * n) // 2
+
+    def copy(self, n):
+        i = self.at(n)
         w = pl.ds(2 * i, 2)
         return send_over(self.sent.at[w], self.got.at[w], self.xs.at[i], self.xr.at[i], self.s)
 
-    def compute(self, i):
+    def compute(self, n):
+        i = self.at(n)
         low = self.s.dp == 0
-        got = rows_dot(self.left[:, pl.ds(i * 256, 256)], self.right[...])
-        for n in range(2):
-            a, b = got[n * 128:n * 128 + 64], got[n * 128 + 64:n * 128 + 128]
-            self.mine[2 * i + n] = jnp.where(low, a, b)
-            self.sent[2 * i + n] = jnp.where(low, b, a).astype(bf16)
-        self.copy(i).start()
-
-    def fold(self, i):
-        self.copy(i).wait_recv()
-        w = pl.ds(2 * i, 2)
+        cols = pl.ds(pl.multiple_of(i * 256, 256), 256)
+        got = rows_dot(self.left[:, cols], self.right[...])
+        for m in range(2):
+            a, b = got[m * 128:m * 128 + 64], got[m * 128 + 64:m * 128 + 128]
+            self.mine[2 * i + m] = jnp.where(low, a, b)
+            self.sent[2 * i + m] = jnp.where(low, b, a).astype(bf16)
+        self.copy(n).start()
+
+    def fold(self, n):
+        self.copy(n).wait_recv()
+        w = pl.ds(2 * self.at(n), 2)
         self.half[w] = (self.mine[w] + self.got[w].astype(f32)).astype(bf16)
+        if self.back is not None:
+            self.back.begin(2 * n)
+            self.back.begin(2 * n + 1)
 
     def products(self):
         return [functools.partial(self.compute, i) for i in range(self.steps)]
@@ -988,14 +1016,13 @@
     gather.start()
 
     def use(j):
-        if j == 1:
+        if j == 0:
             columns.finish()
-        for i in {0: (), 1: (0, 1), 2: (2,), 3: (3,)}[j]:
-            tok = pl.ds(pl.multiple_of(s.arrival(i) * 512, 512), 512)
-            out = jnp.dot(normed_all[tok, :], in_cols[...], preferred_element_type=f32)
-            projected[tok, :] = out.astype(bf16)
-
-    merged(gather.tasks(use), nothing(2) + columns.tasks() + nothing(22))
+        tok = pl.ds(pl.multiple_of(s.arrival(j) * 512, 512), 512)
+        out = jnp.dot(normed_all[tok, :], in_cols[...], preferred_element_type=f32)
+        projected[tok, :] = out.astype(bf16)
+
+    merged(gather.tasks(use), nothing(2) + columns.tasks() + nothing(8))
     gather.drain()
     columns.drain()
     for k in range(1, 16):
@@ -1157,10 +1184,10 @@
         return [(n, i) for n in range(self.segments) for i in range(SEG // ROWS)]
 
 
-def attend_kernel(qkv, keep, mix, out_w, cot, gate_up, down,
+def attend_kernel(qkv, keep, mix, out_w, cot, gate_up,
                   local, mem_out, lse, combined, memory, normal, mixed_tokens, out_all, cot_all,
-                  gate_up_cols, down_cols, copies, t_s, t_r, *rest):
-    sems_o, sems_c, sems_g, sems_d = halves_of(rest, [11, 7, 5, 5])
+                  gate_up_cols, copies, t_s, t_r, *rest):
+    sems_o, sems_c, sems_g = halves_of(rest, [11, 7, 5])
     s = Spot()
     mine = pl.ds(pl.multiple_of(s.me * 128, 128), 128)
     own = [
@@ -1173,11 +1200,9 @@
     gather_o = SharedGather(s, out_w, out_all, sems_o)
     gather_c = Gather(s, cot, cot_all, sems_c)
     columns_g = Columns(s, gate_up, gate_up_cols, 2, sems_g)
-    columns_d = Columns(s, down, down_cols, 1, sems_d)
     gather_o.start()
     gather_c.start()
-    columns_g.start()
-    columns_d.start()
+    columns_g.start(4)
     attend = Attend(qkv, keep, mix, local, mem_out, lse, combined, memory, normal)
 
     def token_copy(j):
@@ -1194,14 +1219,13 @@
 
     compute = [attend.states] + [functools.partial(block, n, i) for n, i in attend.blocks()]
     merged(
-        gather_o.tasks() + nothing(4),
+        gather_o.tasks(),
         gather_c.tasks(),
+        columns_g.tasks(),
         compute + nothing(len(compute)),
-        nothing(2) + columns_g.tasks() + columns_d.tasks(),
     )
     mixed_tokens[:, pl.ds(pl.multiple_of(s.me * DH, DH), DH)] = combined[mine, :]
     columns_g.finish()
-    columns_d.finish()
     for k in range(1, 16):
         src = (s.me + 16 - k) % 16
         b = mixed_tokens.at[:, pl.ds(pl.multiple_of(src * DH, DH), DH)]
@@ -1211,44 +1235,46 @@
     gather_o.drain()
     gather_c.drain()
     columns_g.drain()
-    columns_d.drain()
     for cp in own:
         cp.wait()
 
 
-def attend_forward(qkv, keep, mix, out_weight, cotangent, gate_up, down, number):
+def attend_forward(qkv, keep, mix, out_weight, cotangent, gate_up, number):
     tokens, width = cotangent.shape
     total = qkv.shape[0]
     segments = total // SEG
     shape = jax.ShapeDtypeStruct
     return communicate(
-        attend_kernel, "attend", number, (qkv, keep, mix, out_weight, cotangent, gate_up, down),
-        [vmem()] * 3 + [anywhere()] * 4,
+        attend_kernel, "attend", number, (qkv, keep, mix, out_weight, cotangent, gate_up),
+        [vmem()] * 3 + [anywhere()] * 3,
         [
             shape((total, DH), f32), shape((total, DH), f32), shape((total, DH), f32),
             shape((total, DH), bf16), shape((segments, DH, DH), f32), shape((segments, 8, DH), f32),
             shape((tokens, width), bf16),
             shape((total, width), bf16), shape((total, width), bf16),
-            shape((width, gate_up.shape[1] // 16), bf16), shape((width, down.shape[1] // 16), bf16),
+            shape((width, gate_up.shape[1] // 16), bf16),
         ],
-        [vmem()] * 7 + [anywhere()] * 4,
-        [dma((2,)), dma((16,)), dma((16,))] + SharedGather.sems() + Gather.sems() + Columns.sems(2) + Columns.sems(1),
-    )
-
-
-def feed_kernel(combined, x, gains_all, out_all, cot_all, gate_up_cols, down_cols,
-                middle, hidden_all, act, feed_grad, out_v, cot_v, gate_up_v, down_v, hidden, copies,
-                *sems):
+        [vmem()] * 7 + [anywhere()] * 3,
+        [dma((2,)), dma((16,)), dma((16,))] + SharedGather.sems() + Gather.sems() + Columns.sems(2),
+    )
+
+
+def feed_kernel(combined, x, gains_all, out_all, cot_all, gate_up_cols, down,
+                middle, hidden_all, act, feed_grad, down_v, out_v, cot_v, gate_up_v, hidden, copies,
+                *rest):
+    sems, sems_d = halves_of(rest, [7, 5])
     s = Spot()
     loads = [
         pltpu.make_async_copy(a, b, copies.at[i])
         for i, (a, b) in enumerate(
-            [(out_all, out_v), (gate_up_cols, gate_up_v), (cot_all, cot_v), (down_cols, down_v)]
+            [(out_all, out_v), (gate_up_cols, gate_up_v), (cot_all, cot_v)]
         )
     ]
     for cp in loads:
         cp.start()
-    greet(s, plane=False, other=False)
+    greet(s)
+    columns = Columns(s, down, down_v, 1, sems_d)
+    columns.start()
     loads[0].wait()
     width = x.shape[1]
     squares = jnp.zeros((x.shape[0], 1), f32)
@@ -1273,6 +1299,7 @@
         if j == 0:
             for cp in loads[1:]:
                 cp.wait()
+            columns.finish()
         tok = pl.ds(pl.multiple_of(s.arrival(j) * 512, 512), 512)
         act_grad = jnp.dot(cot_v[tok, :], down_v[...], preferred_element_type=f32)
         gate = jnp.dot(hidden_all[tok, :], gate_up_v[:, :half], preferred_element_type=f32)
@@ -1284,102 +1311,164 @@
         feed_grad[tok, :half] = (act_grad * up * slope).astype(bf16)
         feed_grad[tok, half:] = (act_grad * silu).astype(bf16)
 
-    merged(gather.tasks(use))
+    merged(gather.tasks(use), columns.tasks() + nothing(8))
     gather.drain()
-
-
-def feed(combined, x, gains_all, out_all, cot_all, gate_up_cols, down_cols, number):
+    columns.drain()
+
+
+def feed(combined, x, gains_all, out_all, cot_all, gate_up_cols, down, number):
     tokens, width = x.shape
     total = cot_all.shape[0]
-    half = down_cols.shape[1]
+    half = down.shape[1] // 16
     shape = jax.ShapeDtypeStruct
     return communicate(
         feed_kernel, "feed", number,
-        (combined, x, gains_all, out_all, cot_all, gate_up_cols, down_cols),
+        (combined, x, gains_all, out_all, cot_all, gate_up_cols, down),
         [vmem()] * 3 + [anywhere()] * 4,
         [
             shape((tokens, width), f32), shape((total, width), bf16),
-            shape((total, half), bf16), shape((total, 2 * half), bf16),
+            shape((total, half), bf16), shape((total, 2 * half), bf16), shape((width, half), bf16),
         ],
-        [vmem()] * 4,
+        [vmem()] * 5,
         [
             VM(out_all.shape, bf16), VM(cot_all.shape, bf16), VM(gate_up_cols.shape, bf16),
-            VM(down_cols.shape, bf16), VM((tokens, width), bf16), dma((4,)),
-        ] + Gather.sems(),
-    )
-
-
-def hidden_grad_kernel(feed_grad, gate_up_cols, hidden_all, out, half, *rest):
+            VM((tokens, width), bf16), dma((3,)),
+        ] + Gather.sems() + Columns.sems(1),
+    )
+
+
+def hidden_grad_kernel(feed_grad, gate_up_cols, hidden_all, act, down_cols, out, half, feed_out, *rest):
+    sems_w, scratch, scratch_f = halves_of(rest, [5, 11, 11])
     s = Spot()
     greet(s, plane=False)
-    weigh = Weigh(s, hidden_all, feed_grad, half, rest[:5])
-    scatter = Scatter(s, feed_grad, gate_up_cols, out, rest[5:])
-    products = weigh.products()
+    weigh = Weigh(s, hidden_all, feed_grad, half, sems_w)
+    scatter = Scatter(s, feed_grad, gate_up_cols, out, scratch)
+    filler = Scatter(s, act, down_cols, feed_out, scratch_f, FILL[0][0])
     merged(
         scatter.tasks(),
-        products + nothing(16),
+        weigh.products() + nothing(16),
+        nothing(2) + filler.tasks(),
         nothing(20) + weigh.folds(),
     )
     scatter.finish()
+    filler.finish()
     weigh.drain()
 
 
-def hidden_grad_of(feed_grad, gate_up_cols, hidden_all, number):
+def hidden_grad_of(feed_grad, gate_up_cols, hidden_all, act, down_cols, number):
     shape = jax.ShapeDtypeStruct
     total, cols = feed_grad.shape
     width = gate_up_cols.shape[0]
+    fill = FILL[0][1]
     return communicate(
-        hidden_grad_kernel, "hidden_grad", number, (feed_grad, gate_up_cols, hidden_all),
-        [vmem()] * 3, [shape((total // 16, width), f32), shape((16, 64, cols), bf16)], [vmem()] * 2,
-        Weigh.scratch(cols) + Scatter.scratch(width),
-    )
-
-
-def normed_grad_kernel(grad, in_cols, normed_all, down_half, gate_up_rows,
-                       out, half, down_rows, gate_up_other, x_s, x_r, *rest):
-    sems_d, sems_w, scratch = halves_of(rest, [5, 5, 11])
+        hidden_grad_kernel, "hidden_grad", number,
+        (feed_grad, gate_up_cols, hidden_all, act, down_cols), [vmem()] * 5,
+        [
+            shape((total // 16, width), f32), shape((16, 64, cols), bf16),
+            shape((total // 16, fill), f32),
+        ],
+        [vmem()] * 3, Weigh.scratch(cols) + Scatter.scratch(width) + Scatter.scratch(fill),
+    )
+
+
+def normed_grad_kernel(grad, in_cols, normed_all, x, gain, act, down_cols, gains, down_half, out_rows,
+                       value_grad, gains_out, feed_out, down_rows, down_other, in_mine, in_other,
+                       out_other, normed_grad, half, gains_v, got, total, theirs, x_s, x_r, g_s, g_r,
+                       *rest):
+    sems_d, sems_i, sems_w, scratch, scratch_f = halves_of(rest, [5, 5, 5, 11, 11])
     s = Spot()
     greet(s)
-    weigh = Weigh(s, normed_all, grad, half, sems_w)
-    back = Return(s, down_half, down_rows, 1, sems_d)
-    scatter = Scatter(s, grad, in_cols, out, scratch)
-    over = send_over(gate_up_rows, gate_up_other, x_s.at[0], x_r.at[0], s)
-    back.start()
+    back_i = Return(s, half, in_mine, 3, sems_i, other=in_other)
+    weigh = Weigh(s, normed_all, grad, half, sems_w, back=back_i)
+    back_d = Return(s, down_half, down_rows, 1, sems_d, other=down_other)
+    scatter = Scatter(s, grad, in_cols, normed_grad, scratch)
+    filler = Scatter(s, act, down_cols, feed_out, scratch_f, FILL[2][0])
+    over = send_over(out_rows, out_other, x_s.at[0], x_r.at[0], s)
+    back_d.start()
+
+    def gain_copy(k):
+        to = s.partner(k)
+        return send(gains_v.at[to], got.at[s.me], g_s.at[k], g_r.at[s.me], to)
+
+    def epilogue():
+        width = x.shape[1]
+        values = x[...].astype(f32)
+        factor = lax.rsqrt(jnp.mean(values * values, axis=-1, keepdims=True) + epsilon)
+        row = jnp.sum(normed_grad[...] * gain[0:1, :] * values, axis=-1, keepdims=True)
+        row = row * (1.0 / width) * factor * factor * factor
+        for j in range(16):
+            w = pl.ds(j * 128, 128)
+            v = x[:, w].astype(f32)
+            u = normed_grad[:, w]
+            value_grad[:, w] = factor * (u * gain[0:1, w]) - v * row
+            gains_v[j] = gains[j]
+            gains_v[j, 0:1, :] = jnp.sum(u * v * factor, axis=0, keepdims=True)
+
     merged(
         scatter.tasks(),
-        weigh.products() + [over.start] + nothing(20),
-        nothing(20) + weigh.folds(),
+        weigh.products() + nothing(24),
+        nothing(3) + weigh.folds() + nothing(12),
+        nothing(10) + [over.start] + back_d.tasks() + nothing(5),
+        nothing(2) + filler.tasks(),
+        nothing(16) + back_i.tasks(),
     )
     scatter.finish()
-    for task in back.tasks():
-        task()
-    back.finish()
+    epilogue()
+    for k in range(1, 16):
+        gain_copy(k).start()
+    filler.finish()
+    back_d.finish()
+    back_i.finish()
     weigh.drain()
     over.wait()
-
-
-def normed_grad_of(grad, in_cols, normed_all, down_half, gate_up_rows, number):
+    for k in range(1, 16):
+        src = s.partner(k)
+        b = got.at[src]
+        send(b, b, g_s.at[k], g_r.at[src], s.me).wait_recv()
+    got[s.me] = gains_v[s.me]
+    acc = got[0]
+    for k in range(1, 16):
+        acc = acc + got[k]
+    total[...] = acc
+    cp = send_over(total, theirs, x_s.at[1], x_r.at[1], s)
+    cp.start()
+    for k in range(1, 16):
+        gain_copy(k).wait_send()
+    cp.wait()
+    gains_out[...] = total[...] + theirs[...]
+
+
+def normed_grad_of(grad, in_cols, normed_all, x, gain, act, down_cols, gains, down_half, out_rows, number):
     shape = jax.ShapeDtypeStruct
     total, cols = grad.shape
-    width = in_cols.shape[0]
+    tokens, width = x.shape
+    fill = FILL[2][1]
+    down_rows = shape((64, 16 * down_half.shape[2]), bf16)
+    in_rows = shape((64, 16 * cols), bf16)
     return communicate(
         normed_grad_kernel, "normed_grad", number,
-        (grad, in_cols, normed_all, down_half, gate_up_rows), [vmem()] * 3 + [anywhere()] * 2,
+        (grad, in_cols, normed_all, x, gain, act, down_cols, gains, down_half, out_rows),
+        [vmem()] * 8 + [anywhere()] * 2,
         [
-            shape((total // 16, width), f32), shape((16, 64, cols), bf16),
-            shape((64, 16 * down_half.shape[2]), bf16), shape(gate_up_rows.shape, bf16),
+            shape((tokens, width), f32), shape((8, 128), f32), shape((tokens, fill), f32),
+            down_rows, down_rows, in_rows, in_rows, shape(out_rows.shape, bf16),
         ],
-        [vmem()] * 2 + [anywhere()] * 2,
-        [dma((1,)), dma((1,))] + Return.sems(1) + Weigh.scratch(cols) + Scatter.scratch(width),
+        [vmem()] * 3 + [anywhere()] * 5,
+        [
+            VM((tokens, width), f32), VM((16, 64, cols), bf16), VM((16, 8, 128), f32),
+            VM((16, 8, 128), f32), VM((8, 128), f32), VM((8, 128), f32),
+            dma((2,)), dma((2,)), dma((16,)), dma((16,)),
+        ] + Return.sems(1) + Return.sems(3) + Weigh.scratch(cols) + Scatter.scratch(width)
+        + Scatter.scratch(fill),
     )
 
 
 def attend_back_kernel(attended, out_all, qkv, keep, mix, local, mem_out, lse, memory, normal,
-                       gate_up_half, cot_all, act,
-                       attended_all, grad, mix_grad, gate_up_rows, down_half,
+                       gate_up_half, cot_all, act, down_cols,
+                       attended_all, grad, mix_grad, gate_up_rows, gate_up_other, down_half, feed_out,
                        out_v, cot_v, by_token, upstream, dk, dv, state_grad, norm_grad, copies, h_s, h_r,
                        *rest):
-    sems_a, sems_g, sems_w = halves_of(rest, [7, 5, 5])
+    sems_a, sems_g, sems_w, scratch_f = halves_of(rest, [7, 5, 5, 11])
     s = Spot()
     mine = pl.ds(pl.multiple_of(s.me * 128, 128), 128)
     cot_load = pltpu.make_async_copy(cot_all, cot_v, copies.at[2])
@@ -1390,11 +1479,13 @@
     cot_load.start()
     greet(s)
     gather = Gather(s, attended, attended_all, sems_a)
-    back_g = Return(s, gate_up_half, gate_up_rows, 2, sems_g)
+    back_g = Return(s, gate_up_half, gate_up_rows, 2, sems_g, other=gate_up_other)
+    filler = Scatter(s, act, down_cols, feed_out, scratch_f, FILL[1][0])
     weigh = Weigh(s, cot_v, act, down_half, sems_w)
     attend = AttendBack(qkv, keep, mix, local, mem_out, lse, memory, normal, upstream, grad,
                         mix_grad, dk, dv, state_grad, norm_grad)
     attend.clear()
+    gather.start()
     load.wait()
 
     def head_copy(j):
@@ -1406,9 +1497,8 @@
         for h in range(4 * j, 4 * j + 4):
             pl.when(s.me != h)(lambda: head_copy(h).start())
     upstream[mine, :] = by_token[:, pl.ds(pl.multiple_of(s.me * DH, DH), DH)]
-    gather.start()
-    back_g.start()
     cot_load.wait()
+    filler.lag = 8
 
     def arrive(j):
         b = upstream.at[pl.ds(j * 128, 128)]
@@ -1420,12 +1510,10 @@
         attend.block(n, i)
 
     compute = [functools.partial(block, n, i) for n, i in attend.blocks()] + [attend.states]
-    merged(
-        gather.tasks(),
-        nothing(2) + compute,
-        weigh.products() + weigh.folds(),
-        nothing(10) + back_g.tasks(),
-    )
+    merged(gather.tasks(), nothing(2) + compute, weigh.products() + nothing(12))
+    back_g.start()
+    merged(filler.tasks(), back_g.tasks(), weigh.folds())
+    filler.finish()
     back_g.finish()
     weigh.drain()
     for j in range(16):
@@ -1434,90 +1522,30 @@
     own.wait()
 
 
-def attend_backward(attended, out_all, qkv, keep, mix, saved, gate_up_half, cot_all, act, number):
+def attend_backward(attended, out_all, qkv, keep, mix, saved, gate_up_half, cot_all, act, down_cols,
+                    number):
     tokens, width = attended.shape
     total = qkv.shape[0]
     segments = total // SEG
     shape = jax.ShapeDtypeStruct
     local, mem_out, lse, memory, normal = saved
+    rows = shape((64, 16 * gate_up_half.shape[2]), bf16)
     return communicate(
         attend_back_kernel, "attend_back", number,
         (attended, out_all, qkv, keep, mix, local, mem_out, lse, memory, normal,
-         gate_up_half, cot_all, act),
-        [vmem(), anywhere()] + [vmem()] * 8 + [anywhere()] * 2 + [vmem()],
+         gate_up_half, cot_all, act, down_cols),
+        [vmem(), anywhere()] + [vmem()] * 8 + [anywhere()] * 2 + [vmem()] * 2,
         [
             shape((total, width), bf16), shape((total, 3 * DH), bf16), shape((8, DH), f32),
-            shape((64, 16 * gate_up_half.shape[2]), bf16), shape((16, 64, act.shape[1]), bf16),
+            rows, rows, shape((16, 64, act.shape[1]), bf16), shape((tokens, FILL[1][1]), f32),
         ],
-        [anywhere(), vmem(), vmem(), anywhere(), vmem()],
+        [anywhere(), vmem(), vmem(), anywhere(), anywhere(), vmem(), vmem()],
         [
             VM(out_all.shape, bf16), VM(cot_all.shape, bf16), VM((tokens, width), bf16),
             VM((total, DH), bf16),
             VM((total, DH), f32), VM((total, DH), f32), VM((segments, DH, DH), f32),
             VM((segments, 8, DH), f32), dma((3,)), dma((16,)), dma((16,)),
-        ] + Gather.sems() + Return.sems(2) + Weigh.scratch(act.shape[1]),
-    )
-
-
-def last_kernel(act, down_cols, in_half, down_rows, out_rows, gains,
-                feed_out, in_mine, in_other, down_other, out_other, gains_out,
-                got, total, theirs, x_s, x_r, g_s, g_r, *rest):
-    sems_i, scratch = rest[:5], rest[5:]
-    s = Spot()
-    greet(s)
-
-    def gain_copy(k):
-        to = (s.me + k) % 16
-        return send(gains.at[to], got.at[s.me], g_s.at[k], g_r.at[s.me], to)
-
-    back = Return(s, in_half, in_mine, 3, sems_i, other=in_other)
-    back.start()
-    for k in range(1, 16):
-        gain_copy(k).start()
-    pairs = [(down_rows, down_other), (out_rows, out_other)]
-    overs = [send_over(a, b, x_s.at[i], x_r.at[i], s) for i, (a, b) in enumerate(pairs)]
-    scatter = Scatter(s, act, down_cols, feed_out, scratch)
-    for cp in overs:
-        cp.start()
-
-    def sum_gains():
-        for k in range(1, 16):
-            src = (s.me + 16 - k) % 16
-            b = got.at[src]
-            send(b, b, g_s.at[k], g_r.at[src], s.me).wait_recv()
-        got[s.me] = gains[s.me]
-        acc = got[0]
-        for k in range(1, 16):
-            acc = acc + got[k]
-        total[...] = acc
-        send_over(total, theirs, x_s.at[3], x_r.at[3], s).start()
-
-    merged(scatter.tasks(), [lambda: None] * 3 + back.tasks() + [sum_gains])
-    scatter.finish()
-    back.finish()
-    cp = send_over(total, theirs, x_s.at[3], x_r.at[3], s)
-    cp.wait()
-    gains_out[...] = total[...] + theirs[...]
-    for cp in overs:
-        cp.wait()
-    for k in range(1, 16):
-        gain_copy(k).wait_send()
-
-
-def last(act, down_cols, in_half, down_rows, out_rows, gains, number):
-    shape = jax.ShapeDtypeStruct
-    total = act.shape[0]
-    width = down_cols.shape[0]
-    in_rows = shape((64, 16 * in_half.shape[2]), bf16)
-    like = [shape(a.shape, a.dtype) for a in (down_rows, out_rows)]
-    return communicate(
-        last_kernel, "last", number,
-        (act, down_cols, in_half, down_rows, out_rows, gains),
-        [vmem()] * 2 + [anywhere()] * 3 + [vmem()],
-        [shape((total // 16, width), f32), in_rows, in_rows] + like + [shape((8, 128), f32)],
-        [vmem()] + [anywhere()] * 4 + [vmem()],
-        [VM((16, 8, 128), f32), VM((8, 128), f32), VM((8, 128), f32),
-         dma((4,)), dma((4,)), dma((16,)), dma((16,))] + Return.sems(3) + Scatter.scratch(width),
+        ] + Gather.sems() + Return.sems(2) + Weigh.scratch(act.shape[1]) + Scatter.scratch(FILL[1][1]),
     )
 
 
@@ -1547,12 +1575,14 @@
 
     normed_all, in_cols, gains_all, qkv = project(layer_input, own_gains, in_weight, 0)
     (local, mem_out, lse, combined, memory, normal, mixed_tokens, out_all, cot_all, gate_up_cols,
-     down_cols) = attend_forward(qkv, keep, mix, out_weight, cotangent, gate_up, down_weight, 1)
-    middle, hidden_all, act, feed_grad = feed(
-        mixed_tokens, layer_input, gains_all, out_all, cot_all, gate_up_cols, down_cols, 2
-    )
-
-    hidden_grad, gate_up_half = hidden_grad_of(feed_grad, gate_up_cols, hidden_all, 3)
+     ) = attend_forward(qkv, keep, mix, out_weight, cotangent, gate_up, 1)
+    middle, hidden_all, act, feed_grad, down_cols = feed(
+        mixed_tokens, layer_input, gains_all, out_all, cot_all, gate_up_cols, down_weight, 2
+    )
+
+    hidden_grad, gate_up_half, feed_out_0 = hidden_grad_of(
+        feed_grad, gate_up_cols, hidden_all, act, down_cols, 3
+    )
 
     first_all = gains_all[:, 0].reshape(width)
     second_all = gains_all[:, 1].reshape(width)
@@ -1560,27 +1590,22 @@
     second_factor = lax.rsqrt(jnp.mean(middle * middle, axis=-1, keepdims=True) + epsilon)
     middle_norm_grad, second_local = norm_backward(middle, second_factor, second_all, hidden_grad)
     middle_grad = upstream + middle_norm_grad
-    attended_all, projected_grad, mix_grad, gate_up_rows, down_half = attend_backward(
+    (attended_all, projected_grad, mix_grad, gate_up_rows, gate_up_other, down_half,
+     feed_out_1) = attend_backward(
         middle_grad.astype(bf16), out_all, qkv, keep, mix, (local, mem_out, lse, memory, normal),
-        gate_up_half, cot_all, act, 4,
+        gate_up_half, cot_all, act, down_cols, 4,
     )
     out_rows = rows_dot(combined, attended_all).astype(bf16)
-    normed_grad, in_half, down_rows, gate_up_other = normed_grad_of(
-        projected_grad, in_cols, normed_all, down_half, gate_up_rows, 5
-    )
-    inputs = layer_input.astype(f32)
-    first_factor = lax.rsqrt(jnp.mean(inputs * inputs, axis=-1, keepdims=True) + epsilon)
-    input_norm_grad, first_local = norm_backward(inputs, first_factor, first_all, normed_grad)
-    input_grad = middle_grad + input_norm_grad
-
     mix_rows = jnp.where((jnp.arange(H) == lax.axis_index(AXIS))[:, None], mix_grad[0:1], 0.0)
-    gain_grads = jnp.stack(
-        [first_local.reshape(16, 128), second_local.reshape(16, 128), mix_rows], axis=1
-    )
+    gain_grads = jnp.stack([mix_rows, second_local.reshape(16, 128), mix_rows], axis=1)
     gain_grads = jnp.pad(gain_grads, ((0, 0), (0, 5), (0, 0)))
-    feed_out, in_mine_rows, in_other_rows, down_other, out_other, gains_out = last(
-        act, down_cols, in_half, down_rows, out_rows, gain_grads, 6
-    )
+    (value_grad, gains_out, feed_out_2, down_rows, down_other, in_mine_rows, in_other_rows,
+     out_other) = normed_grad_of(
+        projected_grad, in_cols, normed_all, layer_input, jnp.broadcast_to(first_all[None], (8, width)),
+        act, down_cols, gain_grads, down_half, out_rows, 5,
+    )
+    input_grad = middle_grad + value_grad
+    feed_out = jnp.concatenate([feed_out_0, feed_out_1, feed_out_2], axis=1)
     layer_output = (middle + feed_out).astype(bf16)
 
     def both_halves(mine, other):

time: 683 us -> 632 us (0.925)
  Pallas kernels: 638 us -> 590 us
    pallas_call x7 -> x6, Pallas kernels: 638 us -> 590 us  [communicate(): pl.pallas_call(kernel, out_shape=outs, in_specs=in_specs, out_specs=out_s...]
where the time goes in v4:
time: 632 us; the launch traced here: 623 us
  Pallas kernels  590 us (93%)
  other arithmetic  19.3 us (3%)
  local copies, waits for them, and re-layouts  6.92 us (1%)
    pallas_call x6, Pallas kernels, communicate(): pl.pallas_call(kernel, out_shape=outs, in_specs=in_specs, out_specs=out_s...  590 us

profile of v4, /device:TPU:0, one launch (start us, length us, event | category | flops | bytes accessed | tf_op | source)
XLA Modules:
  0.0 622.9 jit_solution(9345701539861805817)
XLA Ops:
  0.6 0.7 pad_convert_fusion
  1.3 0.7 bitcast_convert_fusion
  2.0 0.6 copy-done.13
  2.6 74.3 %project.1 = (bf16[2048,2048]{1,0:T(8,128)(2,1)}, bf16[2048,384]{1,0:T(8,128)(2,1)}, f32[16,8,128]{2,1,0:T(8,128)}, bf16[2048,384]{1,0:T(8,128)(2,1)}) custom-call(bf16[128,2048]{1,0:T(8,128)(2,1)} %x.9, f32[8,128]{1,0:T(8,128)} %copy-done.13, bf16[128,6144]{1,0:T(8,128)(2,1)} %in_w.1), custom_call_target="tpu_custom_call" | custom-call | bytes 16777216 | tf_op jit(solution)/shard_map/project/pallas_call | solution.py:979
  76.8 0.7 fusion.1
  77.5 0.7 broadcast_in_dim.53.keep
  78.2 0.7 add_divide_fusion
  78.8 0.6 broadcast_in_dim.54.mix
  79.4 118.8 %attend.1 = (f32[2048,128]{1,0:T(8,128)}, f32[2048,128]{1,0:T(8,128)}, f32[2048,128]{1,0:T(8,128)}, bf16[2048,128]{1,0:T(8,128)(2,1)}, f32[2,128,128]{2,1,0:T(8,...) custom-call(bf16[2048,384]{1,0:T(8,128)(2,1)} %get-tuple-element.70., ...), custom_call_target="tpu_custom_call" | custom-call | bytes 16777216 | tf_op jit(solution)/shard_map/attend/pallas_call | solution.py:979
  198.2 87.4 %feed.1 = (f32[128,2048]{1,0:T(8,128)}, bf16[2048,2048]{1,0:T(8,128)(2,1)}, bf16[2048,512]{1,0:T(8,128)(2,1)}, bf16[2048,1024]{1,0:T(8,128)(2,1)}, bf16[2048,512]{1,0:T(8,128)(2,1)}) custom-call(bf16[128,2048]{1,0:T(8,128)(2,1)} %get-tuple-element.71.combined, bf16[128,2048]{1,0:T(8,128)(2,1)} %x.9, f32[16,8,128]{2,1,0:T(8,128)} %get-tuple-element.72.gains_all, ...), custom_call_target="tpu_custom_call" | custom-call | bytes 16777216 | tf_op jit(solution)/shard_map/feed/pallas_call | solution.py:979
  285.6 0.0 copy-start
  285.6 79.9 %hidden_grad.1 = (f32[128,2048]{1,0:T(8,128)}, bf16[16,64,1024]{2,1,0:T(8,128)(2,1)}, f32[128,512]{1,0:T(8,128)}) custom-call(bf16[2048,1024]{1,0:T(8,128)(2,1)} %get-tuple-element.77.feed_grad, bf16[2048,1024]{1,0:T(8,128)(2,1)} %get-tuple-element.75.gate_up_cols, bf16[2048,2048]{1,0:T(8,128)(2,1)} %get-tuple-element.78.hidden_all, ...), custom_call_target="tpu_custom_call" | custom-call | bytes 16777216 | tf_op jit(solution)/shard_map/hidden_grad/pallas_call | solution.py:979
  365.5 0.0 copy-start.2
  365.5 0.0 copy-start.3
  365.5 0.0 copy-done
  365.5 0.2 multiply_reduce_fusion.2
  365.7 1.0 fusion.3
  366.7 1.5 multiply_reduce_fusion
  368.2 0.0 copy-done.2
  368.2 0.0 copy-done.3
  368.2 1.2 fusion.2
  369.4 125.8 %attend_back.1 = (bf16[2048,2048]{1,0:T(8,128)(2,1)}, bf16[2048,384]{1,0:T(8,128)(2,1)}, f32[8,128]{1,0:T(8,128)}, bf16[64,16384]{1,0:T(8,128)(2,1)}, bf16[64,16...) custom-call(bf16[128,2048]{1,0:T(8,128)(2,1)} %get-tuple-element.109.attended, ...), custom_call_target="tpu_custom_call" | custom-call | bytes 16777216 | tf_op jit(solution)/shard_map/attend_back/pallas_call | solution.py:979
  495.2 0.6 broadcast_in_dim.56.gain
  495.9 0.7 slice_bitcast_fusion.3
  496.6 0.1 broadcast_select_fusion.6
  496.6 0.7 select_maximum_fusion.gains
  497.3 0.0 copy-done.6
  497.3 5.5 convolution_convert_fusion.out_rows
  502.8 103.8 %normed_grad.1 = (f32[128,2048]{1,0:T(8,128)}, f32[8,128]{1,0:T(8,128)}, f32[128,512]{1,0:T(8,128)}, bf16[64,8192]{1,0:T(8,128)(2,1)}, bf16[64,8192]{1,0:T(8,128...) custom-call(bf16[2048,384]{1,0:T(8,128)(2,1)} %get-tuple-element.90.grad, ...), custom_call_target="tpu_custom_call" | custom-call | bytes 16777216 | tf_op jit(solution)/shard_map/normed_grad/pallas_call | solution.py:979
  606.6 0.0 copy-start.9
  606.6 0.0 copy-done.1
  606.6 0.0 copy-done.12
  606.6 0.0 copy-start.10
  606.6 2.7 fusion
  609.4 0.0 copy-done.9
  609.4 1.1 add.42
  610.5 1.3 slice_bitcast_fusion
  611.8 0.0 copy-done.10
  611.8 0.0 copy-done.11
  611.8 0.1 broadcast_select_fusion.5
  611.9 0.0 copy-start.4
  611.9 2.0 maximum_convert_fusion.2
  613.9 0.3 copy-done.4
  614.2 1.1 copy-done.5
  615.3 0.3 broadcast_select_fusion.1
  615.6 4.2 maximum_convert_fusion
  619.8 0.1 broadcast_select_fusion.3
  620.0 2.4 maximum_convert_fusion.1
  (14 shorter events, 0.1 us)
Async XLA Ops:
  2.0 0.6 copy-start.13
  285.6 79.9 %copy-start = (f32[128,2048]{1,0:T(8,128)S(1)}, f32[128,2048]{1,0:T(8,128)}, u32[]{:S(2)}) copy-start(f32[128,2048]{1,0:T(8,128)} %get-tuple-element.76) | copy-start | bytes 3145732
  365.5 2.7 copy-start.2
  365.5 2.7 copy-start.3
  369.4 127.9 %copy-start.6 = (bf16[2048,128]{1,0:T(8,128)(2,1)S(1)}, bf16[2048,128]{1,0:T(8,128)(2,1)}, u32[]{:S(2)}) copy-start(bf16[2048,128]{1,0:T(8,128)(2,1)} %get-tuple-element.95) | copy-start | bytes 1572868
  502.8 103.8 %copy-start.1 = (bf16[128,2048]{1,0:T(8,128)(2,1)S(1)}, bf16[128,2048]{1,0:T(8,128)(2,1)}, u32[]{:S(2)}) copy-start(bf16[128,2048]{1,0:T(8,128)(2,1)} %convolution_convert_fusion.out_rows) | copy-start | bytes 1572868
  502.8 103.8 %copy-start.12 = (f32[128,1024]{1,0:T(8,128)S(1)}, f32[128,1024]{1,0:T(8,128)}, u32[]{:S(2)}) copy-start(f32[128,1024]{1,0:T(8,128)} %get-tuple-element.89) | copy-start | bytes 1572868
  606.6 2.8 copy-start.9
  606.6 5.2 copy-start.10
  609.4 2.4 copy-start.11
  611.9 2.3 copy-start.4
  611.9 3.4 copy-start.5
  615.5 4.3 copy-start.7
  615.6 4.3 copy-start.8

commit v5 on v4

--- a/solution.py
+++ b/solution.py
@@ -604,15 +604,19 @@
                     out.append(functools.partial(self.x_arrive, j, yo))
         return out
 
+    def finish(self):
+        s = self.s
+        for ch in range(self.chunks):
+            for n in range(8):
+                b = self.other(ch, n // 2, n % 2, 1 - s.c)
+                send(b, b, self.ts.at[ch, n], self.tr.at[ch, n], s.me).wait_recv()
+
     def drain(self):
         s = self.s
         super().drain()
         for ch in range(self.chunks):
             for zo in range(4):
                 for yo in range(2):
-                    n = zo * 2 + yo
-                    b = self.other(ch, zo, yo, 1 - s.c)
-                    send(b, b, self.ts.at[ch, n], self.tr.at[ch, n], s.me).wait_recv()
                     self.tcopy(ch, zo, yo).wait_send()
                     far = (s.z != zo) | (s.y != yo)
                     pl.when(far)(lambda: self.xcopy(ch, zo, yo).wait_send())
@@ -986,40 +990,48 @@
     )(*ins)
 
 
-def project_kernel(x, gains, in_w, normed_all, in_cols, gains_all, projected, normed, *rest):
-    g_s, g_r = rest[:2]
-    gather_sems, col_sems = halves_of(rest[2:], [7, 5])
+def project_kernel(x, gains, in_w, normed_all, in_cols, gains_all, projected, x_all, normed, row,
+                   copies, g_s, g_r, *rest):
+    gather_sems, col_sems = halves_of(rest, [7, 5])
     s = Spot()
     greet(s)
 
     def gain_copy(k):
-        return send(gains, gains_all.at[s.me], g_s.at[k], g_r.at[s.me], (s.me + k) % 16)
-
+        return send(gains, gains_all.at[s.me], g_s.at[k], g_r.at[s.me], s.partner(k))
+
+    gather = Gather(s, x, x_all, gather_sems)
+    gather.start()
     for k in range(1, 16):
         gain_copy(k).start()
     columns = Columns(s, in_w, in_cols, 3, col_sems)
     columns.start()
     gains_all[s.me] = gains[...]
-    values = x[...].astype(f32)
-    factor = lax.rsqrt(jnp.mean(values * values, axis=-1, keepdims=True) + epsilon)
-    for k in range(1, 16):
-        src = (s.me + 16 - k) % 16
-        b = gains_all.at[src]
-        send(b, b, g_s.at[k], g_r.at[src], s.me).wait_recv()
-    mine = pl.ds(pl.multiple_of(s.me * 128, 128), 128)
-    for j in range(16):
-        w = pl.ds(j * 128, 128)
-        part = (x[:, w].astype(f32) * factor * gains_all[j, 0:1, :]).astype(bf16)
-        normed[:, w] = part
-        normed_all[mine, w] = part
-    gather = Gather(s, normed, normed_all, gather_sems)
-    gather.start()
+    x_all[pl.ds(pl.multiple_of(s.me * 128, 128), 128), :] = x[...]
+
+    def gain_row():
+        for k in range(1, 16):
+            src = s.partner(k)
+            b = gains_all.at[src]
+            send(b, b, g_s.at[k], g_r.at[src], s.me).wait_recv()
+        for j in range(16):
+            row[0:1, pl.ds(j * 128, 128)] = gains_all[j, 0:1, :]
+
+    def out_copy(j):
+        tok = pl.ds(pl.multiple_of(s.arrival(j) * 512, 512), 512)
+        return pltpu.make_async_copy(normed.at[tok], normed_all.at[tok], copies.at[j])
 
     def use(j):
         if j == 0:
             columns.finish()
+            gain_row()
+        for n in range(4):
+            rows = pl.ds(pl.multiple_of(s.arrival(j) * 512 + n * 128, 128), 128)
+            values = x_all[rows, :].astype(f32)
+            factor = lax.rsqrt(jnp.mean(values * values, axis=-1, keepdims=True) + epsilon)
+            normed[rows, :] = (values * factor * row[0:1, :]).astype(bf16)
+        out_copy(j).start()
         tok = pl.ds(pl.multiple_of(s.arrival(j) * 512, 512), 512)
-        out = jnp.dot(normed_all[tok, :], in_cols[...], preferred_element_type=f32)
+        out = jnp.dot(normed[tok, :], in_cols[...], preferred_element_type=f32)
         projected[tok, :] = out.astype(bf16)
 
     merged(gather.tasks(use), nothing(2) + columns.tasks() + nothing(8))
@@ -1027,6 +1039,8 @@
     columns.drain()
     for k in range(1, 16):
         gain_copy(k).wait_send()
+    for j in range(4):
+        out_copy(j).wait()
 
 
 def project(x, gains, in_weight, number):
@@ -1039,8 +1053,11 @@
             jax.ShapeDtypeStruct((16, 8, 128), f32),
             jax.ShapeDtypeStruct((16 * tokens, 3 * DH), bf16),
         ],
-        [vmem()] * 4,
-        [VM((tokens, width), bf16), dma((16,)), dma((16,))] + Gather.sems() + Columns.sems(3),
+        [anywhere(), vmem(), vmem(), vmem()],
+        [
+            VM((16 * tokens, width), bf16), VM((16 * tokens, width), bf16), VM((8, width), f32),
+            dma((4,)), dma((16,)), dma((16,)),
+        ] + Gather.sems() + Columns.sems(3),
     )
 
 
@@ -1184,9 +1201,9 @@
         return [(n, i) for n in range(self.segments) for i in range(SEG // ROWS)]
 
 
-def attend_kernel(qkv, keep, mix, out_w, cot, gate_up,
-                  local, mem_out, lse, combined, memory, normal, mixed_tokens, out_all, cot_all,
-                  gate_up_cols, copies, t_s, t_r, *rest):
+def attend_kernel(qkv, keep, mix, x, gains_all, out_w, cot, gate_up,
+                  local, mem_out, lse, combined, memory, normal, middle, hidden, out_all, cot_all,
+                  gate_up_cols, mixed_tokens, copies, t_s, t_r, *rest):
     sems_o, sems_c, sems_g = halves_of(rest, [11, 7, 5])
     s = Spot()
     mine = pl.ds(pl.multiple_of(s.me * 128, 128), 128)
@@ -1218,136 +1235,161 @@
             pl.when(s.me != j)(lambda: token_copy(j).start())
 
     compute = [attend.states] + [functools.partial(block, n, i) for n, i in attend.blocks()]
+
+    def tokens():
+        own[0].wait()
+        gather_o.finish()
+        mixed_tokens[:, pl.ds(pl.multiple_of(s.me * DH, DH), DH)] = combined[mine, :]
+        for k in range(1, 16):
+            src = s.partner(k)
+            b = mixed_tokens.at[:, pl.ds(pl.multiple_of(src * DH, DH), DH)]
+            send(b, b, t_s.at[0], t_r.at[src], s.me).wait_recv()
+
+    def output(j):
+        w = pl.ds(j * 512, 512)
+        got = jnp.dot(mixed_tokens[...], out_all[:, w], preferred_element_type=f32)
+        middle[:, w] = got + x[:, w].astype(f32)
+
+    def norm():
+        values = middle[...]
+        factor = lax.rsqrt(jnp.mean(values * values, axis=-1, keepdims=True) + epsilon)
+        for j in range(16):
+            w = pl.ds(j * 128, 128)
+            hidden[:, w] = (middle[:, w] * factor * gains_all[j, 1:2, :]).astype(bf16)
+
+    after = [tokens] + [functools.partial(output, j) for j in range(4)] + [norm]
     merged(
         gather_o.tasks(),
         gather_c.tasks(),
         columns_g.tasks(),
         compute + nothing(len(compute)),
     )
-    mixed_tokens[:, pl.ds(pl.multiple_of(s.me * DH, DH), DH)] = combined[mine, :]
+    merged(after)
     columns_g.finish()
-    for k in range(1, 16):
-        src = (s.me + 16 - k) % 16
-        b = mixed_tokens.at[:, pl.ds(pl.multiple_of(src * DH, DH), DH)]
-        send(b, b, t_s.at[0], t_r.at[src], s.me).wait_recv()
     for j in range(16):
         pl.when(s.me != j)(lambda: token_copy(j).wait_send())
     gather_o.drain()
     gather_c.drain()
     columns_g.drain()
-    for cp in own:
-        cp.wait()
-
-
-def attend_forward(qkv, keep, mix, out_weight, cotangent, gate_up, number):
+    own[1].wait()
+
+
+def attend_forward(qkv, keep, mix, x, gains_all, out_weight, cotangent, gate_up, number):
     tokens, width = cotangent.shape
     total = qkv.shape[0]
     segments = total // SEG
     shape = jax.ShapeDtypeStruct
     return communicate(
-        attend_kernel, "attend", number, (qkv, keep, mix, out_weight, cotangent, gate_up),
-        [vmem()] * 3 + [anywhere()] * 3,
+        attend_kernel, "attend", number,
+        (qkv, keep, mix, x, gains_all, out_weight, cotangent, gate_up), [vmem()] * 5 + [anywhere()] * 3,
         [
             shape((total, DH), f32), shape((total, DH), f32), shape((total, DH), f32),
             shape((total, DH), bf16), shape((segments, DH, DH), f32), shape((segments, 8, DH), f32),
-            shape((tokens, width), bf16),
+            shape((tokens, width), f32), shape((tokens, width), bf16),
             shape((total, width), bf16), shape((total, width), bf16),
             shape((width, gate_up.shape[1] // 16), bf16),
         ],
-        [vmem()] * 7 + [anywhere()] * 3,
-        [dma((2,)), dma((16,)), dma((16,))] + SharedGather.sems() + Gather.sems() + Columns.sems(2),
-    )
-
-
-def feed_kernel(combined, x, gains_all, out_all, cot_all, gate_up_cols, down,
-                middle, hidden_all, act, feed_grad, down_v, out_v, cot_v, gate_up_v, hidden, copies,
-                *rest):
+        [vmem()] * 9 + [anywhere()] * 2,
+        [VM((tokens, width), bf16), dma((2,)), dma((16,)), dma((16,))] + SharedGather.sems() + Gather.sems() + Columns.sems(2),
+    )
+
+
+def feed_kernel(hidden, cot_all, gate_up_cols, down,
+                hidden_all, act, feed_grad, down_cols,
+                hidden_v, act_v, grad_v, down_v, cot_v, gate_up_v, copies, outs, *rest):
     sems, sems_d = halves_of(rest, [7, 5])
     s = Spot()
     loads = [
         pltpu.make_async_copy(a, b, copies.at[i])
-        for i, (a, b) in enumerate(
-            [(out_all, out_v), (gate_up_cols, gate_up_v), (cot_all, cot_v)]
-        )
+        for i, (a, b) in enumerate([(gate_up_cols, gate_up_v), (cot_all, cot_v)])
     ]
     for cp in loads:
         cp.start()
     greet(s)
+    gather = Gather(s, hidden, hidden_v, sems)
+    gather.start()
     columns = Columns(s, down, down_v, 1, sems_d)
     columns.start()
-    loads[0].wait()
-    width = x.shape[1]
-    squares = jnp.zeros((x.shape[0], 1), f32)
-    for j in range(4):
-        w = pl.ds(j * 512, 512)
-        got = jnp.dot(combined[...], out_v[:, w], preferred_element_type=f32)
-        got = got + x[:, w].astype(f32)
-        middle[:, w] = got
-        squares = squares + jnp.sum(got * got, axis=-1, keepdims=True)
-    factor = lax.rsqrt(squares * (1.0 / width) + epsilon)
-    mine = pl.ds(pl.multiple_of(s.me * 128, 128), 128)
-    for j in range(16):
-        w = pl.ds(j * 128, 128)
-        part = (middle[:, w] * factor * gains_all[j, 1:2, :]).astype(bf16)
-        hidden[:, w] = part
-        hidden_all[mine, w] = part
-    gather = Gather(s, hidden, hidden_all, sems)
-    gather.start()
+    hidden_v[pl.ds(pl.multiple_of(s.me * 128, 128), 128), :] = hidden[...]
     half = act.shape[1]
+
+    def out_copies(j):
+        tok = pl.ds(pl.multiple_of(s.arrival(j) * 512, 512), 512)
+        pairs = [(hidden_v, hidden_all), (act_v, act), (grad_v, feed_grad)]
+        return [
+            pltpu.make_async_copy(a.at[tok], b.at[tok], outs.at[j, i]) for i, (a, b) in enumerate(pairs)
+        ]
+
+    out_down = pltpu.make_async_copy(down_v, down_cols, outs.at[4, 0])
 
     def use(j):
         if j == 0:
-            for cp in loads[1:]:
+            for cp in loads:
                 cp.wait()
             columns.finish()
+            out_down.start()
         tok = pl.ds(pl.multiple_of(s.arrival(j) * 512, 512), 512)
         act_grad = jnp.dot(cot_v[tok, :], down_v[...], preferred_element_type=f32)
-        gate = jnp.dot(hidden_all[tok, :], gate_up_v[:, :half], preferred_element_type=f32)
-        up = jnp.dot(hidden_all[tok, :], gate_up_v[:, half:], preferred_element_type=f32)
+        gate = jnp.dot(hidden_v[tok, :], gate_up_v[:, :half], preferred_element_type=f32)
+        up = jnp.dot(hidden_v[tok, :], gate_up_v[:, half:], preferred_element_type=f32)
         sigma = jax.nn.sigmoid(gate)
         silu = gate * sigma
-        act[tok, :] = (silu * up).astype(bf16)
+        act_v[tok, :] = (silu * up).astype(bf16)
         slope = sigma * (1.0 + gate * (1.0 - sigma))
-        feed_grad[tok, :half] = (act_grad * up * slope).astype(bf16)
-        feed_grad[tok, half:] = (act_grad * silu).astype(bf16)
-
-    merged(gather.tasks(use), columns.tasks() + nothing(8))
+        grad_v[tok, :half] = (act_grad * up * slope).astype(bf16)
+        grad_v[tok, half:] = (act_grad * silu).astype(bf16)
+        for cp in out_copies(j):
+            cp.start()
+
+    merged(gather.tasks(use), nothing(2) + columns.tasks() + nothing(8))
     gather.drain()
     columns.drain()
-
-
-def feed(combined, x, gains_all, out_all, cot_all, gate_up_cols, down, number):
-    tokens, width = x.shape
-    total = cot_all.shape[0]
+    out_down.wait()
+    for j in range(4):
+        for cp in out_copies(j):
+            cp.wait()
+
+
+def feed(hidden, cot_all, gate_up_cols, down, number):
+    total, width = cot_all.shape
     half = down.shape[1] // 16
     shape = jax.ShapeDtypeStruct
     return communicate(
-        feed_kernel, "feed", number,
-        (combined, x, gains_all, out_all, cot_all, gate_up_cols, down),
-        [vmem()] * 3 + [anywhere()] * 4,
+        feed_kernel, "feed", number, (hidden, cot_all, gate_up_cols, down),
+        [vmem()] + [anywhere()] * 3,
         [
-            shape((tokens, width), f32), shape((total, width), bf16),
-            shape((total, half), bf16), shape((total, 2 * half), bf16), shape((width, half), bf16),
+            shape((total, width), bf16), shape((total, half), bf16), shape((total, 2 * half), bf16),
+            shape((width, half), bf16),
         ],
-        [vmem()] * 5,
+        [anywhere()] * 4,
         [
-            VM(out_all.shape, bf16), VM(cot_all.shape, bf16), VM(gate_up_cols.shape, bf16),
-            VM((tokens, width), bf16), dma((3,)),
+            VM((total, width), bf16), VM((total, half), bf16), VM((total, 2 * half), bf16),
+            VM((width, half), bf16), VM((total, width), bf16), VM(gate_up_cols.shape, bf16),
+            dma((2,)), dma((5, 3)),
         ] + Gather.sems() + Columns.sems(1),
     )
 
 
-def hidden_grad_kernel(feed_grad, gate_up_cols, hidden_all, act, down_cols, out, half, feed_out, *rest):
+def loaded(pairs, sems):
+    copies = [pltpu.make_async_copy(a, b, sems.at[i]) for i, (a, b) in enumerate(pairs)]
+    for cp in copies:
+        cp.start()
+    return [cp.wait for cp in copies]
+
+
+def hidden_grad_kernel(feed_grad, gate_up_cols, hidden_all, act, down_cols, out, half, feed_out,
+                       hidden_v, act_v, down_v, copies, *rest):
     sems_w, scratch, scratch_f = halves_of(rest, [5, 11, 11])
     s = Spot()
+    loads = loaded([(hidden_all, hidden_v), (act, act_v), (down_cols, down_v)], copies)
     greet(s, plane=False)
-    weigh = Weigh(s, hidden_all, feed_grad, half, sems_w)
+    weigh = Weigh(s, hidden_v, feed_grad, half, sems_w)
     scatter = Scatter(s, feed_grad, gate_up_cols, out, scratch)
-    filler = Scatter(s, act, down_cols, feed_out, scratch_f, FILL[0][0])
+    filler = Scatter(s, act_v, down_v, feed_out, scratch_f, FILL[0][0])
     merged(
         scatter.tasks(),
-        weigh.products() + nothing(16),
-        nothing(2) + filler.tasks(),
+        loads + weigh.products() + nothing(16),
+        nothing(4) + filler.tasks(),
         nothing(20) + weigh.folds(),
     )
     scatter.finish()
@@ -1362,27 +1404,31 @@
     fill = FILL[0][1]
     return communicate(
         hidden_grad_kernel, "hidden_grad", number,
-        (feed_grad, gate_up_cols, hidden_all, act, down_cols), [vmem()] * 5,
+        (feed_grad, gate_up_cols, hidden_all, act, down_cols), [vmem()] * 2 + [anywhere()] * 3,
         [
             shape((total // 16, width), f32), shape((16, 64, cols), bf16),
             shape((total // 16, fill), f32),
         ],
-        [vmem()] * 3, Weigh.scratch(cols) + Scatter.scratch(width) + Scatter.scratch(fill),
+        [vmem()] * 3,
+        [VM(hidden_all.shape, bf16), VM(act.shape, bf16), VM(down_cols.shape, bf16), dma((3,))]
+        + Weigh.scratch(cols) + Scatter.scratch(width) + Scatter.scratch(fill),
     )
 
 
 def normed_grad_kernel(grad, in_cols, normed_all, x, gain, act, down_cols, gains, down_half, out_rows,
                        value_grad, gains_out, feed_out, down_rows, down_other, in_mine, in_other,
-                       out_other, normed_grad, half, gains_v, got, total, theirs, x_s, x_r, g_s, g_r,
+                       out_other, normed_grad, half, gains_v, got, total, theirs, normed_v, act_v, down_v,
+                       copies, x_s, x_r, g_s, g_r,
                        *rest):
     sems_d, sems_i, sems_w, scratch, scratch_f = halves_of(rest, [5, 5, 5, 11, 11])
     s = Spot()
+    loads = loaded([(normed_all, normed_v), (act, act_v), (down_cols, down_v)], copies)
     greet(s)
     back_i = Return(s, half, in_mine, 3, sems_i, other=in_other)
-    weigh = Weigh(s, normed_all, grad, half, sems_w, back=back_i)
+    weigh = Weigh(s, normed_v, grad, half, sems_w, back=back_i)
     back_d = Return(s, down_half, down_rows, 1, sems_d, other=down_other)
     scatter = Scatter(s, grad, in_cols, normed_grad, scratch)
-    filler = Scatter(s, act, down_cols, feed_out, scratch_f, FILL[2][0])
+    filler = Scatter(s, act_v, down_v, feed_out, scratch_f, FILL[2][0])
     over = send_over(out_rows, out_other, x_s.at[0], x_r.at[0], s)
     back_d.start()
 
@@ -1406,10 +1452,10 @@
 
     merged(
         scatter.tasks(),
-        weigh.products() + nothing(24),
-        nothing(3) + weigh.folds() + nothing(12),
+        loads + weigh.products() + nothing(24),
+        nothing(5) + weigh.folds() + nothing(12),
         nothing(10) + [over.start] + back_d.tasks() + nothing(5),
-        nothing(2) + filler.tasks(),
+        nothing(4) + filler.tasks(),
         nothing(16) + back_i.tasks(),
     )
     scatter.finish()
@@ -1448,7 +1494,7 @@
     return communicate(
         normed_grad_kernel, "normed_grad", number,
         (grad, in_cols, normed_all, x, gain, act, down_cols, gains, down_half, out_rows),
-        [vmem()] * 8 + [anywhere()] * 2,
+        [vmem()] * 2 + [anywhere()] + [vmem()] * 2 + [anywhere()] * 2 + [vmem()] + [anywhere()] * 2,
         [
             shape((tokens, width), f32), shape((8, 128), f32), shape((tokens, fill), f32),
             down_rows, down_rows, in_rows, in_rows, shape(out_rows.shape, bf16),
@@ -1457,6 +1503,7 @@
         [
             VM((tokens, width), f32), VM((16, 64, cols), bf16), VM((16, 8, 128), f32),
             VM((16, 8, 128), f32), VM((8, 128), f32), VM((8, 128), f32),
+            VM(normed_all.shape, bf16), VM(act.shape, bf16), VM(down_cols.shape, bf16), dma((3,)),
             dma((2,)), dma((2,)), dma((16,)), dma((16,)),
         ] + Return.sems(1) + Return.sems(3) + Weigh.scratch(cols) + Scatter.scratch(width)
         + Scatter.scratch(fill),
@@ -1574,11 +1621,11 @@
     keep = jnp.broadcast_to(jnp.where(fresh, 0.0, 1.0)[:, None, None], (segments, 8, DH))
 
     normed_all, in_cols, gains_all, qkv = project(layer_input, own_gains, in_weight, 0)
-    (local, mem_out, lse, combined, memory, normal, mixed_tokens, out_all, cot_all, gate_up_cols,
-     ) = attend_forward(qkv, keep, mix, out_weight, cotangent, gate_up, 1)
-    middle, hidden_all, act, feed_grad, down_cols = feed(
-        mixed_tokens, layer_input, gains_all, out_all, cot_all, gate_up_cols, down_weight, 2
-    )
+    (local, mem_out, lse, combined, memory, normal, middle, hidden, out_all, cot_all,
+     gate_up_cols) = attend_forward(
+        qkv, keep, mix, layer_input, gains_all, out_weight, cotangent, gate_up, 1
+    )
+    hidden_all, act, feed_grad, down_cols = feed(hidden, cot_all, gate_up_cols, down_weight, 2)
 
     hidden_grad, gate_up_half, feed_out_0 = hidden_grad_of(
         feed_grad, gate_up_cols, hidden_all, act, down_cols, 3

time: 632 us -> 616 us (0.975)
  Pallas kernels: 590 us -> 573 us
    pallas_call x6, Pallas kernels: 590 us -> 573 us  [communicate(): pl.pallas_call(kernel, out_shape=outs, in_specs=in_specs, out_specs=out_s...]
where the time goes in v5:
time: 616 us; the launch traced here: 606 us
  Pallas kernels  573 us (93%)
  other arithmetic  19.6 us (3%)
  local copies, waits for them, and re-layouts  6.72 us (1%)
    pallas_call x6, Pallas kernels, communicate(): pl.pallas_call(kernel, out_shape=outs, in_specs=in_specs, out_specs=out_s...  573 us

profile of v5, /device:TPU:0, one launch (start us, length us, event | category | flops | bytes accessed | tf_op | source)
XLA Modules:
  0.0 606.2 jit_solution(9856468851355159864)
XLA Ops:
  0.6 0.7 pad_convert_fusion
  1.3 0.7 bitcast_convert_fusion
  2.0 0.6 copy-done.14
  2.6 71.3 %project.1 = (bf16[2048,2048]{1,0:T(8,128)(2,1)}, bf16[2048,384]{1,0:T(8,128)(2,1)}, f32[16,8,128]{2,1,0:T(8,128)}, bf16[2048,384]{1,0:T(8,128)(2,1)}) custom-call(bf16[128,2048]{1,0:T(8,128)(2,1)} %x.9, f32[8,128]{1,0:T(8,128)} %copy-done.14, bf16[128,6144]{1,0:T(8,128)(2,1)} %in_w.1), custom_call_target="tpu_custom_call" | custom-call | bytes 16777216 | tf_op jit(solution)/shard_map/project/pallas_call | solution.py:983
  73.9 0.7 fusion.1
  74.6 0.7 broadcast_in_dim.53.keep
  75.3 0.7 add_divide_fusion
  75.9 0.6 broadcast_in_dim.54.mix
  76.5 121.0 %attend.1 = (f32[2048,128]{1,0:T(8,128)}, f32[2048,128]{1,0:T(8,128)}, f32[2048,128]{1,0:T(8,128)}, bf16[2048,128]{1,0:T(8,128)(2,1)}, f32[2,128,128]{2,1,0:T(8,...) custom-call(bf16[2048,384]{1,0:T(8,128)(2,1)} %get-tuple-element.70., ...), custom_call_target="tpu_custom_call" | custom-call | bytes 16777216 | tf_op jit(solution)/shard_map/attend/pallas_call | solution.py:983
  197.6 78.9 %feed.1 = (bf16[2048,2048]{1,0:T(8,128)(2,1)}, bf16[2048,512]{1,0:T(8,128)(2,1)}, bf16[2048,1024]{1,0:T(8,128)(2,1)}, bf16[2048,512]{1,0:T(8,128)(2,1)}) custom-call(bf16[128,2048]{1,0:T(8,128)(2,1)} %get-tuple-element.73.hidden, bf16[2048,2048]{1,0:T(8,128)(2,1)} %get-tuple-element.74.cot_all, bf16[2048,1024]{1,0:T(8,128)(2,1)} %get-tuple-element.75.gate_up_cols, ...), custom_call_target="tpu_custom_call" | custom-call | bytes 16777216 | tf_op jit(solution)/shard_map/feed/pallas_call | solution.py:983
  276.5 0.0 copy-start
  276.5 77.8 %hidden_grad.1 = (f32[128,2048]{1,0:T(8,128)}, bf16[16,64,1024]{2,1,0:T(8,128)(2,1)}, f32[128,512]{1,0:T(8,128)}) custom-call(bf16[2048,1024]{1,0:T(8,128)(2,1)} %get-tuple-element.76.feed_grad, bf16[2048,1024]{1,0:T(8,128)(2,1)} %get-tuple-element.75.gate_up_cols, bf16[2048,2048]{1,0:T(8,128)(2,1)} %get-tuple-element.77.hidden_all, ...), custom_call_target="tpu_custom_call" | custom-call | bytes 16777216 | tf_op jit(solution)/shard_map/hidden_grad/pallas_call | solution.py:983
  354.3 0.0 copy-start.2
  354.3 0.0 copy-start.3
  354.3 0.0 copy-done
  354.4 0.2 multiply_reduce_fusion.2
  354.5 1.0 fusion.3
  355.5 1.5 multiply_reduce_fusion
  357.0 0.0 copy-done.2
  357.0 0.0 copy-done.3
  357.1 1.2 fusion.2
  358.3 124.2 %attend_back.1 = (bf16[2048,2048]{1,0:T(8,128)(2,1)}, bf16[2048,384]{1,0:T(8,128)(2,1)}, f32[8,128]{1,0:T(8,128)}, bf16[64,16384]{1,0:T(8,128)(2,1)}, bf16[64,16...) custom-call(bf16[128,2048]{1,0:T(8,128)(2,1)} %get-tuple-element.109.attended, ...), custom_call_target="tpu_custom_call" | custom-call | bytes 16777216 | tf_op jit(solution)/shard_map/attend_back/pallas_call | solution.py:983
  482.5 0.0 copy-done.6
  482.5 5.5 convolution_convert_fusion.out_rows
  487.9 0.7 slice_bitcast_fusion.3
  488.6 0.1 broadcast_select_fusion.6
  488.7 0.7 select_maximum_fusion.gains
  489.4 0.6 broadcast_in_dim.56.gain
  490.0 99.7 %normed_grad.1 = (f32[128,2048]{1,0:T(8,128)}, f32[8,128]{1,0:T(8,128)}, f32[128,512]{1,0:T(8,128)}, bf16[64,8192]{1,0:T(8,128)(2,1)}, bf16[64,8192]{1,0:T(8,128...) custom-call(bf16[2048,384]{1,0:T(8,128)(2,1)} %get-tuple-element.90.grad, ...), custom_call_target="tpu_custom_call" | custom-call | bytes 16777216 | tf_op jit(solution)/shard_map/normed_grad/pallas_call | solution.py:983
  589.7 1.7 broadcast_select_fusion.3
  591.4 0.0 copy-start.4
  591.4 0.0 copy-start.5
  591.4 2.6 maximum_convert_fusion.1
  594.0 0.0 copy-done.4
  594.0 1.2 copy-done.5
  595.1 0.3 broadcast_select_fusion.1
  595.4 0.0 copy-start.8
  595.4 0.0 copy-start.9
  595.4 4.2 maximum_convert_fusion
  599.7 0.0 copy-done.8
  599.7 0.1 broadcast_select_fusion.5
  599.8 0.0 copy-start.1
  599.8 2.0 maximum_convert_fusion.2
  601.8 0.0 copy-done.7
  601.8 1.1 add.42
  602.9 0.0 copy-done.10
  603.0 1.4 fusion
  604.4 1.3 slice_bitcast_fusion
  (16 shorter events, 0.1 us)
Async XLA Ops:
  2.0 0.6 copy-start.14
  276.5 77.9 %copy-start = (f32[128,2048]{1,0:T(8,128)S(1)}, f32[128,2048]{1,0:T(8,128)}, u32[]{:S(2)}) copy-start(f32[128,2048]{1,0:T(8,128)} %get-tuple-element.72) | copy-start | bytes 3145732
  354.3 2.7 copy-start.2
  354.3 2.7 copy-start.3
  358.2 124.2 %copy-start.6 = (bf16[2048,128]{1,0:T(8,128)(2,1)S(1)}, bf16[2048,128]{1,0:T(8,128)(2,1)}, u32[]{:S(2)}) copy-start(bf16[2048,128]{1,0:T(8,128)(2,1)} %get-tuple-element.95) | copy-start | bytes 1572868
  591.4 2.6 copy-start.4
  591.4 3.7 copy-start.5
  595.4 4.3 copy-start.8
  595.4 4.3 copy-start.9
  599.8 2.0 copy-start.7
  599.8 3.1 copy-start.1
  599.8 3.1 copy-start.10
  599.8 3.1 copy-start.11
  599.8 3.1 copy-start.12
  599.8 3.1 copy-start.13

commit v6 on v5

--- a/solution.py
+++ b/solution.py
@@ -1201,22 +1201,26 @@
         return [(n, i) for n in range(self.segments) for i in range(SEG // ROWS)]
 
 
-def attend_kernel(qkv, keep, mix, x, gains_all, out_w, cot, gate_up,
-                  local, mem_out, lse, combined, memory, normal, middle, hidden, out_all, cot_all,
-                  gate_up_cols, mixed_tokens, copies, t_s, t_r, *rest):
-    sems_o, sems_c, sems_g = halves_of(rest, [11, 7, 5])
+def forward_kernel(qkv, keep, mix, x, gains_all, out_w, cot, gate_up, down,
+                   local, mem_out, lse, combined, memory, normal, middle, out_all, cot_all,
+                   gate_up_cols, down_cols, hidden_all, act, feed_grad,
+                   mixed_tokens, hidden, out_v, cot_v, gate_up_v, down_v, hidden_v, act_v, grad_v,
+                   copies, outs, t_s, t_r, *rest):
+    sems_o, sems_c, sems_g, sems_d, sems_h = halves_of(rest, [11, 7, 5, 5, 7])
     s = Spot()
     mine = pl.ds(pl.multiple_of(s.me * 128, 128), 128)
     own = [
-        pltpu.make_async_copy(out_w, out_all.at[mine], copies.at[0]),
-        pltpu.make_async_copy(cot, cot_all.at[mine], copies.at[1]),
+        pltpu.make_async_copy(out_w, out_v.at[mine], copies.at[0]),
+        pltpu.make_async_copy(cot, cot_v.at[mine], copies.at[1]),
     ]
     for cp in own:
         cp.start()
     greet(s)
-    gather_o = SharedGather(s, out_w, out_all, sems_o)
-    gather_c = Gather(s, cot, cot_all, sems_c)
-    columns_g = Columns(s, gate_up, gate_up_cols, 2, sems_g)
+    gather_o = SharedGather(s, out_w, out_v, sems_o)
+    gather_c = Gather(s, cot, cot_v, sems_c)
+    gather_h = Gather(s, hidden, hidden_v, sems_h)
+    columns_g = Columns(s, gate_up, gate_up_v, 2, sems_g)
+    columns_d = Columns(s, down, down_v, 1, sems_d)
     gather_o.start()
     gather_c.start()
     columns_g.start(4)
@@ -1235,6 +1239,12 @@
             pl.when(s.me != j)(lambda: token_copy(j).start())
 
     compute = [attend.states] + [functools.partial(block, n, i) for n, i in attend.blocks()]
+    wholes = [
+        pltpu.make_async_copy(a, b, outs.at[4, i])
+        for i, (a, b) in enumerate(
+            [(out_v, out_all), (cot_v, cot_all), (gate_up_v, gate_up_cols), (down_v, down_cols)]
+        )
+    ]
 
     def tokens():
         own[0].wait()
@@ -1247,7 +1257,7 @@
 
     def output(j):
         w = pl.ds(j * 512, 512)
-        got = jnp.dot(mixed_tokens[...], out_all[:, w], preferred_element_type=f32)
+        got = jnp.dot(mixed_tokens[...], out_v[:, w], preferred_element_type=f32)
         middle[:, w] = got + x[:, w].astype(f32)
 
     def norm():
@@ -1255,62 +1265,12 @@
         factor = lax.rsqrt(jnp.mean(values * values, axis=-1, keepdims=True) + epsilon)
         for j in range(16):
             w = pl.ds(j * 128, 128)
-            hidden[:, w] = (middle[:, w] * factor * gains_all[j, 1:2, :]).astype(bf16)
-
-    after = [tokens] + [functools.partial(output, j) for j in range(4)] + [norm]
-    merged(
-        gather_o.tasks(),
-        gather_c.tasks(),
-        columns_g.tasks(),
-        compute + nothing(len(compute)),
-    )
-    merged(after)
-    columns_g.finish()
-    for j in range(16):
-        pl.when(s.me != j)(lambda: token_copy(j).wait_send())
-    gather_o.drain()
-    gather_c.drain()
-    columns_g.drain()
-    own[1].wait()
-
-
-def attend_forward(qkv, keep, mix, x, gains_all, out_weight, cotangent, gate_up, number):
-    tokens, width = cotangent.shape
-    total = qkv.shape[0]
-    segments = total // SEG
-    shape = jax.ShapeDtypeStruct
-    return communicate(
-        attend_kernel, "attend", number,
-        (qkv, keep, mix, x, gains_all, out_weight, cotangent, gate_up), [vmem()] * 5 + [anywhere()] * 3,
-        [
-            shape((total, DH), f32), shape((total, DH), f32), shape((total, DH), f32),
-            shape((total, DH), bf16), shape((segments, DH, DH), f32), shape((segments, 8, DH), f32),
-            shape((tokens, width), f32), shape((tokens, width), bf16),
-            shape((total, width), bf16), shape((total, width), bf16),
-            shape((width, gate_up.shape[1] // 16), bf16),
-        ],
-        [vmem()] * 9 + [anywhere()] * 2,
-        [VM((tokens, width), bf16), dma((2,)), dma((16,)), dma((16,))] + SharedGather.sems() + Gather.sems() + Columns.sems(2),
-    )
-
-
-def feed_kernel(hidden, cot_all, gate_up_cols, down,
-                hidden_all, act, feed_grad, down_cols,
-                hidden_v, act_v, grad_v, down_v, cot_v, gate_up_v, copies, outs, *rest):
-    sems, sems_d = halves_of(rest, [7, 5])
-    s = Spot()
-    loads = [
-        pltpu.make_async_copy(a, b, copies.at[i])
-        for i, (a, b) in enumerate([(gate_up_cols, gate_up_v), (cot_all, cot_v)])
-    ]
-    for cp in loads:
-        cp.start()
-    greet(s)
-    gather = Gather(s, hidden, hidden_v, sems)
-    gather.start()
-    columns = Columns(s, down, down_v, 1, sems_d)
-    columns.start()
-    hidden_v[pl.ds(pl.multiple_of(s.me * 128, 128), 128), :] = hidden[...]
+            part = (middle[:, w] * factor * gains_all[j, 1:2, :]).astype(bf16)
+            hidden[:, w] = part
+            hidden_v[mine, w] = part
+        gather_h.start()
+        wholes[0].start()
+
     half = act.shape[1]
 
     def out_copies(j):
@@ -1320,14 +1280,13 @@
             pltpu.make_async_copy(a.at[tok], b.at[tok], outs.at[j, i]) for i, (a, b) in enumerate(pairs)
         ]
 
-    out_down = pltpu.make_async_copy(down_v, down_cols, outs.at[4, 0])
-
     def use(j):
         if j == 0:
-            for cp in loads:
-                cp.wait()
-            columns.finish()
-            out_down.start()
+            own[1].wait()
+            columns_g.finish()
+            columns_d.finish()
+            for cp in wholes[1:]:
+                cp.start()
         tok = pl.ds(pl.multiple_of(s.arrival(j) * 512, 512), 512)
         act_grad = jnp.dot(cot_v[tok, :], down_v[...], preferred_element_type=f32)
         gate = jnp.dot(hidden_v[tok, :], gate_up_v[:, :half], preferred_element_type=f32)
@@ -1341,32 +1300,51 @@
         for cp in out_copies(j):
             cp.start()
 
-    merged(gather.tasks(use), nothing(2) + columns.tasks() + nothing(8))
-    gather.drain()
-    columns.drain()
-    out_down.wait()
+    after = [tokens] + [functools.partial(output, j) for j in range(4)] + [norm]
+    c_tasks = gather_c.tasks()
+    early = len(c_tasks) * 4 // 5
+    merged(gather_o.tasks(), c_tasks[:early], columns_g.tasks(), compute + nothing(len(compute)))
+    merged(after, [functools.partial(columns_d.start, 4)])
+    merged(
+        gather_h.tasks(use),
+        c_tasks[early:] + nothing(12),
+        nothing(2) + columns_d.tasks() + nothing(8),
+    )
+    for j in range(16):
+        pl.when(s.me != j)(lambda: token_copy(j).wait_send())
+    for part in (gather_o, gather_c, gather_h, columns_g, columns_d):
+        part.drain()
+    for cp in wholes:
+        cp.wait()
     for j in range(4):
         for cp in out_copies(j):
             cp.wait()
 
 
-def feed(hidden, cot_all, gate_up_cols, down, number):
-    total, width = cot_all.shape
+def forward_of(qkv, keep, mix, x, gains_all, out_weight, cotangent, gate_up, down, number):
+    tokens, width = x.shape
+    total = qkv.shape[0]
+    segments = total // SEG
     half = down.shape[1] // 16
     shape = jax.ShapeDtypeStruct
+    rows, cols, fine = (total, width), (width, 2 * half), (total, half)
     return communicate(
-        feed_kernel, "feed", number, (hidden, cot_all, gate_up_cols, down),
-        [vmem()] + [anywhere()] * 3,
+        forward_kernel, "forward", number,
+        (qkv, keep, mix, x, gains_all, out_weight, cotangent, gate_up, down),
+        [vmem()] * 5 + [anywhere()] * 4,
         [
-            shape((total, width), bf16), shape((total, half), bf16), shape((total, 2 * half), bf16),
-            shape((width, half), bf16),
+            shape((total, DH), f32), shape((total, DH), f32), shape((total, DH), f32),
+            shape((total, DH), bf16), shape((segments, DH, DH), f32), shape((segments, 8, DH), f32),
+            shape((tokens, width), f32),
+            shape((width, width), bf16), shape(rows, bf16), shape(cols, bf16), shape((width, half), bf16),
+            shape(rows, bf16), shape(fine, bf16), shape((total, 2 * half), bf16),
         ],
-        [anywhere()] * 4,
+        [vmem()] * 7 + [anywhere()] * 7,
         [
-            VM((total, width), bf16), VM((total, half), bf16), VM((total, 2 * half), bf16),
-            VM((width, half), bf16), VM((total, width), bf16), VM(gate_up_cols.shape, bf16),
-            dma((2,)), dma((5, 3)),
-        ] + Gather.sems() + Columns.sems(1),
+            VM((tokens, width), bf16), VM((tokens, width), bf16), VM((width, width), bf16),
+            VM(rows, bf16), VM(cols, bf16), VM((width, half), bf16), VM(rows, bf16), VM(fine, bf16),
+            VM((total, 2 * half), bf16), dma((2,)), dma((5, 4)), dma((16,)), dma((16,)),
+        ] + SharedGather.sems() + Gather.sems() + Columns.sems(2) + Columns.sems(1) + Gather.sems(),
     )
 
 
@@ -1415,14 +1393,17 @@
     )
 
 
-def normed_grad_kernel(grad, in_cols, normed_all, x, gain, act, down_cols, gains, down_half, out_rows,
-                       value_grad, gains_out, feed_out, down_rows, down_other, in_mine, in_other,
-                       out_other, normed_grad, half, gains_v, got, total, theirs, normed_v, act_v, down_v,
+def normed_grad_kernel(grad, in_cols, normed_all, x, gain, act, down_cols, gains, down_half, combined,
+                       attended_all,
+                       value_grad, gains_out, feed_out, out_rows, down_rows, down_other, in_mine,
+                       in_other, out_other, attended_v, normed_grad, half, gains_v, got, total, theirs, normed_v, act_v, down_v,
                        copies, x_s, x_r, g_s, g_r,
                        *rest):
     sems_d, sems_i, sems_w, scratch, scratch_f = halves_of(rest, [5, 5, 5, 11, 11])
     s = Spot()
-    loads = loaded([(normed_all, normed_v), (act, act_v), (down_cols, down_v)], copies)
+    loads = loaded(
+        [(normed_all, normed_v), (act, act_v), (down_cols, down_v), (attended_all, attended_v)], copies
+    )
     greet(s)
     back_i = Return(s, half, in_mine, 3, sems_i, other=in_other)
     weigh = Weigh(s, normed_v, grad, half, sems_w, back=back_i)
@@ -1431,6 +1412,12 @@
     filler = Scatter(s, act_v, down_v, feed_out, scratch_f, FILL[2][0])
     over = send_over(out_rows, out_other, x_s.at[0], x_r.at[0], s)
     back_d.start()
+
+    def out_product(j):
+        w = pl.ds(j * 512, 512)
+        out_rows[:, w] = rows_dot(combined[...], attended_v[:, w]).astype(bf16)
+
+    products = [functools.partial(out_product, j) for j in range(4)]
 
     def gain_copy(k):
         to = s.partner(k)
@@ -1452,9 +1439,9 @@
 
     merged(
         scatter.tasks(),
-        loads + weigh.products() + nothing(24),
+        loads[:3] + weigh.products() + nothing(24),
         nothing(5) + weigh.folds() + nothing(12),
-        nothing(10) + [over.start] + back_d.tasks() + nothing(5),
+        nothing(4) + loads[3:] + products + [over.start] + back_d.tasks() + nothing(5),
         nothing(4) + filler.tasks(),
         nothing(16) + back_i.tasks(),
     )
@@ -1484,7 +1471,8 @@
     gains_out[...] = total[...] + theirs[...]
 
 
-def normed_grad_of(grad, in_cols, normed_all, x, gain, act, down_cols, gains, down_half, out_rows, number):
+def normed_grad_of(grad, in_cols, normed_all, x, gain, act, down_cols, gains, down_half, combined,
+                   attended_all, number):
     shape = jax.ShapeDtypeStruct
     total, cols = grad.shape
     tokens, width = x.shape
@@ -1493,17 +1481,18 @@
     in_rows = shape((64, 16 * cols), bf16)
     return communicate(
         normed_grad_kernel, "normed_grad", number,
-        (grad, in_cols, normed_all, x, gain, act, down_cols, gains, down_half, out_rows),
-        [vmem()] * 2 + [anywhere()] + [vmem()] * 2 + [anywhere()] * 2 + [vmem()] + [anywhere()] * 2,
+        (grad, in_cols, normed_all, x, gain, act, down_cols, gains, down_half, combined, attended_all),
+        [vmem()] * 2 + [anywhere()] + [vmem()] * 2 + [anywhere()] * 2 + [vmem(), anywhere(), vmem(), anywhere()],
         [
             shape((tokens, width), f32), shape((8, 128), f32), shape((tokens, fill), f32),
-            down_rows, down_rows, in_rows, in_rows, shape(out_rows.shape, bf16),
+            shape((DH, width), bf16), down_rows, down_rows, in_rows, in_rows, shape((DH, width), bf16),
         ],
-        [vmem()] * 3 + [anywhere()] * 5,
+        [vmem()] * 4 + [anywhere()] * 5,
         [
+            VM(attended_all.shape, bf16),
             VM((tokens, width), f32), VM((16, 64, cols), bf16), VM((16, 8, 128), f32),
             VM((16, 8, 128), f32), VM((8, 128), f32), VM((8, 128), f32),
-            VM(normed_all.shape, bf16), VM(act.shape, bf16), VM(down_cols.shape, bf16), dma((3,)),
+            VM(normed_all.shape, bf16), VM(act.shape, bf16), VM(down_cols.shape, bf16), dma((4,)),
             dma((2,)), dma((2,)), dma((16,)), dma((16,)),
         ] + Return.sems(1) + Return.sems(3) + Weigh.scratch(cols) + Scatter.scratch(width)
         + Scatter.scratch(fill),
@@ -1621,12 +1610,10 @@
     keep = jnp.broadcast_to(jnp.where(fresh, 0.0, 1.0)[:, None, None], (segments, 8, DH))
 
     normed_all, in_cols, gains_all, qkv = project(layer_input, own_gains, in_weight, 0)
-    (local, mem_out, lse, combined, memory, normal, middle, hidden, out_all, cot_all,
-     gate_up_cols) = attend_forward(
-        qkv, keep, mix, layer_input, gains_all, out_weight, cotangent, gate_up, 1
-    )
-    hidden_all, act, feed_grad, down_cols = feed(hidden, cot_all, gate_up_cols, down_weight, 2)
-
+    (local, mem_out, lse, combined, memory, normal, middle, out_all, cot_all, gate_up_cols, down_cols,
+     hidden_all, act, feed_grad) = forward_of(
+        qkv, keep, mix, layer_input, gains_all, out_weight, cotangent, gate_up, down_weight, 1
+    )
     hidden_grad, gate_up_half, feed_out_0 = hidden_grad_of(
         feed_grad, gate_up_cols, hidden_all, act, down_cols, 3
     )
@@ -1642,14 +1629,13 @@
         middle_grad.astype(bf16), out_all, qkv, keep, mix, (local, mem_out, lse, memory, normal),
         gate_up_half, cot_all, act, down_cols, 4,
     )
-    out_rows = rows_dot(combined, attended_all).astype(bf16)
     mix_rows = jnp.where((jnp.arange(H) == lax.axis_index(AXIS))[:, None], mix_grad[0:1], 0.0)
     gain_grads = jnp.stack([mix_rows, second_local.reshape(16, 128), mix_rows], axis=1)
     gain_grads = jnp.pad(gain_grads, ((0, 0), (0, 5), (0, 0)))
-    (value_grad, gains_out, feed_out_2, down_rows, down_other, in_mine_rows, in_other_rows,
+    (value_grad, gains_out, feed_out_2, out_rows, down_rows, down_other, in_mine_rows, in_other_rows,
      out_other) = normed_grad_of(
         projected_grad, in_cols, normed_all, layer_input, jnp.broadcast_to(first_all[None], (8, width)),
-        act, down_cols, gain_grads, down_half, out_rows, 5,
+        act, down_cols, gain_grads, down_half, combined, attended_all, 5,
     )
     input_grad = middle_grad + value_grad
     feed_out = jnp.concatenate([feed_out_0, feed_out_1, feed_out_2], axis=1)

time: 616 us -> 596 us (0.968)
  Pallas kernels: 573 us -> 559 us
    pallas_call x6 -> x5, Pallas kernels: 573 us -> 559 us  [communicate(): pl.pallas_call(kernel, out_shape=outs, in_specs=in_specs, out_specs=out_s...]
where the time goes in v6:
time: 596 us; the launch traced here: 587 us
  Pallas kernels  559 us (94%)
  other arithmetic  19.6 us (3%)
  local copies, waits for them, and re-layouts  6.73 us (1%)
    pallas_call x5, Pallas kernels, communicate(): pl.pallas_call(kernel, out_shape=outs, in_specs=in_specs, out_specs=out_s...  559 us

profile of v6, /device:TPU:0, one launch (start us, length us, event | category | flops | bytes accessed | tf_op | source)
XLA Modules:
  0.0 586.6 jit_solution(1490930454922746423)
XLA Ops:
  0.6 0.7 pad_convert_fusion
  1.3 0.7 bitcast_convert_fusion
  2.0 0.6 copy-done.13
  2.6 71.3 %project.1 = (bf16[2048,2048]{1,0:T(8,128)(2,1)}, bf16[2048,384]{1,0:T(8,128)(2,1)}, f32[16,8,128]{2,1,0:T(8,128)}, bf16[2048,384]{1,0:T(8,128)(2,1)}) custom-call(bf16[128,2048]{1,0:T(8,128)(2,1)} %x.9, f32[8,128]{1,0:T(8,128)} %copy-done.13, bf16[128,6144]{1,0:T(8,128)(2,1)} %in_w.1), custom_call_target="tpu_custom_call" | custom-call | bytes 16777216 | tf_op jit(solution)/shard_map/project/pallas_call | solution.py:983
  73.9 0.7 fusion.1
  74.6 0.7 broadcast_in_dim.53.keep
  75.3 0.7 add_divide_fusion
  75.9 0.6 broadcast_in_dim.54.mix
  76.5 183.8 %forward.1 = (f32[2048,128]{1,0:T(8,128)}, f32[2048,128]{1,0:T(8,128)}, f32[2048,128]{1,0:T(8,128)}, bf16[2048,128]{1,0:T(8,128)(2,1)}, f32[2,128,128]{2,1,0:T(8...) custom-call(bf16[2048,384]{1,0:T(8,128)(2,1)} %get-tuple-element.70., ...), custom_call_target="tpu_custom_call" | custom-call | bytes 16777216 | tf_op jit(solution)/shard_map/forward/pallas_call | solution.py:983
  260.3 0.0 copy-start
  260.3 79.0 %hidden_grad.1 = (f32[128,2048]{1,0:T(8,128)}, bf16[16,64,1024]{2,1,0:T(8,128)(2,1)}, f32[128,512]{1,0:T(8,128)}) custom-call(bf16[2048,1024]{1,0:T(8,128)(2,1)} %get-tuple-element.73.feed_grad, bf16[2048,1024]{1,0:T(8,128)(2,1)} %get-tuple-element.74.gate_up_cols, bf16[2048,2048]{1,0:T(8,128)(2,1)} %get-tuple-element.75.hidden_all, ...), custom_call_target="tpu_custom_call" | custom-call | bytes 16777216 | tf_op jit(solution)/shard_map/hidden_grad/pallas_call | solution.py:983
  339.3 0.0 copy-start.1
  339.3 0.0 copy-start.2
  339.3 0.0 copy-done
  339.3 0.2 multiply_reduce_fusion.2
  339.5 1.0 fusion.3
  340.5 1.5 multiply_reduce_fusion
  342.0 0.0 copy-done.1
  342.0 0.0 copy-done.2
  342.0 1.2 fusion.2
  343.2 123.7 %attend_back.1 = (bf16[2048,2048]{1,0:T(8,128)(2,1)}, bf16[2048,384]{1,0:T(8,128)(2,1)}, f32[8,128]{1,0:T(8,128)}, bf16[64,16384]{1,0:T(8,128)(2,1)}, bf16[64,16...) custom-call(bf16[128,2048]{1,0:T(8,128)(2,1)} %get-tuple-element.109.attended, ...), custom_call_target="tpu_custom_call" | custom-call | bytes 16777216 | tf_op jit(solution)/shard_map/attend_back/pallas_call | solution.py:983
  467.0 0.7 slice_bitcast_fusion.3
  467.7 0.1 broadcast_select_fusion.6
  467.8 0.7 select_maximum_fusion.gains
  468.4 0.6 broadcast_in_dim.56.gain
  469.1 101.0 %normed_grad.1 = (f32[128,2048]{1,0:T(8,128)}, f32[8,128]{1,0:T(8,128)}, f32[128,512]{1,0:T(8,128)}, bf16[128,2048]{1,0:T(8,128)(2,1)}, bf16[64,8192]{1,0:T(8,12...) custom-call(bf16[2048,384]{1,0:T(8,128)(2,1)} %get-tuple-element.89., ...), custom_call_target="tpu_custom_call" | custom-call | bytes 16777216 | tf_op jit(solution)/shard_map/normed_grad/pallas_call | solution.py:983
  570.1 1.7 broadcast_select_fusion.3
  571.8 0.0 copy-start.3
  571.8 0.0 copy-start.4
  571.8 2.6 maximum_convert_fusion.1
  574.4 0.0 copy-done.3
  574.4 1.2 copy-done.4
  575.5 0.3 broadcast_select_fusion.1
  575.8 0.0 copy-start.6
  575.8 0.0 copy-start.7
  575.8 4.2 maximum_convert_fusion
  580.1 0.0 copy-done.6
  580.1 0.0 copy-done.7
  580.1 0.1 broadcast_select_fusion.5
  580.2 0.0 copy-start.5
  580.2 0.0 copy-start.8
  580.2 0.0 copy-start.9
  580.2 0.0 copy-start.10
  580.2 2.0 maximum_convert_fusion.2
  582.2 1.1 add.42
  583.3 0.0 copy-done.10
  583.4 1.4 fusion
  584.8 1.3 slice_bitcast_fusion
  (12 shorter events, 0.1 us)
Async XLA Ops:
  2.0 0.6 copy-start.13
  260.3 79.0 %copy-start = (f32[128,2048]{1,0:T(8,128)S(1)}, f32[128,2048]{1,0:T(8,128)}, u32[]{:S(2)}) copy-start(f32[128,2048]{1,0:T(8,128)} %get-tuple-element.72) | copy-start | bytes 3145732
  339.3 2.7 copy-start.1
  339.3 2.7 copy-start.2
  571.8 2.6 copy-start.3
  571.8 3.7 copy-start.4
  575.8 4.3 copy-start.6
  575.8 4.3 copy-start.7
  580.2 2.0 copy-start.5
  580.2 3.1 copy-start.8
  580.2 3.1 copy-start.9
  580.2 3.1 copy-start.10
  580.2 3.1 copy-start.11
  580.2 3.1 copy-start.12

commit v7 on v6

--- a/solution.py
+++ b/solution.py
@@ -701,34 +701,40 @@
 
 
 class Return:
+    ahead = 16
+
     @staticmethod
     def sems(parts):
         return [dma((16, parts))] * 4 + [dma((parts,))]
 
-    ahead = 16
-
-    def __init__(self, s, src, dst, parts, sems, other=None):
-        self.s, self.src, self.dst, self.parts, self.other = s, src, dst, parts, other
+    def __init__(self, s, src, dst, parts, sems):
+        self.s, self.src, self.dst, self.parts = s, src, dst, parts
         self.e = src.shape[2] // parts
         self.ps, self.pr, self.xs, self.xr, self.own = sems
 
-    def place(self, ref, p, h):
-        return ref.at[:, pl.ds(pl.multiple_of(p * 16 * self.e + h * self.e, 128), self.e)]
+    def place(self, p, h, half):
+        cols = pl.ds(pl.multiple_of(p * 16 * self.e + h * self.e, 128), self.e)
+        return self.dst.at[pl.ds(pl.multiple_of(half * 64, 64), 64), cols]
+
+    def block(self, h, p):
+        return self.src.at[h, :, pl.ds(p * self.e, self.e)]
 
     def copy(self, k, p):
         s = self.s
         to = s.partner(k)
         return send(
-            self.src.at[to, :, pl.ds(p * self.e, self.e)], self.place(self.dst, p, s.me),
-            self.ps.at[k, p], self.pr.at[s.me, p], to,
+            self.block(to, p), self.place(p, s.me, s.dp), self.ps.at[k, p], self.pr.at[s.me, p], to
         )
 
     def local(self, p):
         s = self.s
-        return pltpu.make_async_copy(
-            self.src.at[s.me, :, pl.ds(p * self.e, self.e)], self.place(self.dst, p, s.me),
-            self.own.at[p],
-        )
+        return pltpu.make_async_copy(self.block(s.me, p), self.place(p, s.me, s.dp), self.own.at[p])
+
+    def over(self, h, p, own=False):
+        s = self.s
+        dst = self.place(p, h, s.dp)
+        src = self.block(s.me, p) if own else dst
+        return send_over(src, dst, self.xs.at[h, p], self.xr.at[h, p], s)
 
     def begin(self, k):
         for p in range(self.parts):
@@ -736,29 +742,19 @@
                 self.copy(k, p).start()
                 continue
             self.local(p).start()
-            if self.other is not None:
-                self.over(self.s.me, p, own=True).start()
-
-    def start(self, ahead=16):
-        self.ahead = ahead
-        for k in range(ahead):
+            self.over(self.s.me, p, own=True).start()
+
+    def start(self):
+        for k in range(16):
             self.begin(k)
 
-    def over(self, h, p, own=False):
-        s = self.s
-        src = self.src.at[s.me, :, pl.ds(p * self.e, self.e)] if own else self.place(self.dst, p, h)
-        return send_over(src, self.place(self.other, p, h), self.xs.at[h, p], self.xr.at[h, p], s)
-
     def arrive(self, k):
         s = self.s
-        if k + self.ahead - 1 < 16:
-            self.begin(k + self.ahead - 1)
         h = s.partner(k)
         for p in range(self.parts):
-            b = self.place(self.dst, p, h)
+            b = self.place(p, h, s.dp)
             send(b, b, self.ps.at[k, p], self.pr.at[h, p], s.me).wait_recv()
-            if self.other is not None:
-                self.over(h, p).start()
+            self.over(h, p).start()
 
     def tasks(self):
         return [functools.partial(self.arrive, k) for k in range(1, 16)]
@@ -767,19 +763,16 @@
         s = self.s
         for p in range(self.parts):
             self.local(p).wait()
-        if self.other is not None:
-            for k in range(16):
-                h = s.partner(k)
-                for p in range(self.parts):
-                    b = self.place(self.other, p, h)
-                    send_over(b, b, self.xs.at[h, p], self.xr.at[h, p], s).wait_recv()
-        for k in range(1, 16):
+        for k in range(16):
+            h = s.partner(k)
             for p in range(self.parts):
-                self.copy(k, p).wait_send()
-        if self.other is not None:
-            for k in range(16):
-                for p in range(self.parts):
-                    self.over(s.partner(k), p).wait_send()
+                b = self.place(p, h, 1 - s.dp)
+                send_over(b, b, self.xs.at[h, p], self.xr.at[h, p], s).wait_recv()
+        for k in range(16):
+            for p in range(self.parts):
+                if k:
+                    self.copy(k, p).wait_send()
+                self.over(s.partner(k), p).wait_send()
 
 
 class Scatter:
@@ -977,6 +970,30 @@
         out.append(refs[at:at + n])
         at += n
     return out
+
+
+def loaded(pairs, sems):
+    copies = [pltpu.make_async_copy(a, b, sems.at[i]) for i, (a, b) in enumerate(pairs)]
+    for cp in copies:
+        cp.start()
+    return [cp.wait for cp in copies]
+
+
+def norm_back(values, upstream, gains_all, which, write):
+    whole = values[...].astype(f32)
+    width = whole.shape[1]
+    factor = lax.rsqrt(jnp.mean(whole * whole, axis=-1, keepdims=True) + epsilon)
+    dot_row = jnp.zeros_like(factor)
+    for j in range(16):
+        w = pl.ds(j * 128, 128)
+        scaled = upstream[:, w] * gains_all[j, which:which + 1, :] * values[:, w].astype(f32)
+        dot_row = dot_row + jnp.sum(scaled, axis=-1, keepdims=True)
+    dot_row = dot_row * (1.0 / width) * factor * factor * factor
+    for j in range(16):
+        w = pl.ds(j * 128, 128)
+        v, u = values[:, w].astype(f32), upstream[:, w]
+        grad = factor * (u * gains_all[j, which:which + 1, :]) - v * dot_row
+        write(j, grad, jnp.sum(u * v * factor, axis=0, keepdims=True))
 
 
 def communicate(kernel, name, number, ins, in_specs, outs, out_specs, scratch, flops=0):
@@ -1348,27 +1365,25 @@
     )
 
 
-def loaded(pairs, sems):
-    copies = [pltpu.make_async_copy(a, b, sems.at[i]) for i, (a, b) in enumerate(pairs)]
-    for cp in copies:
-        cp.start()
-    return [cp.wait for cp in copies]
-
-
 def hidden_grad_kernel(feed_grad, gate_up_cols, hidden_all, act, down_cols, out, half, feed_out,
-                       hidden_v, act_v, down_v, copies, *rest):
+                       grad_v, gate_up_v, hidden_v, act_v, down_v, copies, *rest):
     sems_w, scratch, scratch_f = halves_of(rest, [5, 11, 11])
     s = Spot()
-    loads = loaded([(hidden_all, hidden_v), (act, act_v), (down_cols, down_v)], copies)
+    loads = loaded(
+        [(feed_grad, grad_v), (gate_up_cols, gate_up_v), (hidden_all, hidden_v), (act, act_v),
+         (down_cols, down_v)],
+        copies,
+    )
     greet(s, plane=False)
-    weigh = Weigh(s, hidden_v, feed_grad, half, sems_w)
-    scatter = Scatter(s, feed_grad, gate_up_cols, out, scratch)
+    weigh = Weigh(s, hidden_v, grad_v, half, sems_w)
+    scatter = Scatter(s, grad_v, gate_up_v, out, scratch)
+    scatter.lag = 2
     filler = Scatter(s, act_v, down_v, feed_out, scratch_f, FILL[0][0])
     merged(
-        scatter.tasks(),
-        loads + weigh.products() + nothing(16),
+        loads[:2] + scatter.tasks(),
+        nothing(1) + loads[2:] + weigh.products() + nothing(8),
         nothing(4) + filler.tasks(),
-        nothing(20) + weigh.folds(),
+        nothing(40) + weigh.folds(),
     )
     scatter.finish()
     filler.finish()
@@ -1382,21 +1397,21 @@
     fill = FILL[0][1]
     return communicate(
         hidden_grad_kernel, "hidden_grad", number,
-        (feed_grad, gate_up_cols, hidden_all, act, down_cols), [vmem()] * 2 + [anywhere()] * 3,
+        (feed_grad, gate_up_cols, hidden_all, act, down_cols), [anywhere()] * 5,
         [
             shape((total // 16, width), f32), shape((16, 64, cols), bf16),
             shape((total // 16, fill), f32),
         ],
         [vmem()] * 3,
-        [VM(hidden_all.shape, bf16), VM(act.shape, bf16), VM(down_cols.shape, bf16), dma((3,))]
+        [VM(a.shape, bf16) for a in (feed_grad, gate_up_cols, hidden_all, act, down_cols)] + [dma((5,))]
         + Weigh.scratch(cols) + Scatter.scratch(width) + Scatter.scratch(fill),
     )
 
 
-def normed_grad_kernel(grad, in_cols, normed_all, x, gain, act, down_cols, gains, down_half, combined,
+def normed_grad_kernel(grad, in_cols, normed_all, x, gains_all, act, down_cols, gains, down_half, combined,
                        attended_all,
-                       value_grad, gains_out, feed_out, out_rows, down_rows, down_other, in_mine,
-                       in_other, out_other, attended_v, normed_grad, half, gains_v, got, total, theirs, normed_v, act_v, down_v,
+                       value_grad, gains_out, feed_out, out_rows, down_rows, in_rows, out_other,
+                       attended_v, normed_grad, half, gains_v, got, total, theirs, normed_v, act_v, down_v,
                        copies, x_s, x_r, g_s, g_r,
                        *rest):
     sems_d, sems_i, sems_w, scratch, scratch_f = halves_of(rest, [5, 5, 5, 11, 11])
@@ -1405,9 +1420,9 @@
         [(normed_all, normed_v), (act, act_v), (down_cols, down_v), (attended_all, attended_v)], copies
     )
     greet(s)
-    back_i = Return(s, half, in_mine, 3, sems_i, other=in_other)
+    back_i = Return(s, half, in_rows, 3, sems_i)
     weigh = Weigh(s, normed_v, grad, half, sems_w, back=back_i)
-    back_d = Return(s, down_half, down_rows, 1, sems_d, other=down_other)
+    back_d = Return(s, down_half, down_rows, 1, sems_d)
     scatter = Scatter(s, grad, in_cols, normed_grad, scratch)
     filler = Scatter(s, act_v, down_v, feed_out, scratch_f, FILL[2][0])
     over = send_over(out_rows, out_other, x_s.at[0], x_r.at[0], s)
@@ -1423,19 +1438,10 @@
         to = s.partner(k)
         return send(gains_v.at[to], got.at[s.me], g_s.at[k], g_r.at[s.me], to)
 
-    def epilogue():
-        width = x.shape[1]
-        values = x[...].astype(f32)
-        factor = lax.rsqrt(jnp.mean(values * values, axis=-1, keepdims=True) + epsilon)
-        row = jnp.sum(normed_grad[...] * gain[0:1, :] * values, axis=-1, keepdims=True)
-        row = row * (1.0 / width) * factor * factor * factor
-        for j in range(16):
-            w = pl.ds(j * 128, 128)
-            v = x[:, w].astype(f32)
-            u = normed_grad[:, w]
-            value_grad[:, w] = factor * (u * gain[0:1, w]) - v * row
-            gains_v[j] = gains[j]
-            gains_v[j, 0:1, :] = jnp.sum(u * v * factor, axis=0, keepdims=True)
+    def write(j, value, gain):
+        value_grad[:, pl.ds(j * 128, 128)] = value
+        gains_v[j] = gains[j]
+        gains_v[j, 0:1, :] = gain
 
     merged(
         scatter.tasks(),
@@ -1446,7 +1452,7 @@
         nothing(16) + back_i.tasks(),
     )
     scatter.finish()
-    epilogue()
+    norm_back(x, normed_grad, gains_all, 0, write)
     for k in range(1, 16):
         gain_copy(k).start()
     filler.finish()
@@ -1471,23 +1477,24 @@
     gains_out[...] = total[...] + theirs[...]
 
 
-def normed_grad_of(grad, in_cols, normed_all, x, gain, act, down_cols, gains, down_half, combined,
+def normed_grad_of(grad, in_cols, normed_all, x, gains_all, act, down_cols, gains, down_half, combined,
                    attended_all, number):
     shape = jax.ShapeDtypeStruct
     total, cols = grad.shape
     tokens, width = x.shape
     fill = FILL[2][1]
-    down_rows = shape((64, 16 * down_half.shape[2]), bf16)
-    in_rows = shape((64, 16 * cols), bf16)
+    down_rows = shape((DH, 16 * down_half.shape[2]), bf16)
+    in_rows = shape((DH, 16 * cols), bf16)
     return communicate(
         normed_grad_kernel, "normed_grad", number,
-        (grad, in_cols, normed_all, x, gain, act, down_cols, gains, down_half, combined, attended_all),
+        (grad, in_cols, normed_all, x, gains_all, act, down_cols, gains, down_half, combined,
+         attended_all),
         [vmem()] * 2 + [anywhere()] + [vmem()] * 2 + [anywhere()] * 2 + [vmem(), anywhere(), vmem(), anywhere()],
         [
             shape((tokens, width), f32), shape((8, 128), f32), shape((tokens, fill), f32),
-            shape((DH, width), bf16), down_rows, down_rows, in_rows, in_rows, shape((DH, width), bf16),
+            shape((DH, width), bf16), down_rows, in_rows, shape((DH, width), bf16),
         ],
-        [vmem()] * 4 + [anywhere()] * 5,
+        [vmem()] * 4 + [anywhere()] * 3,
         [
             VM(attended_all.shape, bf16),
             VM((tokens, width), f32), VM((16, 64, cols), bf16), VM((16, 8, 128), f32),
@@ -1499,30 +1506,42 @@
     )
 
 
-def attend_back_kernel(attended, out_all, qkv, keep, mix, local, mem_out, lse, memory, normal,
-                       gate_up_half, cot_all, act, down_cols,
-                       attended_all, grad, mix_grad, gate_up_rows, gate_up_other, down_half, feed_out,
-                       out_v, cot_v, by_token, upstream, dk, dv, state_grad, norm_grad, copies, h_s, h_r,
-                       *rest):
+def attend_back_kernel(hidden_grad, middle, cot, gains_all, keep, mix, memory, normal, out_all, qkv, local,
+                       mem_out, lse, gate_up_half, cot_all, act, down_cols,
+                       middle_grad, gains, grad, down_half, feed_out, attended_all, gate_up_rows,
+                       attended, out_v, qkv_v, local_v, mem_v, lse_v, cot_v, act_v, down_v, by_token,
+                       upstream, mix_grad, dk, dv, state_grad, norm_grad, copies, own_s, h_s, h_r, *rest):
     sems_a, sems_g, sems_w, scratch_f = halves_of(rest, [7, 5, 5, 11])
     s = Spot()
     mine = pl.ds(pl.multiple_of(s.me * 128, 128), 128)
-    cot_load = pltpu.make_async_copy(cot_all, cot_v, copies.at[2])
-    load = pltpu.make_async_copy(out_all, out_v, copies.at[0])
-    load.start()
-    own = pltpu.make_async_copy(attended, attended_all.at[mine], copies.at[1])
+    loads = loaded(
+        [(out_all, out_v), (qkv, qkv_v), (local, local_v), (mem_out, mem_v), (lse, lse_v),
+         (cot_all, cot_v), (act, act_v), (down_cols, down_v)],
+        copies,
+    )
+    greet(s)
+    gains[...] = jnp.zeros_like(gains)
+
+    def write(j, value, gain):
+        w = pl.ds(j * 128, 128)
+        total = cot[:, w].astype(f32) + value
+        middle_grad[:, w] = total
+        attended[:, w] = total.astype(bf16)
+        gains[j, 1:2, :] = gain
+
+    norm_back(middle, hidden_grad, gains_all, 1, write)
+    own = pltpu.make_async_copy(attended, attended_all.at[mine], own_s.at[0])
     own.start()
-    cot_load.start()
-    greet(s)
     gather = Gather(s, attended, attended_all, sems_a)
-    back_g = Return(s, gate_up_half, gate_up_rows, 2, sems_g, other=gate_up_other)
-    filler = Scatter(s, act, down_cols, feed_out, scratch_f, FILL[1][0])
-    weigh = Weigh(s, cot_v, act, down_half, sems_w)
-    attend = AttendBack(qkv, keep, mix, local, mem_out, lse, memory, normal, upstream, grad,
+    back_g = Return(s, gate_up_half, gate_up_rows, 2, sems_g)
+    filler = Scatter(s, act_v, down_v, feed_out, scratch_f, FILL[1][0])
+    filler.lag = 8
+    weigh = Weigh(s, cot_v, act_v, down_half, sems_w)
+    attend = AttendBack(qkv_v, keep, mix, local_v, mem_v, lse_v, memory, normal, upstream, grad,
                         mix_grad, dk, dv, state_grad, norm_grad)
+    gather.start()
     attend.clear()
-    gather.start()
-    load.wait()
+    loads[0]()
 
     def head_copy(j):
         return send(by_token.at[:, pl.ds(j * DH, DH)], upstream.at[mine], h_s.at[j], h_r.at[s.me], j)
@@ -1533,8 +1552,8 @@
         for h in range(4 * j, 4 * j + 4):
             pl.when(s.me != h)(lambda: head_copy(h).start())
     upstream[mine, :] = by_token[:, pl.ds(pl.multiple_of(s.me * DH, DH), DH)]
-    cot_load.wait()
-    filler.lag = 8
+    for wait in loads[1:]:
+        wait()
 
     def arrive(j):
         b = upstream.at[pl.ds(j * 128, 128)]
@@ -1556,31 +1575,32 @@
         pl.when(s.me != j)(lambda: head_copy(j).wait_send())
     gather.drain()
     own.wait()
-
-
-def attend_backward(attended, out_all, qkv, keep, mix, saved, gate_up_half, cot_all, act, down_cols,
-                    number):
-    tokens, width = attended.shape
+    gains[s.me, 2:3, :] = mix_grad[0:1, :]
+
+
+def attend_backward(hidden_grad, middle, cot, gains_all, keep, mix, memory, normal, out_all, qkv, local,
+                    mem_out, lse, gate_up_half, cot_all, act, down_cols, number):
+    tokens, width = cot.shape
     total = qkv.shape[0]
     segments = total // SEG
     shape = jax.ShapeDtypeStruct
-    local, mem_out, lse, memory, normal = saved
-    rows = shape((64, 16 * gate_up_half.shape[2]), bf16)
+    whole = (out_all, qkv, local, mem_out, lse, cot_all, act, down_cols)
     return communicate(
         attend_back_kernel, "attend_back", number,
-        (attended, out_all, qkv, keep, mix, local, mem_out, lse, memory, normal,
-         gate_up_half, cot_all, act, down_cols),
-        [vmem(), anywhere()] + [vmem()] * 8 + [anywhere()] * 2 + [vmem()] * 2,
+        (hidden_grad, middle, cot, gains_all, keep, mix, memory, normal, out_all, qkv, local, mem_out,
+         lse, gate_up_half, cot_all, act, down_cols),
+        [vmem()] * 8 + [anywhere()] * 9,
         [
-            shape((total, width), bf16), shape((total, 3 * DH), bf16), shape((8, DH), f32),
-            rows, rows, shape((16, 64, act.shape[1]), bf16), shape((tokens, FILL[1][1]), f32),
+            shape((tokens, width), f32), shape((16, 8, DH), f32), shape((total, 3 * DH), bf16),
+            shape((16, 64, act.shape[1]), bf16), shape((tokens, FILL[1][1]), f32),
+            shape((total, width), bf16), shape((DH, 16 * gate_up_half.shape[2]), bf16),
         ],
-        [anywhere(), vmem(), vmem(), anywhere(), anywhere(), vmem(), vmem()],
-        [
-            VM(out_all.shape, bf16), VM(cot_all.shape, bf16), VM((tokens, width), bf16),
-            VM((total, DH), bf16),
+        [vmem()] * 5 + [anywhere()] * 2,
+        [VM((tokens, width), bf16)] + [VM(a.shape, a.dtype) for a in whole]
+        + [
+            VM((tokens, width), bf16), VM((total, DH), bf16), VM((8, DH), f32),
             VM((total, DH), f32), VM((total, DH), f32), VM((segments, DH, DH), f32),
-            VM((segments, 8, DH), f32), dma((3,)), dma((16,)), dma((16,)),
+            VM((segments, 8, DH), f32), dma((8,)), dma((1,)), dma((16,)), dma((16,)),
         ] + Gather.sems() + Return.sems(2) + Weigh.scratch(act.shape[1]) + Scatter.scratch(FILL[1][1]),
     )
 
@@ -1600,7 +1620,6 @@
     tokens, width = layer_input.shape
     total = tokens * H
     segments = total // SEG
-    dp = lax.axis_index("dp")
 
     own_gains = jnp.zeros((8, tokens), f32)
     own_gains = own_gains.at[0].set(first_gain.astype(f32)).at[1].set(second_gain.astype(f32))
@@ -1618,44 +1637,29 @@
         feed_grad, gate_up_cols, hidden_all, act, down_cols, 3
     )
 
-    first_all = gains_all[:, 0].reshape(width)
-    second_all = gains_all[:, 1].reshape(width)
-    upstream = cotangent.astype(f32)
-    second_factor = lax.rsqrt(jnp.mean(middle * middle, axis=-1, keepdims=True) + epsilon)
-    middle_norm_grad, second_local = norm_backward(middle, second_factor, second_all, hidden_grad)
-    middle_grad = upstream + middle_norm_grad
-    (attended_all, projected_grad, mix_grad, gate_up_rows, gate_up_other, down_half,
-     feed_out_1) = attend_backward(
-        middle_grad.astype(bf16), out_all, qkv, keep, mix, (local, mem_out, lse, memory, normal),
-        gate_up_half, cot_all, act, down_cols, 4,
-    )
-    mix_rows = jnp.where((jnp.arange(H) == lax.axis_index(AXIS))[:, None], mix_grad[0:1], 0.0)
-    gain_grads = jnp.stack([mix_rows, second_local.reshape(16, 128), mix_rows], axis=1)
-    gain_grads = jnp.pad(gain_grads, ((0, 0), (0, 5), (0, 0)))
-    (value_grad, gains_out, feed_out_2, out_rows, down_rows, down_other, in_mine_rows, in_other_rows,
-     out_other) = normed_grad_of(
-        projected_grad, in_cols, normed_all, layer_input, jnp.broadcast_to(first_all[None], (8, width)),
-        act, down_cols, gain_grads, down_half, combined, attended_all, 5,
+    (middle_grad, gain_grads, projected_grad, down_half, feed_out_1, attended_all,
+     gate_up_rows) = attend_backward(
+        hidden_grad, middle, cotangent, gains_all, keep, mix, memory, normal, out_all, qkv, local, mem_out,
+        lse, gate_up_half, cot_all, act, down_cols, 4,
+    )
+    (value_grad, gains_out, feed_out_2, out_rows, down_rows, in_rows, out_other) = normed_grad_of(
+        projected_grad, in_cols, normed_all, layer_input, gains_all, act, down_cols, gain_grads, down_half,
+        combined, attended_all, 5,
     )
     input_grad = middle_grad + value_grad
     feed_out = jnp.concatenate([feed_out_0, feed_out_1, feed_out_2], axis=1)
     layer_output = (middle + feed_out).astype(bf16)
-
-    def both_halves(mine, other):
-        low = jnp.where(dp == 0, mine, other)
-        high = jnp.where(dp == 0, other, mine)
-        return jnp.concatenate([low, high]).astype(f32)
 
     return (
         layer_output,
         input_grad,
         gains_out[0],
-        both_halves(in_mine_rows, in_other_rows),
+        in_rows.astype(f32),
         out_rows.astype(f32) + out_other.astype(f32),
         gains_out[2],
         gains_out[1],
-        both_halves(gate_up_rows, gate_up_other),
-        both_halves(down_rows, down_other),
+        gate_up_rows.astype(f32),
+        down_rows.astype(f32),
     )
 
 

time: 596 us -> 584 us (0.980)
  no operation moved by 1% of the time
where the time goes in v7:
time: 584 us; the launch traced here: 575 us
  Pallas kernels  555 us (95%)
  other arithmetic  15.3 us (3%)
    pallas_call x5, Pallas kernels, communicate(): pl.pallas_call(kernel, out_shape=outs, in_specs=in_specs, out_specs=out_s...  555 us

profile of v7, /device:TPU:0, one launch (start us, length us, event | category | flops | bytes accessed | tf_op | source)
XLA Modules:
  0.0 574.9 jit_solution(1400644120789834173)
XLA Ops:
  0.6 0.7 add_divide_fusion
  1.3 0.7 bitcast_convert_fusion
  2.0 0.7 fusion.1
  2.6 0.6 broadcast_in_dim.24.mix
  3.2 0.7 pad_convert_fusion
  3.9 0.0 copy-start.8
  3.9 0.7 broadcast_in_dim.23.keep
  4.6 0.0 copy-done.8
  4.6 71.3 %project.1 = (bf16[2048,2048]{1,0:T(8,128)(2,1)}, bf16[2048,384]{1,0:T(8,128)(2,1)}, f32[16,8,128]{2,1,0:T(8,128)}, bf16[2048,384]{1,0:T(8,128)(2,1)}) custom-call(bf16[128,2048]{1,0:T(8,128)(2,1)} %x.7, f32[8,128]{1,0:T(8,128)} %copy-done.8, bf16[128,6144]{1,0:T(8,128)(2,1)} %in_w.1), custom_call_target="tpu_custom_call" | custom-call | bytes 16777216 | tf_op jit(solution)/shard_map/project/pallas_call | solution.py:1000
  75.9 183.5 %forward.1 = (f32[2048,128]{1,0:T(8,128)}, f32[2048,128]{1,0:T(8,128)}, f32[2048,128]{1,0:T(8,128)}, bf16[2048,128]{1,0:T(8,128)(2,1)}, f32[2,128,128]{2,1,0:T(8...) custom-call(bf16[2048,384]{1,0:T(8,128)(2,1)} %get-tuple-element.68., ...), custom_call_target="tpu_custom_call" | custom-call | bytes 16777216 | tf_op jit(solution)/shard_map/forward/pallas_call | solution.py:1000
  259.4 73.9 %hidden_grad.1 = (f32[128,2048]{1,0:T(8,128)}, bf16[16,64,1024]{2,1,0:T(8,128)(2,1)}, f32[128,512]{1,0:T(8,128)}) custom-call(bf16[2048,1024]{1,0:T(8,128)(2,1)} %get-tuple-element.71.feed_grad, bf16[2048,1024]{1,0:T(8,128)(2,1)} %get-tuple-element.72.gate_up_cols, bf16[2048,2048]{1,0:T(8,128)(2,1)} %get-tuple-element.73.hidden_all, ...), custom_call_target="tpu_custom_call" | custom-call | bytes 16777216 | tf_op jit(solution)/shard_map/hidden_grad/pallas_call | solution.py:1000
  333.4 124.4 %attend_back.1 = (f32[128,2048]{1,0:T(8,128)}, f32[16,8,128]{2,1,0:T(8,128)}, bf16[2048,384]{1,0:T(8,128)(2,1)}, bf16[16,64,512]{2,1,0:T(8,128)(2,1)}, f32[128,1...) custom-call(f32[128,2048]{1,0:T(8,128)} %get-tuple-element.77.hidden_grad, ...), custom_call_target="tpu_custom_call" | custom-call | bytes 16777216 | tf_op jit(solution)/shard_map/attend_back/pallas_call | solution.py:1000
  457.8 0.0 copy-start.1
  457.8 0.0 copy-start.6
  457.8 0.0 copy-start.7
  457.8 101.4 %normed_grad.1 = (f32[128,2048]{1,0:T(8,128)}, f32[8,128]{1,0:T(8,128)}, f32[128,512]{1,0:T(8,128)}, bf16[128,2048]{1,0:T(8,128)(2,1)}, bf16[128,8192]{1,0:T(8,1...) custom-call(bf16[2048,384]{1,0:T(8,128)(2,1)} %get-tuple-element.87.grad, ...), custom_call_target="tpu_custom_call" | custom-call | bytes 16777216 | tf_op jit(solution)/shard_map/normed_grad/pallas_call | solution.py:1000
  559.2 0.0 copy-start.4
  559.3 0.0 copy-start.5
  559.3 0.0 copy-start.3
  559.3 0.0 copy-done.1
  559.3 0.0 copy-done.6
  559.3 0.0 copy-done.7
  559.3 2.8 fusion
  562.1 0.0 copy-start.2
  562.1 0.0 copy-done.4
  562.1 0.0 copy-done.5
  562.2 1.1 add.20
  563.2 1.3 slice_bitcast_fusion
  564.5 0.0 copy-done.3
  564.5 2.0 convert_element_type.25
  566.5 0.0 copy-done.2
  566.5 0.0 copy-start
  566.5 2.6 convert_element_type.29
  569.1 1.1 copy-done
  570.2 4.2 convert_element_type.28
  (1 shorter events, 0.0 us)
Async XLA Ops:
  3.9 0.7 copy-start.8
  457.8 101.5 %copy-start.1 = (f32[128,2048]{1,0:T(8,128)S(1)}, f32[128,2048]{1,0:T(8,128)}, u32[]{:S(2)}) copy-start(f32[128,2048]{1,0:T(8,128)} %get-tuple-element.70.middle) | copy-start | bytes 3145732
  457.8 101.5 %copy-start.6 = (f32[128,1024]{1,0:T(8,128)S(1)}, f32[128,1024]{1,0:T(8,128)}, u32[]{:S(2)}) copy-start(f32[128,1024]{1,0:T(8,128)} %get-tuple-element.86) | copy-start | bytes 1572868
  457.8 101.5 %copy-start.7 = (f32[128,512]{1,0:T(8,128)S(1)}, f32[128,512]{1,0:T(8,128)}, u32[]{:S(2)}) copy-start(f32[128,512]{1,0:T(8,128)} %get-tuple-element.76) | copy-start | bytes 786436
  559.2 2.9 copy-start.4
  559.3 2.9 copy-start.5
  559.3 5.3 copy-start.3
  562.1 4.4 copy-start.2
  566.5 3.7 copy-start

commit v8 on v7

--- a/solution.py
+++ b/solution.py
@@ -361,7 +361,8 @@
 
 
 MESH = pl.DeviceIdType.MESH
-LIMIT = 60 * 2**20
+LIMIT = 62 * 2**20
+EARLY = 18
 FILL = ((0, 512), (512, 1024), (1536, 512))
 ROWS = 256
 dma = pltpu.SemaphoreType.DMA
@@ -1005,77 +1006,6 @@
         cost_estimate=pl.CostEstimate(flops=flops, bytes_accessed=2**24, transcendentals=0),
         name=name,
     )(*ins)
-
-
-def project_kernel(x, gains, in_w, normed_all, in_cols, gains_all, projected, x_all, normed, row,
-                   copies, g_s, g_r, *rest):
-    gather_sems, col_sems = halves_of(rest, [7, 5])
-    s = Spot()
-    greet(s)
-
-    def gain_copy(k):
-        return send(gains, gains_all.at[s.me], g_s.at[k], g_r.at[s.me], s.partner(k))
-
-    gather = Gather(s, x, x_all, gather_sems)
-    gather.start()
-    for k in range(1, 16):
-        gain_copy(k).start()
-    columns = Columns(s, in_w, in_cols, 3, col_sems)
-    columns.start()
-    gains_all[s.me] = gains[...]
-    x_all[pl.ds(pl.multiple_of(s.me * 128, 128), 128), :] = x[...]
-
-    def gain_row():
-        for k in range(1, 16):
-            src = s.partner(k)
-            b = gains_all.at[src]
-            send(b, b, g_s.at[k], g_r.at[src], s.me).wait_recv()
-        for j in range(16):
-            row[0:1, pl.ds(j * 128, 128)] = gains_all[j, 0:1, :]
-
-    def out_copy(j):
-        tok = pl.ds(pl.multiple_of(s.arrival(j) * 512, 512), 512)
-        return pltpu.make_async_copy(normed.at[tok], normed_all.at[tok], copies.at[j])
-
-    def use(j):
-        if j == 0:
-            columns.finish()
-            gain_row()
-        for n in range(4):
-            rows = pl.ds(pl.multiple_of(s.arrival(j) * 512 + n * 128, 128), 128)
-            values = x_all[rows, :].astype(f32)
-            factor = lax.rsqrt(jnp.mean(values * values, axis=-1, keepdims=True) + epsilon)
-            normed[rows, :] = (values * factor * row[0:1, :]).astype(bf16)
-        out_copy(j).start()
-        tok = pl.ds(pl.multiple_of(s.arrival(j) * 512, 512), 512)
-        out = jnp.dot(normed[tok, :], in_cols[...], preferred_element_type=f32)
-        projected[tok, :] = out.astype(bf16)
-
-    merged(gather.tasks(use), nothing(2) + columns.tasks() + nothing(8))
-    gather.drain()
-    columns.drain()
-    for k in range(1, 16):
-        gain_copy(k).wait_send()
-    for j in range(4):
-        out_copy(j).wait()
-
-
-def project(x, gains, in_weight, number):
-    tokens, width = x.shape
-    return communicate(
-        project_kernel, "project", number, (x, gains, in_weight), [vmem(), vmem(), anywhere()],
-        [
-            jax.ShapeDtypeStruct((16 * tokens, width), bf16),
-            jax.ShapeDtypeStruct((width, 3 * DH), bf16),
-            jax.ShapeDtypeStruct((16, 8, 128), f32),
-            jax.ShapeDtypeStruct((16 * tokens, 3 * DH), bf16),
-        ],
-        [anywhere(), vmem(), vmem(), vmem()],
-        [
-            VM((16 * tokens, width), bf16), VM((16 * tokens, width), bf16), VM((8, width), f32),
-            dma((4,)), dma((16,)), dma((16,)),
-        ] + Gather.sems() + Columns.sems(3),
-    )
 
 
 def kernel_feature(t):
@@ -1218,13 +1148,14 @@
         return [(n, i) for n in range(self.segments) for i in range(SEG // ROWS)]
 
 
-def forward_kernel(qkv, keep, mix, x, gains_all, out_w, cot, gate_up, down,
-                   local, mem_out, lse, combined, memory, normal, middle, out_all, cot_all,
-                   gate_up_cols, down_cols, hidden_all, act, feed_grad,
-                   mixed_tokens, hidden, out_v, cot_v, gate_up_v, down_v, hidden_v, act_v, grad_v,
-                   copies, outs, t_s, t_r, *rest):
-    sems_o, sems_c, sems_g, sems_d, sems_h = halves_of(rest, [11, 7, 5, 5, 7])
+def forward_kernel(starts, mix_gate, first_gain, second_gain, x, in_w, out_w, cot, gate_up, down,
+                   keep, mix, qkv, in_cols, gains_all, local, mem_out, lse, combined, memory, normal, middle,
+                   normed_all, out_all, cot_all, gate_up_cols, down_cols, hidden_all, act, feed_grad,
+                   gains, x_all, normed, row, mixed_tokens, hidden, out_v, cot_v, gate_up_v, down_v, hidden_v,
+                   copies, outs, g_s, g_r, t_s, t_r, *rest):
+    sems_o, sems_c, sems_g, sems_d, sems_h, sems_x, sems_i = halves_of(rest, [11, 7, 5, 5, 7, 7, 5])
     s = Spot()
+    half = act.shape[1]
     mine = pl.ds(pl.multiple_of(s.me * 128, 128), 128)
     own = [
         pltpu.make_async_copy(out_w, out_v.at[mine], copies.at[0]),
@@ -1232,15 +1163,68 @@
     ]
     for cp in own:
         cp.start()
+    gains[...] = jnp.zeros_like(gains)
+    gains[0:1, :] = first_gain[...].astype(f32)
+    gains[1:2, :] = second_gain[...].astype(f32)
+    mix[...] = jnp.broadcast_to(jax.nn.sigmoid(mix_gate[...].astype(f32)), mix.shape)
+    keep[0] = jnp.zeros(keep.shape[1:], f32)
+    for n in range(1, keep.shape[0]):
+        kept = jnp.where(starts[0:1, n:n + 1] > 0, 0.0, 1.0)
+        keep[n] = jnp.broadcast_to(kept, keep.shape[1:])
     greet(s)
+
+    def gain_copy(k):
+        return send(gains, gains_all.at[s.me], g_s.at[k], g_r.at[s.me], s.partner(k))
+
+    gather_x = Gather(s, x, x_all, sems_x)
+    columns_i = Columns(s, in_w, in_cols, 3, sems_i)
+    gather_x.start()
+    for k in range(1, 16):
+        gain_copy(k).start()
+    columns_i.start()
+    gains_all[s.me] = gains[...]
+    x_all[mine, :] = x[...]
+
+    def gain_row():
+        for k in range(1, 16):
+            src = s.partner(k)
+            b = gains_all.at[src]
+            send(b, b, g_s.at[k], g_r.at[src], s.me).wait_recv()
+        for j in range(16):
+            row[0:1, pl.ds(j * 128, 128)] = gains_all[j, 0:1, :]
+
+    def normed_copy(j):
+        tok = pl.ds(pl.multiple_of(s.arrival(j) * 512, 512), 512)
+        return pltpu.make_async_copy(normed.at[tok], normed_all.at[tok], outs.at[j, 3])
+
+    def project(j):
+        if j == 0:
+            columns_i.finish()
+            gain_row()
+        for n in range(4):
+            rows = pl.ds(pl.multiple_of(s.arrival(j) * 512 + n * 128, 128), 128)
+            values = x_all[rows, :].astype(f32)
+            factor = lax.rsqrt(jnp.mean(values * values, axis=-1, keepdims=True) + epsilon)
+            normed[rows, :] = (values * factor * row[0:1, :]).astype(bf16)
+        normed_copy(j).start()
+        tok = pl.ds(pl.multiple_of(s.arrival(j) * 512, 512), 512)
+        out = jnp.dot(normed[tok, :], in_cols[...], preferred_element_type=f32)
+        qkv[tok, :] = out.astype(bf16)
+
+    x_tasks = gather_x.tasks(project)
     gather_o = SharedGather(s, out_w, out_v, sems_o)
     gather_c = Gather(s, cot, cot_v, sems_c)
     gather_h = Gather(s, hidden, hidden_v, sems_h)
     columns_g = Columns(s, gate_up, gate_up_v, 2, sems_g)
     columns_d = Columns(s, down, down_v, 1, sems_d)
-    gather_o.start()
-    gather_c.start()
-    columns_g.start(4)
+
+    def others():
+        gather_o.start()
+        gather_c.start()
+        columns_g.start(4)
+
+    merged(x_tasks[:EARLY] + [others] + x_tasks[EARLY:27], nothing(2) + columns_i.tasks())
+    merged(x_tasks[27:])
     attend = Attend(qkv, keep, mix, local, mem_out, lse, combined, memory, normal)
 
     def token_copy(j):
@@ -1288,17 +1272,21 @@
         gather_h.start()
         wholes[0].start()
 
-    half = act.shape[1]
-
     def out_copies(j):
         tok = pl.ds(pl.multiple_of(s.arrival(j) * 512, 512), 512)
-        pairs = [(hidden_v, hidden_all), (act_v, act), (grad_v, feed_grad)]
+        pairs = [
+            (hidden_v.at[tok], hidden_all),
+            (normed.at[tok, pl.ds(2 * half, half)], act),
+            (normed.at[tok, pl.ds(0, 2 * half)], feed_grad),
+        ]
         return [
-            pltpu.make_async_copy(a.at[tok], b.at[tok], outs.at[j, i]) for i, (a, b) in enumerate(pairs)
+            pltpu.make_async_copy(a, b.at[tok], outs.at[j, i]) for i, (a, b) in enumerate(pairs)
         ]
 
     def use(j):
         if j == 0:
+            for i in range(4):
+                normed_copy(i).wait()
             own[1].wait()
             columns_g.finish()
             columns_d.finish()
@@ -1310,10 +1298,10 @@
         up = jnp.dot(hidden_v[tok, :], gate_up_v[:, half:], preferred_element_type=f32)
         sigma = jax.nn.sigmoid(gate)
         silu = gate * sigma
-        act_v[tok, :] = (silu * up).astype(bf16)
+        normed[tok, 2 * half:3 * half] = (silu * up).astype(bf16)
         slope = sigma * (1.0 + gate * (1.0 - sigma))
-        grad_v[tok, :half] = (act_grad * up * slope).astype(bf16)
-        grad_v[tok, half:] = (act_grad * silu).astype(bf16)
+        normed[tok, :half] = (act_grad * up * slope).astype(bf16)
+        normed[tok, half:2 * half] = (act_grad * silu).astype(bf16)
         for cp in out_copies(j):
             cp.start()
 
@@ -1329,8 +1317,10 @@
     )
     for j in range(16):
         pl.when(s.me != j)(lambda: token_copy(j).wait_send())
-    for part in (gather_o, gather_c, gather_h, columns_g, columns_d):
+    for part in (gather_x, columns_i, gather_o, gather_c, gather_h, columns_g, columns_d):
         part.drain()
+    for k in range(1, 16):
+        gain_copy(k).wait_send()
     for cp in wholes:
         cp.wait()
     for j in range(4):
@@ -1338,30 +1328,35 @@
             cp.wait()
 
 
-def forward_of(qkv, keep, mix, x, gains_all, out_weight, cotangent, gate_up, down, number):
+def forward_of(starts, mix_gate, first_gain, second_gain, x, in_weight, out_weight, cotangent, gate_up, down, number):
     tokens, width = x.shape
-    total = qkv.shape[0]
+    total = tokens * 16
     segments = total // SEG
     half = down.shape[1] // 16
     shape = jax.ShapeDtypeStruct
     rows, cols, fine = (total, width), (width, 2 * half), (total, half)
     return communicate(
         forward_kernel, "forward", number,
-        (qkv, keep, mix, x, gains_all, out_weight, cotangent, gate_up, down),
-        [vmem()] * 5 + [anywhere()] * 4,
+        (starts, mix_gate, first_gain, second_gain, x, in_weight, out_weight, cotangent, gate_up, down),
+        [vmem()] * 5 + [anywhere()] * 5,
         [
+            shape((segments, 8, DH), f32), shape((8, DH), f32),
+            shape((total, 3 * DH), bf16), shape((width, 3 * DH), bf16), shape((16, 8, 128), f32),
             shape((total, DH), f32), shape((total, DH), f32), shape((total, DH), f32),
             shape((total, DH), bf16), shape((segments, DH, DH), f32), shape((segments, 8, DH), f32),
             shape((tokens, width), f32),
-            shape((width, width), bf16), shape(rows, bf16), shape(cols, bf16), shape((width, half), bf16),
-            shape(rows, bf16), shape(fine, bf16), shape((total, 2 * half), bf16),
+            shape(rows, bf16), shape((width, width), bf16), shape(rows, bf16), shape(cols, bf16),
+            shape((width, half), bf16), shape(rows, bf16), shape(fine, bf16),
+            shape((total, 2 * half), bf16),
         ],
-        [vmem()] * 7 + [anywhere()] * 7,
+        [vmem()] * 12 + [anywhere()] * 8,
         [
+            VM((8, tokens), f32), VM(rows, bf16), VM(rows, bf16), VM((8, width), f32),
             VM((tokens, width), bf16), VM((tokens, width), bf16), VM((width, width), bf16),
-            VM(rows, bf16), VM(cols, bf16), VM((width, half), bf16), VM(rows, bf16), VM(fine, bf16),
-            VM((total, 2 * half), bf16), dma((2,)), dma((5, 4)), dma((16,)), dma((16,)),
-        ] + SharedGather.sems() + Gather.sems() + Columns.sems(2) + Columns.sems(1) + Gather.sems(),
+            VM(rows, bf16), VM(cols, bf16), VM((width, half), bf16), VM(rows, bf16),
+            dma((2,)), dma((5, 4)), dma((16,)), dma((16,)), dma((16,)), dma((16,)),
+        ] + SharedGather.sems() + Gather.sems() + Columns.sems(2) + Columns.sems(1) + Gather.sems()
+        + Gather.sems() + Columns.sems(3),
     )
 
 
@@ -1618,20 +1613,11 @@
     cotangent,
 ):
     tokens, width = layer_input.shape
-    total = tokens * H
-    segments = total // SEG
-
-    own_gains = jnp.zeros((8, tokens), f32)
-    own_gains = own_gains.at[0].set(first_gain.astype(f32)).at[1].set(second_gain.astype(f32))
-    mix = jnp.broadcast_to(jax.nn.sigmoid(mix_gate.astype(f32))[None], (8, DH))
-    numbers = jnp.arange(segments)
-    fresh = (numbers == 0) | (document_starts[0] > 0)
-    keep = jnp.broadcast_to(jnp.where(fresh, 0.0, 1.0)[:, None, None], (segments, 8, DH))
-
-    normed_all, in_cols, gains_all, qkv = project(layer_input, own_gains, in_weight, 0)
-    (local, mem_out, lse, combined, memory, normal, middle, out_all, cot_all, gate_up_cols, down_cols,
-     hidden_all, act, feed_grad) = forward_of(
-        qkv, keep, mix, layer_input, gains_all, out_weight, cotangent, gate_up, down_weight, 1
+    (keep, mix, qkv, in_cols, gains_all, local, mem_out, lse, combined, memory, normal, middle, normed_all,
+     out_all, cot_all, gate_up_cols, down_cols, hidden_all, act, feed_grad) = forward_of(
+        document_starts, mix_gate.reshape(1, tokens), first_gain.reshape(1, tokens),
+        second_gain.reshape(1, tokens), layer_input, in_weight, out_weight, cotangent, gate_up,
+        down_weight, 0,
     )
     hidden_grad, gate_up_half, feed_out_0 = hidden_grad_of(
         feed_grad, gate_up_cols, hidden_all, act, down_cols, 3

time: 584 us -> 579 us (level)
    pallas_call x5 -> x4, Pallas kernels: 555 us -> 553 us  [communicate(): pl.pallas_call(kernel, out_shape=outs, in_specs=in_specs, out_specs=out_s...]
where the time goes in v8:
time: 579 us; the launch traced here: 570 us
  Pallas kernels  553 us (96%)
  other arithmetic  12.7 us (2%)
    pallas_call x4, Pallas kernels, communicate(): pl.pallas_call(kernel, out_shape=outs, in_specs=in_specs, out_specs=out_s...  553 us

profile of v8, /device:TPU:0, one launch (start us, length us, event | category | flops | bytes accessed | tf_op | source)
XLA Modules:
  0.0 569.9 jit_solution(9920092313161349303)
XLA Ops:
  0.6 254.4 %forward.1 = (f32[2,8,128]{2,1,0:T(8,128)}, f32[8,128]{1,0:T(8,128)}, bf16[2048,384]{1,0:T(8,128)(2,1)}, bf16[2048,384]{1,0:T(8,128)(2,1)}, f32[16,8,128]{2,1,0:...) custom-call(s32[1,2]{1,0:T(1,128)} %starts.1, ...), custom_call_target="tpu_custom_call" | custom-call | bytes 16777216 | tf_op jit(solution)/shard_map/forward/pallas_call | solution.py:1001
  255.1 74.1 %hidden_grad.1 = (f32[128,2048]{1,0:T(8,128)}, bf16[16,64,1024]{2,1,0:T(8,128)(2,1)}, f32[128,512]{1,0:T(8,128)}) custom-call(bf16[2048,1024]{1,0:T(8,128)(2,1)} %get-tuple-element.47.feed_grad, bf16[2048,1024]{1,0:T(8,128)(2,1)} %get-tuple-element.48.gate_up_cols, bf16[2048,2048]{1,0:T(8,128)(2,1)} %get-tuple-element.49.hidden_all, ...), custom_call_target="tpu_custom_call" | custom-call | bytes 16777216 | tf_op jit(solution)/shard_map/hidden_grad/pallas_call | solution.py:1001
  329.2 123.6 %attend_back.1 = (f32[128,2048]{1,0:T(8,128)}, f32[16,8,128]{2,1,0:T(8,128)}, bf16[2048,384]{1,0:T(8,128)(2,1)}, bf16[16,64,512]{2,1,0:T(8,128)(2,1)}, f32[128,1...) custom-call(f32[128,2048]{1,0:T(8,128)} %get-tuple-element.53.hidden_grad, ...), custom_call_target="tpu_custom_call" | custom-call | bytes 16777216 | tf_op jit(solution)/shard_map/attend_back/pallas_call | solution.py:1001
  452.7 0.0 copy-start.1
  452.7 0.0 copy-start.6
  452.7 0.0 copy-start.7
  452.8 101.4 %normed_grad.1 = (f32[128,2048]{1,0:T(8,128)}, f32[8,128]{1,0:T(8,128)}, f32[128,512]{1,0:T(8,128)}, bf16[128,2048]{1,0:T(8,128)(2,1)}, bf16[128,8192]{1,0:T(8,1...) custom-call(bf16[2048,384]{1,0:T(8,128)(2,1)} %get-tuple-element.67.grad, ...), custom_call_target="tpu_custom_call" | custom-call | bytes 16777216 | tf_op jit(solution)/shard_map/normed_grad/pallas_call | solution.py:1001
  554.2 0.0 copy-start.4
  554.2 0.0 copy-start.5
  554.2 0.0 copy-start.3
  554.2 0.0 copy-done.1
  554.2 0.0 copy-done.6
  554.3 0.0 copy-done.7
  554.3 2.8 fusion
  557.1 0.0 copy-start.2
  557.1 0.0 copy-done.4
  557.1 0.0 copy-done.5
  557.1 1.1 add.10
  558.2 1.3 slice_bitcast_fusion
  559.5 0.0 copy-done.3
  559.5 2.0 convert_element_type.19
  561.5 0.0 copy-done.2
  561.5 0.0 copy-start
  561.5 2.6 convert_element_type.23
  564.0 1.1 copy-done
  565.2 4.2 convert_element_type.22
Async XLA Ops:
  452.7 101.5 %copy-start.1 = (f32[128,2048]{1,0:T(8,128)S(1)}, f32[128,2048]{1,0:T(8,128)}, u32[]{:S(2)}) copy-start(f32[128,2048]{1,0:T(8,128)} %get-tuple-element.46.middle) | copy-start | bytes 3145732
  452.7 101.5 %copy-start.6 = (f32[128,1024]{1,0:T(8,128)S(1)}, f32[128,1024]{1,0:T(8,128)}, u32[]{:S(2)}) copy-start(f32[128,1024]{1,0:T(8,128)} %get-tuple-element.66) | copy-start | bytes 1572868
  452.7 101.5 %copy-start.7 = (f32[128,512]{1,0:T(8,128)S(1)}, f32[128,512]{1,0:T(8,128)}, u32[]{:S(2)}) copy-start(f32[128,512]{1,0:T(8,128)} %get-tuple-element.52) | copy-start | bytes 786436
  554.2 2.9 copy-start.4
  554.2 2.9 copy-start.5
  554.2 5.3 copy-start.3
  557.1 4.4 copy-start.2
  561.5 3.7 copy-start

commit v9 on v8

--- a/solution.py
+++ b/solution.py
@@ -1442,7 +1442,7 @@
         scatter.tasks(),
         loads[:3] + weigh.products() + nothing(24),
         nothing(5) + weigh.folds() + nothing(12),
-        nothing(4) + loads[3:] + products + [over.start] + back_d.tasks() + nothing(5),
+        back_d.tasks() + loads[3:] + products + [over.start] + nothing(9),
         nothing(4) + filler.tasks(),
         nothing(16) + back_i.tasks(),
     )

time: 579 us -> 578 us (level)
  no operation moved by 1% of the time
where the time goes in v9:
time: 578 us; the launch traced here: 569 us
  Pallas kernels  553 us (96%)
  other arithmetic  12.7 us (2%)
    pallas_call x4, Pallas kernels, communicate(): pl.pallas_call(kernel, out_shape=outs, in_specs=in_specs, out_specs=out_s...  553 us

profile of v9, /device:TPU:0, one launch (start us, length us, event | category | flops | bytes accessed | tf_op | source)
XLA Modules:
  0.0 569.3 jit_solution(6317481239044898713)
XLA Ops:
  0.6 254.4 %forward.1 = (f32[2,8,128]{2,1,0:T(8,128)}, f32[8,128]{1,0:T(8,128)}, bf16[2048,384]{1,0:T(8,128)(2,1)}, bf16[2048,384]{1,0:T(8,128)(2,1)}, f32[16,8,128]{2,1,0:...) custom-call(s32[1,2]{1,0:T(1,128)} %starts.1, ...), custom_call_target="tpu_custom_call" | custom-call | bytes 16777216 | tf_op jit(solution)/shard_map/forward/pallas_call | solution.py:1001
  255.1 74.1 %hidden_grad.1 = (f32[128,2048]{1,0:T(8,128)}, bf16[16,64,1024]{2,1,0:T(8,128)(2,1)}, f32[128,512]{1,0:T(8,128)}) custom-call(bf16[2048,1024]{1,0:T(8,128)(2,1)} %get-tuple-element.47.feed_grad, bf16[2048,1024]{1,0:T(8,128)(2,1)} %get-tuple-element.48.gate_up_cols, bf16[2048,2048]{1,0:T(8,128)(2,1)} %get-tuple-element.49.hidden_all, ...), custom_call_target="tpu_custom_call" | custom-call | bytes 16777216 | tf_op jit(solution)/shard_map/hidden_grad/pallas_call | solution.py:1001
  329.2 123.6 %attend_back.1 = (f32[128,2048]{1,0:T(8,128)}, f32[16,8,128]{2,1,0:T(8,128)}, bf16[2048,384]{1,0:T(8,128)(2,1)}, bf16[16,64,512]{2,1,0:T(8,128)(2,1)}, f32[128,1...) custom-call(f32[128,2048]{1,0:T(8,128)} %get-tuple-element.53.hidden_grad, ...), custom_call_target="tpu_custom_call" | custom-call | bytes 16777216 | tf_op jit(solution)/shard_map/attend_back/pallas_call | solution.py:1001
  452.7 0.0 copy-start.1
  452.7 0.0 copy-start.6
  452.7 0.0 copy-start.7
  452.8 100.9 %normed_grad.1 = (f32[128,2048]{1,0:T(8,128)}, f32[8,128]{1,0:T(8,128)}, f32[128,512]{1,0:T(8,128)}, bf16[128,2048]{1,0:T(8,128)(2,1)}, bf16[128,8192]{1,0:T(8,1...) custom-call(bf16[2048,384]{1,0:T(8,128)(2,1)} %get-tuple-element.67.grad, ...), custom_call_target="tpu_custom_call" | custom-call | bytes 16777216 | tf_op jit(solution)/shard_map/normed_grad/pallas_call | solution.py:1001
  553.6 0.0 copy-start.4
  553.6 0.0 copy-start.5
  553.7 0.0 copy-start.3
  553.7 0.0 copy-done.1
  553.7 0.0 copy-done.6
  553.7 0.0 copy-done.7
  553.7 2.8 fusion
  556.5 0.0 copy-start.2
  556.5 0.0 copy-done.4
  556.5 0.0 copy-done.5
  556.5 1.1 add.10
  557.6 1.3 slice_bitcast_fusion
  558.9 0.0 copy-done.3
  558.9 2.0 convert_element_type.19
  560.9 0.0 copy-done.2
  560.9 0.0 copy-start
  560.9 2.6 convert_element_type.23
  563.5 1.1 copy-done
  564.6 4.2 convert_element_type.22
Async XLA Ops:
  452.7 100.9 %copy-start.1 = (f32[128,2048]{1,0:T(8,128)S(1)}, f32[128,2048]{1,0:T(8,128)}, u32[]{:S(2)}) copy-start(f32[128,2048]{1,0:T(8,128)} %get-tuple-element.46.middle) | copy-start | bytes 3145732
  452.7 100.9 %copy-start.6 = (f32[128,1024]{1,0:T(8,128)S(1)}, f32[128,1024]{1,0:T(8,128)}, u32[]{:S(2)}) copy-start(f32[128,1024]{1,0:T(8,128)} %get-tuple-element.66) | copy-start | bytes 1572868
  452.7 100.9 %copy-start.7 = (f32[128,512]{1,0:T(8,128)S(1)}, f32[128,512]{1,0:T(8,128)}, u32[]{:S(2)}) copy-start(f32[128,512]{1,0:T(8,128)} %get-tuple-element.52) | copy-start | bytes 786436
  553.6 2.9 copy-start.4
  553.6 2.9 copy-start.5
  553.7 5.3 copy-start.3
  556.5 4.4 copy-start.2
  560.9 3.7 copy-start
